TPU v7x, 32 devices: a whole 2x2x4 slice. The times are simulated.
32 devices in a mesh: groups: 2 (over x), train: 16 (over z, y, core).
Axes of the slice: x: 2, y: 2, z: 4, core: 2. Of those that a mesh axis runs over, the one named last changes fastest.
Arguments:
- q_left: bfloat16 [2, 5120, 256], P(None, 'train', 'groups'), parts along dimension 2, may hold values from -6 to 6
- q_right: bfloat16 [2, 5120, 256], P(None, 'train', 'groups'), parts along dimension 2, may hold values from -6 to 6
- left_basis: bfloat16 [2, 5120, 5120], P(None, None, 'train'), may hold values from -0.078125 to 0.078125
- right_basis: bfloat16 [2, 5120, 5120], P(None, None, 'train'), may hold values from -0.078125 to 0.078125
- left_eig: float32 [2, 5120], P(None, 'train'), may hold values from 0.05 to 8
- right_eig: float32 [2, 5120], P(None, 'train'), may hold values from 0.05 to 8
- train_left: bfloat16 [192, 2, 32, 5120], P(('groups', 'train')), parts along dimension 0, may hold values from -0.078125 to 0.078125
- train_right: bfloat16 [192, 2, 32, 5120], P(('groups', 'train')), parts along dimension 0, may hold values from -0.078125 to 0.078125
- seq_ids: int32 [4096], P(('groups', 'train')), parts along dimension 0, may hold values from 0 to 5
Outputs:
- scores: float32 [8, 2048], P('groups', 'train'), parts along dimension 0
There are 2 independent parts, one for each index of `groups`. A program takes and returns all parts, laid end to end along the dimension named above; an argument that names none is the same for every part. Nothing has to cross between parts.
Inputs may be any that keep to these rules, and one draw needn't show every extreme that they name: seq_ids[j] names a row of the table held with entry j, that is of rows (j // 128) * 6 to that plus 6 - 1; rows may repeat.
All inputs are finite; a program needn't handle non-finite values.
Results may differ from a plain program's by a relative error of at most 0.0055.
Values may be sent and summed in bfloat16 or wider, within the bound.
No kernel may reach another device: no remote copies, remote signals or barrier semaphores. Data moves between devices by JAX's collectives and lax.ppermute only.
A program may use at most 128 MiB of HBM per device.

v0:
```python
import jax
import jax.numpy as jnp
from jax import lax
from jax.sharding import PartitionSpec as P

R = 32
QUERIES = 4


DAMP = 0.5


def on_device(
    q_left, q_right, left_basis, right_basis, left_eig, right_eig, train_left, train_right, seq_ids
):
    layers, own_rows, width = q_left.shape
    tables = train_left.shape[0]
    left_part = left_basis
    right_part = right_basis
    new_left = jnp.einsum(
        "ldc,ldq->lcq",
        left_part,
        lax.all_gather(q_left, "train", axis=1, tiled=True),
        preferred_element_type=jnp.float32,
    )
    new_right = jnp.einsum(
        "ldc,ldq->lcq",
        right_part,
        lax.all_gather(q_right, "train", axis=1, tiled=True),
        preferred_element_type=jnp.float32,
    )
    coeff_left = new_left
    coeff_right = new_right
    scaled_left = (coeff_left / (left_eig[:, :, None] + DAMP)).astype(jnp.bfloat16)
    scaled_right = (coeff_right / (right_eig[:, :, None] + DAMP)).astype(jnp.bfloat16)
    left_part = left_basis
    right_part = right_basis
    term_left = jnp.einsum(
        "ldc,lcq->dlq", left_part, scaled_left, preferred_element_type=jnp.float32
    )
    term_right = jnp.einsum(
        "ldc,lcq->dlq", right_part, scaled_right, preferred_element_type=jnp.float32
    )
    summed = lax.psum_scatter(
        jnp.stack((term_left, term_right), axis=1), "train", scatter_dimension=0, tiled=True
    )
    precond = summed.astype(jnp.bfloat16)
    piece = lax.all_gather(precond, "train", axis=0, tiled=True)
    left_part = train_left
    right_part = train_right
    new_left = jnp.einsum(
        "dlq,tlsd->lqts", piece[:, 0], left_part, preferred_element_type=jnp.float32
    )
    new_right = jnp.einsum(
        "dlq,tlsd->lqts", piece[:, 1], right_part, preferred_element_type=jnp.float32
    )
    product = (new_left * new_right).reshape(layers, QUERIES, R, tables, train_left.shape[2])
    table_scores = jnp.sum(product, axis=(0, 2, 4))
    match = (seq_ids[None, :] == jnp.arange(tables, dtype=jnp.int32)[:, None]).astype(jnp.float32)
    return jnp.dot(
        table_scores, match, precision=lax.Precision.HIGHEST, preferred_element_type=jnp.float32
    )


def solution(mesh):
    placed = (
        P(None, "train", "groups"),
        P(None, "train", "groups"),
        P(None, None, "train"),
        P(None, None, "train"),
        P(None, "train"),
        P(None, "train"),
        P(("groups", "train"), None, None, None),
        P(("groups", "train"), None, None, None),
        P(("groups", "train")),
    )
    return jax.shard_map(
        on_device, mesh=mesh, in_specs=placed, out_specs=P("groups", "train"), check_vma=False
    )
```

profile of v0, /device:TPU:0, one launch (start us, length us, event | category | flops | bytes accessed | tf_op | source)
XLA Modules:
  0.0 435.6 jit_solution(18306338954372877985)
XLA Ops:
  6.5 0.0 all-gather.6.cloned.1.call-start
  6.5 0.7 all-gather.6.cloned.1.call-update
  7.3 0.0 all-gather.4.cloned.1.call-start
  7.3 0.7 all-gather.4.cloned.1.call-update
  8.0 0.0 all-gather.8.cloned.1.call-start
  8.1 1.2 dynamic-slice
  10.0 0.7 broadcast_add_fusion
  10.6 0.7 broadcast_add_fusion.1
  11.3 44.3 %all-gather.6.cloned.1.call-done = bf16[2,5120,128]{2,1,0:T(8,128)(2,1)} async-done(((bf16[2,320,128]{2,1,0:T(8,128)(2,1)}), bf16[2,5120,128]{2,1,0:T(8,128)(2,1)}) %all-gather.6.cloned.1.call-update) | async-done | bytes 2621456 | tf_op jit(solution)/shard_map/all_gather | solution.py:29
  55.6 11.3 %convolution_bitcast_fusion = f32[5120,1,2,128]{0,3,2,1:T(8,128)} fusion(bf16[2,5120,320]{1,2,0:T(8,128)(2,1)} %param.12, bf16[2,5120,128]{2,1,0:T(8,128)(2,1)} %all-gather.6.cloned.1.call-done, f32[2,320]{1,0:T(2,128)S(1)} %broadcast_add_fusion), kind=kOutput, calls=%fused_computation.1 | convolution fusion | flops 1677885440 | bytes 14420480 | tf_op jit(solution)/shard_map/ldc,lcq->dlq/dot_general | solution.py:41
  66.9 32.9 %all-gather.4.cloned.1.call-done = bf16[2,5120,128]{2,1,0:T(8,128)(2,1)} async-done(((bf16[2,320,128]{2,1,0:T(8,128)(2,1)}), bf16[2,5120,128]{2,1,0:T(8,128)(2,1)}) %all-gather.4.cloned.1.call-update) | async-done | bytes 2621456 | tf_op jit(solution)/shard_map/all_gather | solution.py:23
  99.8 11.2 %convolution_bitcast_fusion.1 = f32[5120,1,2,128]{0,3,2,1:T(8,128)} fusion(bf16[2,5120,320]{1,2,0:T(8,128)(2,1)} %param.11, bf16[2,5120,128]{2,1,0:T(8,128)(2,1)} %all-gather.4.cloned.1.call-done, f32[2,320]{1,0:T(2,128)S(1)} %broadcast_add_fusion.1), kind=kOutput, calls=%fused_computation.2 | convolution fusion | flops 1677885440 | bytes 14420480 | tf_op jit(solution)/shard_map/ldc,lcq->dlq/dot_general | solution.py:38
  111.0 9.3 %pad_maximum_fusion = f32[5120,2,2,128]{0,3,2,1:T(8,128)} fusion(f32[5120,1,2,128]{0,3,2,1:T(8,128)} %convolution_bitcast_fusion, f32[5120,1,2,128]{0,3,2,1:T(8,128)} %convolution_bitcast_fusion.1), kind=kLoop, calls=%fused_computation | loop fusion | flops 2621440 | bytes 20971520 | tf_op jit(solution)/shard_map/stack | solution.py:45
  120.3 16.1 %copy.19 = f32[5120,2,2,128]{3,2,1,0:T(2,128)} copy(f32[5120,2,2,128]{0,3,2,1:T(8,128)} %pad_maximum_fusion) | data formatting | bytes 20971520 | tf_op jit(solution)/shard_map/stack | solution.py:45
  136.4 221.2 %all-reduce.2 = bf16[5120,2,2,128]{3,2,1,0:T(2,128)(2,1)} all-reduce(f32[5120,2,2,128]{3,2,1,0:T(2,128)} %copy.19), channel_id=2, replica_groups=mesh['groups'=2,'train'=16] {'train'}, use_global_device_ids=true, to_apply=%region_0.0.clone | all-reduce | flops 2621440 | bytes 15728640
  357.5 1.9 dynamic-slice_convert_fusion
  359.5 0.0 all-gather.8.cloned.1.call-update
  359.5 59.4 %all-gather.8.cloned.1.call-done = bf16[5120,2,2,128]{3,2,1,0:T(2,128)(2,1)} async-done(((bf16[320,2,2,128]{3,2,1,0:T(2,128)(2,1)}), bf16[5120,2,2,128]{3,2,1,0:T(2,128)(2,1)}) %all-gather.8.cloned.1.call-update) | async-done | bytes 5242896 | tf_op jit(solution)/shard_map/all_gather | solution.py:48
  418.8 0.0 copy-start.1
  418.8 6.0 %fusion.16 = (bf16[5120,1,2,128]{3,2,1,0:T(2,128)(2,1)S(1)}, bf16[5120,1,2,128]{3,2,1,0:T(2,128)(2,1)S(1)}) fusion(bf16[5120,2,2,128]{3,2,1,0:T(2,128)(2,1)} %all-gather.8.cloned.1.call-done), kind=kLoop, calls=%fused_computation.23 | loop fusion | bytes 10485760 | tf_op jit(solution)/shard_map/slice | solution.py:52
  424.8 0.0 copy-done.1
  424.8 0.0 copy-start.2
  424.8 1.2 fusion
  426.0 0.9 copy-done.2
  426.9 0.0 copy-start
  426.9 1.2 fusion.9
  428.1 0.1 reduce_sum.14
  428.2 0.1 reduce_sum.18
  428.3 0.0 copy-done
  428.3 0.8 fusion.14
Async XLA Ops:
  6.5 49.1 %all-gather.6.cloned.1.call-start = ((), (), s32[]{:S(2)}) async-start(), calls=%async_computation.1 | async-start | bytes 2785280 | tf_op jit(solution)/shard_map/all_gather | solution.py:29
  7.3 92.6 %all-gather.4.cloned.1.call-start = ((), (), s32[]{:S(2)}) async-start(), calls=%async_computation | async-start | bytes 2785280 | tf_op jit(solution)/shard_map/all_gather | solution.py:23
  8.0 410.8 %all-gather.8.cloned.1.call-start = ((), (), s32[]{:S(2)}) async-start(), calls=%async_computation.2 | async-start | bytes 5570560 | tf_op jit(solution)/shard_map/all_gather | solution.py:48
  418.8 6.0 %copy-start.1 = (bf16[6,2,32,5120]{3,2,1,0:T(8,128)(2,1)S(1)}, bf16[6,2,32,5120]{3,2,1,0:T(8,128)(2,1)}, u32[]{:S(2)}) copy-start(bf16[6,2,32,5120]{3,2,1,0:T(8,128)(2,1)} %param.16) | copy-start | bytes 11796484
  424.8 2.1 copy-start.2
  426.9 1.4 copy-start
Sparse Core Ops, SparseCore 0:
  9.6 45.9 all-gather.5
  57.9 41.8 all-gather.3
  359.6 59.1 all-gather.7
where the time goes:
time: 436 us
  blocking collectives  221 us (51%)
  waiting for transfers between devices  138 us (32%)
  local copies, waits for them, and re-layouts  26.2 us (6%)
  matrix products  25.6 us (6%)
  between operations  13.8 us (3%)
  other arithmetic  10.7 us (2%)
    unnamed x1, blocking collectives  221 us
    all_gather x1, waiting for transfers between devices, on_device(): piece = lax.all_gather(precond, 'train', axis=0, tiled=True)  59.4 us
    all_gather x1, waiting for transfers between devices, on_device(): lax.all_gather(q_right, 'train', axis=1, tiled=True)  44.3 us
    all_gather x1, waiting for transfers between devices, on_device(): lax.all_gather(q_left, 'train', axis=1, tiled=True)  32.9 us
    another operation x1, local copies, waits for them, and re-layouts, on_device(): jnp.stack((term_left, term_right), axis=1)  16.1 us
    dot_general x1, matrix products, on_device(): jnp.einsum('ldc,lcq->dlq', right_part, scaled_right, preferred_element_ty...  11.3 us
    dot_general x1, matrix products, on_device(): jnp.einsum('ldc,lcq->dlq', left_part, scaled_left, preferred_element_type...  11.2 us
    another operation x1, other arithmetic, on_device(): jnp.stack((term_left, term_right), axis=1)  9.26 us
  transfers between devices with their start and end apart: 3, of which 3 were waited for; matrix products, arithmetic and copies ran while one was open for 3% of the time, Pallas kernels for 0%

commit v1 on v0

v1 whole, which is shorter than its diff:
```python
import functools

import jax
import jax.numpy as jnp
from jax import lax
from jax.experimental import pallas as pl
from jax.experimental.pallas import tpu as pltpu
from jax.sharding import PartitionSpec as P

R = 32
QUERIES = 4
DAMP = 0.5
AXIS = "train"
F32 = jnp.float32
BF16 = jnp.bfloat16


def far_stages(n):
    stages, bit = [], 4
    while bit < n:
        stages.append([bit, 2 * bit, 3 * bit] if 2 * bit < n else [bit])
        bit *= 4
    return stages


def order(n):
    ks = [0]
    for masks in far_stages(n):
        ks = [k ^ m for m in [0] + masks for k in ks]
    return ks


def swap(x, n, mask):
    return lax.ppermute(x, AXIS, [(t, t ^ mask) for t in range(n)])


def gather(own, n):
    block = own
    for masks in far_stages(n):
        block = jnp.concatenate([block] + [swap(block, n, m) for m in masks], axis=0)
    across = swap(block, n, 2)
    return block, across, swap(block, n, 1), swap(across, n, 1)


def scatter_sum(send, keep_near, keep_far, n):
    got = swap(send, n, 1)
    half = keep_near.shape[0]
    across = swap((keep_far + got[half:].astype(F32)).astype(BF16), n, 2)
    total = keep_near + got[:half].astype(F32) + across.astype(F32)
    for masks in reversed(far_stages(n)):
        rows = total.shape[0] // (len(masks) + 1)
        rounded = total.astype(BF16)
        acc = total[:rows]
        for i, m in enumerate(masks, 1):
            acc = acc + swap(rounded[i * rows : (i + 1) * rows], n, m).astype(F32)
        total = acc
    return total.astype(BF16)


def place(me, quarters, full, n):
    rows = full.shape[0] // n
    ks = order(n)
    for quarter, mask in zip(quarters, (0, 2, 1, 3)):
        for i, k in enumerate(ks):
            at = pl.multiple_of((me ^ (k ^ mask)) * rows, rows)
            full[pl.ds(at, rows), :] = quarter[i * rows : (i + 1) * rows, :]


def term_kernel(n, layer, me_ref, qa, qb, qc, qd, basis, eig, send, near, far, full):
    me = me_ref[0]
    place(me, (qa, qb, qc, qd), full, n)
    coeff = lax.dot_general(
        full[...], basis[0], (((0,), (0,)), ((), ())), preferred_element_type=F32
    )
    scaled = (coeff / (eig[layer : layer + 1, :] + DAMP)).astype(BF16)
    rows = full.shape[0] // n
    ks = order(n)
    quarter = len(ks) * rows

    def term(k):
        at = pl.multiple_of((me ^ k) * rows, rows)
        return lax.dot_general(
            basis[0, pl.ds(at, rows), :],
            scaled,
            (((1,), (1,)), ((), ())),
            preferred_element_type=F32,
        )

    for i, k in enumerate(ks):
        at = i * rows
        send[at : at + rows, :] = term(k ^ 1).astype(BF16)
        send[quarter + at : quarter + at + rows, :] = term(k ^ 3).astype(BF16)
        near[at : at + rows, :] = term(k)
        far[at : at + rows, :] = term(k ^ 2)


def terms(me, quarters, basis, eig, layer, n):
    _, width, cols = basis.shape
    q = quarters[0].shape[1]
    whole = lambda a: pl.BlockSpec(a.shape, lambda i, s: (0,) * a.ndim)
    quarter = width // 4
    out = lambda r: pl.BlockSpec((r, q), lambda i, s: (0, 0))
    return pl.pallas_call(
        functools.partial(term_kernel, n, layer),
        grid_spec=pltpu.PrefetchScalarGridSpec(
            num_scalar_prefetch=1,
            grid=(1,),
            in_specs=[whole(a) for a in quarters]
            + [pl.BlockSpec((1, width, cols), lambda i, s: (layer, 0, 0)), whole(eig)],
            out_specs=[out(2 * quarter), out(quarter), out(quarter)],
            scratch_shapes=[pltpu.VMEM((width, q), BF16)],
        ),
        out_shape=[
            jax.ShapeDtypeStruct((2 * quarter, q), BF16),
            jax.ShapeDtypeStruct((quarter, q), F32),
            jax.ShapeDtypeStruct((quarter, q), F32),
        ],
        compiler_params=pltpu.CompilerParams(vmem_limit_bytes=40 * 2**20),
        cost_estimate=pl.CostEstimate(
            flops=4 * width * cols * q, bytes_accessed=2 * width * (cols + 2 * q), transcendentals=0
        ),
        name="terms",
    )(me, *quarters, basis, eig)


def proj_kernel(n, me_ref, pa, pb, pc, pd, train, *rest):
    *other, out, full = rest
    place(me_ref[0], (pa, pb, pc, pd), full, n)
    tables, _, s, width = train.shape
    proj = jnp.dot(
        train[...].reshape(tables * s, width), full[...], preferred_element_type=F32
    )
    if other:
        product = (proj * other[0][...]).reshape(tables, s, proj.shape[1])
        out[...] = jnp.sum(product, axis=1)
    else:
        out[...] = proj


def project(me, quarters, train, layer, n, other=()):
    tables, _, s, width = train.shape
    q = quarters[0].shape[1]
    whole = lambda a: pl.BlockSpec(a.shape, lambda i, r: (0,) * a.ndim)
    shape = (tables, q) if other else (tables * s, q)
    return pl.pallas_call(
        functools.partial(proj_kernel, n),
        grid_spec=pltpu.PrefetchScalarGridSpec(
            num_scalar_prefetch=1,
            grid=(1,),
            in_specs=[whole(a) for a in quarters]
            + [pl.BlockSpec((tables, 1, s, width), lambda i, r: (0, layer, 0, 0))]
            + [whole(a) for a in other],
            out_specs=pl.BlockSpec(shape, lambda i, r: (0, 0)),
            scratch_shapes=[pltpu.VMEM((width, q), BF16)],
        ),
        out_shape=jax.ShapeDtypeStruct(shape, F32),
        compiler_params=pltpu.CompilerParams(vmem_limit_bytes=40 * 2**20),
        cost_estimate=pl.CostEstimate(
            flops=2 * width * tables * s * q,
            bytes_accessed=2 * width * (tables * s + q),
            transcendentals=0,
        ),
        name="project",
    )(me, *quarters, train, *other)


def on_device(
    n, q_left, q_right, left_basis, right_basis, left_eig, right_eig, train_left, train_right, seq_ids
):
    layers = q_left.shape[0]
    tables = train_left.shape[0]
    me = lax.axis_index(AXIS).astype(jnp.int32).reshape(1)
    sides = ((q_left, left_basis, left_eig), (q_right, right_basis, right_eig))
    chunks = [(layer, side) for layer in range(layers) for side in range(2)]
    gathered = {c: gather(sides[c[1]][0][c[0]], n) for c in chunks}
    term = {c: terms(me, gathered[c], sides[c[1]][1], sides[c[1]][2], c[0], n) for c in chunks}
    precond = {c: gather(scatter_sum(*term[c], n), n) for c in chunks}
    total = 0.0
    for layer in range(layers):
        left = project(me, precond[layer, 0], train_left, layer, n)
        total = total + project(me, precond[layer, 1], train_right, layer, n, (left,))
    table_scores = jnp.sum(total.reshape(tables, QUERIES, R), axis=2).T
    match = (seq_ids[None, :] == jnp.arange(tables, dtype=jnp.int32)[:, None]).astype(F32)
    return jnp.dot(table_scores, match, precision=lax.Precision.HIGHEST, preferred_element_type=F32)


def solution(mesh):
    placed = (
        P(None, "train", "groups"),
        P(None, "train", "groups"),
        P(None, None, "train"),
        P(None, None, "train"),
        P(None, "train"),
        P(None, "train"),
        P(("groups", "train"), None, None, None),
        P(("groups", "train"), None, None, None),
        P(("groups", "train")),
    )
    return jax.shard_map(
        functools.partial(on_device, mesh.shape[AXIS]),
        mesh=mesh,
        in_specs=placed,
        out_specs=P("groups", "train"),
        check_vma=False,
    )
```

time: 436 us -> 205 us (0.47)
  blocking collectives: 221 us -> 0 us
  starting transfers between devices: 0.08 us -> 72.3 us
  waiting for transfers between devices: 138 us -> 76 us
  matrix products: 25.6 us -> 0.78 us
  Pallas kernels: 0 us -> 15.5 us
  between operations: 13.8 us -> 0.43 us
  local copies, waits for them, and re-layouts: 26.2 us -> 36.2 us
  other arithmetic: 10.7 us -> 3.25 us
    unnamed x1 -> x0, blocking collectives: 221 us -> none
    all_gather x3 -> x0, waiting for transfers between devices: 137 us -> none  [the longest x1 59.4 us: on_device(): piece = lax.all_gather(precond, 'train', axis=0, tiled=True)]
    ppermute x0 -> x68, waiting for transfers between devices: none -> 76 us  [swap(): return lax.ppermute(x, AXIS, [(t, t ^ mask) for t in range(n)])]
    ppermute x0 -> x68, starting transfers between devices: none -> 72.3 us  [swap(): return lax.ppermute(x, AXIS, [(t, t ^ mask) for t in range(n)])]
    unnamed x7 -> x38, local copies, waits for them, and re-layouts: 2.17 us -> 34.2 us
    dot_general x4 -> x0, matrix products: 24.9 us -> none  [the longest x1 11.3 us: on_device(): jnp.einsum('ldc,lcq->dlq', right_part, scaled_right, preferred_element_ty...]
    another operation x1 -> x0, local copies, waits for them, and re-layouts: 16.1 us -> none  [on_device(): jnp.stack((term_left, term_right), axis=1)]
    pallas_call x0 -> x8, Pallas kernels: none -> 15.5 us  [the longest x4 12.4 us: terms(): pl.pallas_call(functools.partial(term_kernel, n, layer), grid_spec=pltpu....]
  transfers between devices with their start and end apart: 3 -> 68, of which waited for: 3 -> 20; matrix products, arithmetic and copies ran while one was open for 3% -> 12% of each run, Pallas kernels for 0% -> 7%
where the time goes in v1:
time: 205 us; the launch traced here: 204 us
  waiting for transfers between devices  76 us (37%)
  starting transfers between devices  72.3 us (35%)
  local copies, waits for them, and re-layouts  36.2 us (18%)
  Pallas kernels  15.5 us (8%)
  other arithmetic  3.25 us (2%)
    ppermute x68, waiting for transfers between devices, swap(): return lax.ppermute(x, AXIS, [(t, t ^ mask) for t in range(n)])  76 us
    ppermute x68, starting transfers between devices, swap(): return lax.ppermute(x, AXIS, [(t, t ^ mask) for t in range(n)])  72.3 us
    unnamed x38, local copies, waits for them, and re-layouts  34.2 us
    pallas_call x4, Pallas kernels, terms(): pl.pallas_call(functools.partial(term_kernel, n, layer), grid_spec=pltpu....  12.4 us
  transfers between devices with their start and end apart: 68, of which 20 were waited for; matrix products, arithmetic and copies ran while one was open for 12% of the time, Pallas kernels for 7%

profile of v1, /device:TPU:0, one launch (start us, length us, event | category | flops | bytes accessed | tf_op | source)
XLA Modules:
  0.0 204.5 jit_solution(4141656230386112116)
XLA Ops:
  0.0 0.9 slice_bitcast_fusion
  0.9 5.1 %collective-permute-start.53 = (bf16[320,128]{1,0:T(8,128)(2,1)S(1)}, bf16[320,128]{1,0:T(8,128)(2,1)S(1)}, u32[]{:S(2)}, u32[]{:S(2)}) collective-permute-start(bf16[320,128]{1,0:T(8,128)(2,1)S(1)} %get-tuple-element.49), channel_id=1, source_target_pairs={{0,12},{1,13},{2,14},{3,15},{4,8},{5,9},{6,10},{7,11},{8,4},{9,5},... | collective-permute-start | bytes 245768 | tf_op jit(solution)/shard_map/ppermute | solution.py:34
  6.7 3.7 %collective-permute-start.19 = (bf16[320,128]{1,0:T(8,128)(2,1)S(1)}, bf16[320,128]{1,0:T(8,128)(2,1)S(1)}, u32[]{:S(2)}, u32[]{:S(2)}) collective-permute-start(bf16[320,128]{1,0:T(8,128)(2,1)S(1)} %get-tuple-element.50), channel_id=1, source_target_pairs={{0,12},{1,13},{2,14},{3,15},{4,8},{5,9},{6,10},{7,11},{8,4},{9,5},... | collective-permute-start | bytes 245768 | tf_op jit(solution)/shard_map/ppermute | solution.py:34
  10.5 3.6 %collective-permute-start.17 = (bf16[320,128]{1,0:T(8,128)(2,1)S(1)}, bf16[320,128]{1,0:T(8,128)(2,1)S(1)}, u32[]{:S(2)}, u32[]{:S(2)}) collective-permute-start(bf16[320,128]{1,0:T(8,128)(2,1)S(1)} %get-tuple-element.50), channel_id=1, source_target_pairs={{0,4},{1,5},{2,6},{3,7},{4,0},{5,1},{6,2},{7,3},{8,12},{9,13},{10,... | collective-permute-start | bytes 245768 | tf_op jit(solution)/shard_map/ppermute | solution.py:34
  14.0 3.2 %collective-permute-done.52 = bf16[320,128]{1,0:T(8,128)(2,1)S(1)} collective-permute-done((bf16[320,128]{1,0:T(8,128)(2,1)S(1)}, bf16[320,128]{1,0:T(8,128)(2,1)S(1)}, u32[]{:S(2)}, u32[]{:S(2)}) %collective-permute-start.52) | collective-permute-done | bytes 81952 | tf_op jit(solution)/shard_map/ppermute | solution.py:34
  17.3 1.4 collective-permute-start.54
  18.7 0.9 slice_bitcast_fusion.1
  19.6 3.0 %collective-permute-start.2 = (bf16[320,128]{1,0:T(8,128)(2,1)S(1)}, bf16[320,128]{1,0:T(8,128)(2,1)S(1)}, u32[]{:S(2)}, u32[]{:S(2)}) collective-permute-start(bf16[320,128]{1,0:T(8,128)(2,1)S(1)} %get-tuple-element.52), channel_id=1, source_target_pairs={{0,12},{1,13},{2,14},{3,15},{4,8},{5,9},{6,10},{7,11},{8,4},{9,5},... | collective-permute-start | bytes 245768 | tf_op jit(solution)/shard_map/ppermute | solution.py:34
  22.7 1.4 collective-permute-start
  24.1 2.9 %collective-permute-start.36 = (bf16[320,128]{1,0:T(8,128)(2,1)S(1)}, bf16[320,128]{1,0:T(8,128)(2,1)S(1)}, u32[]{:S(2)}, u32[]{:S(2)}) collective-permute-start(bf16[320,128]{1,0:T(8,128)(2,1)S(1)} %get-tuple-element.51), channel_id=1, source_target_pairs={{0,12},{1,13},{2,14},{3,15},{4,8},{5,9},{6,10},{7,11},{8,4},{9,5},... | collective-permute-start | bytes 245768 | tf_op jit(solution)/shard_map/ppermute | solution.py:34
  27.1 3.4 %collective-permute-done.36 = bf16[320,128]{1,0:T(8,128)(2,1)S(1)} collective-permute-done((bf16[320,128]{1,0:T(8,128)(2,1)S(1)}, bf16[320,128]{1,0:T(8,128)(2,1)S(1)}, u32[]{:S(2)}, u32[]{:S(2)}) %collective-permute-start.36) | collective-permute-done | bytes 81952 | tf_op jit(solution)/shard_map/ppermute | solution.py:34
  30.5 1.0 collective-permute-start.35
  31.4 2.5 %collective-permute-start.34 = (bf16[320,128]{1,0:T(8,128)(2,1)S(1)}, bf16[320,128]{1,0:T(8,128)(2,1)S(1)}, u32[]{:S(2)}, u32[]{:S(2)}) collective-permute-start(bf16[320,128]{1,0:T(8,128)(2,1)S(1)} %get-tuple-element.51), channel_id=1, source_target_pairs={{0,4},{1,5},{2,6},{3,7},{4,0},{5,1},{6,2},{7,3},{8,12},{9,13},{10,... | collective-permute-start | bytes 245768 | tf_op jit(solution)/shard_map/ppermute | solution.py:34
  34.7 2.0 collective-permute-done.35
  37.2 1.7 collective-permute-start.37
  38.9 9.9 %copy.11.basis = bf16[2,5120,320]{2,1,0:T(8,128)(2,1)} copy(bf16[2,5120,320]{1,2,0:T(8,128)(2,1)} %param.11) | data formatting | bytes 13107200 | tf_op args[2]
  50.8 3.2 %copy-done = bf16[2,5120,320]{2,1,0:T(8,128)(2,1)S(1)} copy-done((bf16[2,5120,320]{2,1,0:T(8,128)(2,1)S(1)}, bf16[2,5120,320]{2,1,0:T(8,128)(2,1)}, u32[]{:S(2)}) %copy-start) | copy-done | bytes 6553624
  54.0 1.0 copy-done.8
  55.0 1.0 copy-done.12
  56.0 2.9 %terms.7 = (bf16[2560,128]{1,0:T(8,128)(2,1)}, f32[1280,128]{1,0:T(8,128)S(1)}, f32[1280,128]{1,0:T(8,128)S(1)}) custom-call(s32[1]{0:T(128)} %bitcast.me_ref, bf16[1280,128]{1,0:T(8,128)(2,1)S(1)} %pad_maximum_fusion.6.qa, bf16[1280,128]{1,0:T(8,128)(2,1)S(1)} %collective-permute-done.54.qb, bf16[1280,128]{1,0:T(8,128)(2,1)S(1)} %copy-done.8, ...), custom_call_target="tpu_custom_call" | custom-call | flops 838860800 | bytes 5898240 | tf_op jit(solution)/shard_map/terms/pallas_call | solution.py:103
  61.4 9.9 %copy.10.basis = bf16[2,5120,320]{2,1,0:T(8,128)(2,1)} copy(bf16[2,5120,320]{1,2,0:T(8,128)(2,1)} %param.12) | data formatting | bytes 13107200 | tf_op args[3]
  71.3 3.2 %copy-done.1 = bf16[2,5120,320]{2,1,0:T(8,128)(2,1)S(1)} copy-done((bf16[2,5120,320]{2,1,0:T(8,128)(2,1)S(1)}, bf16[2,5120,320]{2,1,0:T(8,128)(2,1)}, u32[]{:S(2)}) %copy-start.1) | copy-done | bytes 6553624
  74.5 1.0 copy-done.6
  75.5 1.0 copy-done.10
  76.5 1.0 copy-done.14
  77.4 2.9 %terms.5 = (bf16[2560,128]{1,0:T(8,128)(2,1)}, f32[1280,128]{1,0:T(8,128)S(1)}, f32[1280,128]{1,0:T(8,128)S(1)}) custom-call(s32[1]{0:T(128)} %bitcast.me_ref, bf16[1280,128]{1,0:T(8,128)(2,1)S(1)} %pad_maximum_fusion.2.qa, bf16[1280,128]{1,0:T(8,128)(2,1)S(1)} %copy-done.6, bf16[1280,128]{1,0:T(8,128)(2,1)S(1)} %copy-done.10, ...), custom_call_target="tpu_custom_call" | custom-call | flops 838860800 | bytes 5898240 | tf_op jit(solution)/shard_map/terms/pallas_call | solution.py:103
  80.9 3.3 %terms.6 = (bf16[2560,128]{1,0:T(8,128)(2,1)S(1)}, f32[1280,128]{1,0:T(8,128)S(1)}, f32[1280,128]{1,0:T(8,128)S(1)}) custom-call(s32[1]{0:T(128)} %bitcast.me_ref, bf16[1280,128]{1,0:T(8,128)(2,1)S(1)} %pad_maximum_fusion.4.qa, bf16[1280,128]{1,0:T(8,128)(2,1)} %collective-permute-done.37.qb, bf16[1280,128]{1,0:T(8,128)(2,1)} %collective-permute-done.38.qc, ...), custom_call_target="tpu_custom_call" | custom-call | flops 838860800 | bytes 5898240 | tf_op jit(solution)/shard_map/terms/pallas_call | solution.py:103
  84.8 3.3 %terms.4 = (bf16[2560,128]{1,0:T(8,128)(2,1)S(1)}, f32[1280,128]{1,0:T(8,128)S(1)}, f32[1280,128]{1,0:T(8,128)S(1)}) custom-call(s32[1]{0:T(128)} %bitcast.me_ref, bf16[1280,128]{1,0:T(8,128)(2,1)S(1)} %pad_maximum_fusion.qa, bf16[1280,128]{1,0:T(8,128)(2,1)} %collective-permute-done.3.qb, bf16[1280,128]{1,0:T(8,128)(2,1)} %collective-permute-done.4.qc, ...), custom_call_target="tpu_custom_call" | custom-call | flops 838860800 | bytes 5898240 | tf_op jit(solution)/shard_map/terms/pallas_call | solution.py:103
  88.2 1.0 add_convert_fusion
  89.8 1.7 collective-permute-start.24
  92.1 1.7 collective-permute-start.7
  93.9 6.0 %collective-permute-done.58 = bf16[1280,128]{1,0:T(8,128)(2,1)S(1)} collective-permute-done((bf16[1280,128]{1,0:T(8,128)(2,1)S(1)}, bf16[1280,128]{1,0:T(8,128)(2,1)S(1)}, u32[]{:S(2)}, u32[]{:S(2)}) %collective-permute-start.58) | collective-permute-done | bytes 327712 | tf_op jit(solution)/shard_map/ppermute | solution.py:34
  99.8 1.1 fusion.14
  101.3 1.7 collective-permute-start.61
  103.1 3.8 %collective-permute-done.24 = bf16[1280,128]{1,0:T(8,128)(2,1)S(1)} collective-permute-done((bf16[1280,128]{1,0:T(8,128)(2,1)S(1)}, bf16[1280,128]{1,0:T(8,128)(2,1)S(1)}, u32[]{:S(2)}, u32[]{:S(2)}) %collective-permute-start.24) | collective-permute-done | bytes 327712 | tf_op jit(solution)/shard_map/ppermute | solution.py:34
  107.5 6.3 %collective-permute-done.41 = bf16[1280,128]{1,0:T(8,128)(2,1)S(1)} collective-permute-done((bf16[1280,128]{1,0:T(8,128)(2,1)S(1)}, bf16[1280,128]{1,0:T(8,128)(2,1)S(1)}, u32[]{:S(2)}, u32[]{:S(2)}) %collective-permute-start.41) | collective-permute-done | bytes 327712 | tf_op jit(solution)/shard_map/ppermute | solution.py:34
  114.3 6.1 %collective-permute-done.7 = bf16[1280,128]{1,0:T(8,128)(2,1)S(1)} collective-permute-done((bf16[1280,128]{1,0:T(8,128)(2,1)S(1)}, bf16[1280,128]{1,0:T(8,128)(2,1)S(1)}, u32[]{:S(2)}, u32[]{:S(2)}) %collective-permute-start.7) | collective-permute-done | bytes 327712 | tf_op jit(solution)/shard_map/ppermute | solution.py:34
  120.5 2.0 collective-permute-start.27
  122.7 2.4 %collective-permute-start.42 = (bf16[320,128]{1,0:T(8,128)(2,1)S(1)}, bf16[320,128]{1,0:T(8,128)(2,1)S(1)}, u32[]{:S(2)}, u32[]{:S(2)}) collective-permute-start(bf16[320,128]{1,0:T(8,128)(2,1)S(1)} %get-tuple-element.40), channel_id=1, source_target_pairs={{0,4},{1,5},{2,6},{3,7},{4,0},{5,1},{6,2},{7,3},{8,12},{9,13},{10,... | collective-permute-start | bytes 245768 | tf_op jit(solution)/shard_map/ppermute | solution.py:34
  125.1 2.0 collective-permute-start.44
  127.7 1.9 collective-permute-start.8
  129.6 2.8 %collective-permute-done.26 = bf16[320,128]{1,0:T(8,128)(2,1)S(1)} collective-permute-done((bf16[320,128]{1,0:T(8,128)(2,1)S(1)}, bf16[320,128]{1,0:T(8,128)(2,1)S(1)}, u32[]{:S(2)}, u32[]{:S(2)}) %collective-permute-start.26) | collective-permute-done | bytes 81952 | tf_op jit(solution)/shard_map/ppermute | solution.py:34
  132.4 1.9 collective-permute-start.10
  134.4 2.0 collective-permute-start.64
  136.4 5.9 %collective-permute-done.43 = bf16[320,128]{1,0:T(8,128)(2,1)S(1)} collective-permute-done((bf16[320,128]{1,0:T(8,128)(2,1)S(1)}, bf16[320,128]{1,0:T(8,128)(2,1)S(1)}, u32[]{:S(2)}, u32[]{:S(2)}) %collective-permute-start.43) | collective-permute-done | bytes 81952 | tf_op jit(solution)/shard_map/ppermute | solution.py:34
  142.3 2.5 %collective-permute-start.62 = (bf16[320,128]{1,0:T(8,128)(2,1)S(1)}, bf16[320,128]{1,0:T(8,128)(2,1)S(1)}, u32[]{:S(2)}, u32[]{:S(2)}) collective-permute-start(bf16[320,128]{1,0:T(8,128)(2,1)S(1)} %fusion.2), channel_id=1, source_target_pairs={{0,4},{1,5},{2,6},{3,7},{4,0},{5,1},{6,2},{7,3},{8,12},{9,13},{10,... | collective-permute-start | bytes 245768 | tf_op jit(solution)/shard_map/ppermute | solution.py:34
  144.9 1.9 collective-permute-start.30
  147.6 2.9 %collective-permute-start.28 = (bf16[320,128]{1,0:T(8,128)(2,1)S(1)}, bf16[320,128]{1,0:T(8,128)(2,1)S(1)}, u32[]{:S(2)}, u32[]{:S(2)}) collective-permute-start(bf16[320,128]{1,0:T(8,128)(2,1)S(1)} %fusion.8), channel_id=1, source_target_pairs={{0,4},{1,5},{2,6},{3,7},{4,0},{5,1},{6,2},{7,3},{8,12},{9,13},{10,... | collective-permute-start | bytes 245768 | tf_op jit(solution)/shard_map/ppermute | solution.py:34
  150.6 4.1 %collective-permute-done.63 = bf16[320,128]{1,0:T(8,128)(2,1)S(1)} collective-permute-done((bf16[320,128]{1,0:T(8,128)(2,1)S(1)}, bf16[320,128]{1,0:T(8,128)(2,1)S(1)}, u32[]{:S(2)}, u32[]{:S(2)}) %collective-permute-start.63) | collective-permute-done | bytes 81952 | tf_op jit(solution)/shard_map/ppermute | solution.py:34
  154.6 1.9 collective-permute-start.47
  156.6 2.5 %collective-permute-start.45 = (bf16[320,128]{1,0:T(8,128)(2,1)S(1)}, bf16[320,128]{1,0:T(8,128)(2,1)S(1)}, u32[]{:S(2)}, u32[]{:S(2)}) collective-permute-start(bf16[320,128]{1,0:T(8,128)(2,1)S(1)} %fusion.5), channel_id=1, source_target_pairs={{0,4},{1,5},{2,6},{3,7},{4,0},{5,1},{6,2},{7,3},{8,12},{9,13},{10,... | collective-permute-start | bytes 245768 | tf_op jit(solution)/shard_map/ppermute | solution.py:34
  159.1 1.9 collective-permute-start.13
  161.7 2.4 %collective-permute-start.11 = (bf16[320,128]{1,0:T(8,128)(2,1)S(1)}, bf16[320,128]{1,0:T(8,128)(2,1)S(1)}, u32[]{:S(2)}, u32[]{:S(2)}) collective-permute-start(bf16[320,128]{1,0:T(8,128)(2,1)S(1)} %fusion.11), channel_id=1, source_target_pairs={{0,4},{1,5},{2,6},{3,7},{4,0},{5,1},{6,2},{7,3},{8,12},{9,13},{10,... | collective-permute-start | bytes 245768 | tf_op jit(solution)/shard_map/ppermute | solution.py:34
  164.2 4.5 %collective-permute-done.46 = bf16[320,128]{1,0:T(8,128)(2,1)S(1)} collective-permute-done((bf16[320,128]{1,0:T(8,128)(2,1)S(1)}, bf16[320,128]{1,0:T(8,128)(2,1)S(1)}, u32[]{:S(2)}, u32[]{:S(2)}) %collective-permute-start.46) | collective-permute-done | bytes 81952 | tf_op jit(solution)/shard_map/ppermute | solution.py:34
  168.7 1.5 collective-permute-start.65
  170.5 1.5 collective-permute-done.12
  172.1 1.1 collective-permute-start.31
  173.1 1.0 collective-permute-start.48
  174.1 1.1 collective-permute-start.14
  175.2 3.9 %collective-permute-done.65.pb = bf16[1280,128]{1,0:T(8,128)(2,1)S(1)} collective-permute-done((bf16[1280,128]{1,0:T(8,128)(2,1)S(1)}, bf16[1280,128]{1,0:T(8,128)(2,1)S(1)}, u32[]{:S(2)}, u32[]{:S(2)}) %collective-permute-start.65) | collective-permute-done | bytes 327712 | tf_op jit(solution)/shard_map/ppermute | solution.py:34
  179.2 7.0 %collective-permute-done.31.pb = bf16[1280,128]{1,0:T(8,128)(2,1)S(1)} collective-permute-done((bf16[1280,128]{1,0:T(8,128)(2,1)S(1)}, bf16[1280,128]{1,0:T(8,128)(2,1)S(1)}, u32[]{:S(2)}, u32[]{:S(2)}) %collective-permute-start.31) | collective-permute-done | bytes 327712 | tf_op jit(solution)/shard_map/ppermute | solution.py:34
  186.7 6.5 %collective-permute-done.48.pb = bf16[1280,128]{1,0:T(8,128)(2,1)S(1)} collective-permute-done((bf16[1280,128]{1,0:T(8,128)(2,1)S(1)}, bf16[1280,128]{1,0:T(8,128)(2,1)S(1)}, u32[]{:S(2)}, u32[]{:S(2)}) %collective-permute-start.48) | collective-permute-done | bytes 327712 | tf_op jit(solution)/shard_map/ppermute | solution.py:34
  193.2 6.6 %collective-permute-done.14.pb = bf16[1280,128]{1,0:T(8,128)(2,1)S(1)} collective-permute-done((bf16[1280,128]{1,0:T(8,128)(2,1)S(1)}, bf16[1280,128]{1,0:T(8,128)(2,1)S(1)}, u32[]{:S(2)}, u32[]{:S(2)}) %collective-permute-start.14) | collective-permute-done | bytes 327712 | tf_op jit(solution)/shard_map/ppermute | solution.py:34
  203.7 0.8 fusion.12
  (148 shorter events, 17.5 us)
Async XLA Ops:
  0.9 9.5 %collective-permute-start.53 = (bf16[320,128]{1,0:T(8,128)(2,1)S(1)}, bf16[320,128]{1,0:T(8,128)(2,1)S(1)}, u32[]{:S(2)}, u32[]{:S(2)}) collective-permute-start(bf16[320,128]{1,0:T(8,128)(2,1)S(1)} %get-tuple-element.49), channel_id=1, source_target_pairs={{0,12},{1,13},{2,14},{3,15},{4,8},{5,9},{6,10},{7,11},{8,4},{9,5},... | collective-permute-start | bytes 245768 | tf_op jit(solution)/shard_map/ppermute | solution.py:34
  6.1 11.2 %collective-permute-start.52 = (bf16[320,128]{1,0:T(8,128)(2,1)S(1)}, bf16[320,128]{1,0:T(8,128)(2,1)S(1)}, u32[]{:S(2)}, u32[]{:S(2)}) collective-permute-start(bf16[320,128]{1,0:T(8,128)(2,1)S(1)} %get-tuple-element.49), channel_id=1, source_target_pairs={{0,8},{1,9},{2,10},{3,11},{4,12},{5,13},{6,14},{7,15},{8,0},{9,1},... | collective-permute-start | bytes 245768 | tf_op jit(solution)/shard_map/ppermute | solution.py:34
  6.1 11.2 %collective-permute-start.51 = (bf16[320,128]{1,0:T(8,128)(2,1)S(1)}, bf16[320,128]{1,0:T(8,128)(2,1)S(1)}, u32[]{:S(2)}, u32[]{:S(2)}) collective-permute-start(bf16[320,128]{1,0:T(8,128)(2,1)S(1)} %get-tuple-element.49), channel_id=1, source_target_pairs={{0,4},{1,5},{2,6},{3,7},{4,0},{5,1},{6,2},{7,3},{8,12},{9,13},{10,... | collective-permute-start | bytes 245768 | tf_op jit(solution)/shard_map/ppermute | solution.py:34
  6.7 16.0 %collective-permute-start.19 = (bf16[320,128]{1,0:T(8,128)(2,1)S(1)}, bf16[320,128]{1,0:T(8,128)(2,1)S(1)}, u32[]{:S(2)}, u32[]{:S(2)}) collective-permute-start(bf16[320,128]{1,0:T(8,128)(2,1)S(1)} %get-tuple-element.50), channel_id=1, source_target_pairs={{0,12},{1,13},{2,14},{3,15},{4,8},{5,9},{6,10},{7,11},{8,4},{9,5},... | collective-permute-start | bytes 245768 | tf_op jit(solution)/shard_map/ppermute | solution.py:34
  10.4 12.2 %collective-permute-start.18 = (bf16[320,128]{1,0:T(8,128)(2,1)S(1)}, bf16[320,128]{1,0:T(8,128)(2,1)S(1)}, u32[]{:S(2)}, u32[]{:S(2)}) collective-permute-start(bf16[320,128]{1,0:T(8,128)(2,1)S(1)} %get-tuple-element.50), channel_id=1, source_target_pairs={{0,8},{1,9},{2,10},{3,11},{4,12},{5,13},{6,14},{7,15},{8,0},{9,1},... | collective-permute-start | bytes 245768 | tf_op jit(solution)/shard_map/ppermute | solution.py:34
  10.5 13.7 %collective-permute-start.17 = (bf16[320,128]{1,0:T(8,128)(2,1)S(1)}, bf16[320,128]{1,0:T(8,128)(2,1)S(1)}, u32[]{:S(2)}, u32[]{:S(2)}) collective-permute-start(bf16[320,128]{1,0:T(8,128)(2,1)S(1)} %get-tuple-element.50), channel_id=1, source_target_pairs={{0,4},{1,5},{2,6},{3,7},{4,0},{5,1},{6,2},{7,3},{8,12},{9,13},{10,... | collective-permute-start | bytes 245768 | tf_op jit(solution)/shard_map/ppermute | solution.py:34
  17.3 17.3 %collective-permute-start.54 = (bf16[1280,128]{1,0:T(8,128)(2,1)S(1)}, bf16[1280,128]{1,0:T(8,128)(2,1)S(1)}, u32[]{:S(2)}, u32[]{:S(2)}) collective-permute-start(bf16[1280,128]{1,0:T(8,128)(2,1)S(1)} %pad_maximum_fusion.6.qa), channel_id=1, source_target_pairs={{0,2},{1,3},{2,0},{3,1},{4,6},{5,7},{6,4},{7,5},{8,10},{9,11},{10,... | collective-permute-start | bytes 983048 | tf_op jit(solution)/shard_map/ppermute | solution.py:34
  19.6 11.8 %collective-permute-start.2 = (bf16[320,128]{1,0:T(8,128)(2,1)S(1)}, bf16[320,128]{1,0:T(8,128)(2,1)S(1)}, u32[]{:S(2)}, u32[]{:S(2)}) collective-permute-start(bf16[320,128]{1,0:T(8,128)(2,1)S(1)} %get-tuple-element.52), channel_id=1, source_target_pairs={{0,12},{1,13},{2,14},{3,15},{4,8},{5,9},{6,10},{7,11},{8,4},{9,5},... | collective-permute-start | bytes 245768 | tf_op jit(solution)/shard_map/ppermute | solution.py:34
  22.7 11.3 %collective-permute-start.1 = (bf16[320,128]{1,0:T(8,128)(2,1)S(1)}, bf16[320,128]{1,0:T(8,128)(2,1)S(1)}, u32[]{:S(2)}, u32[]{:S(2)}) collective-permute-start(bf16[320,128]{1,0:T(8,128)(2,1)S(1)} %get-tuple-element.52), channel_id=1, source_target_pairs={{0,8},{1,9},{2,10},{3,11},{4,12},{5,13},{6,14},{7,15},{8,0},{9,1},... | collective-permute-start | bytes 245768 | tf_op jit(solution)/shard_map/ppermute | solution.py:34
  22.7 11.3 %collective-permute-start = (bf16[320,128]{1,0:T(8,128)(2,1)S(1)}, bf16[320,128]{1,0:T(8,128)(2,1)S(1)}, u32[]{:S(2)}, u32[]{:S(2)}) collective-permute-start(bf16[320,128]{1,0:T(8,128)(2,1)S(1)} %get-tuple-element.52), channel_id=1, source_target_pairs={{0,4},{1,5},{2,6},{3,7},{4,0},{5,1},{6,2},{7,3},{8,12},{9,13},{10,... | collective-permute-start | bytes 245768 | tf_op jit(solution)/shard_map/ppermute | solution.py:34
  24.1 6.3 %collective-permute-start.36 = (bf16[320,128]{1,0:T(8,128)(2,1)S(1)}, bf16[320,128]{1,0:T(8,128)(2,1)S(1)}, u32[]{:S(2)}, u32[]{:S(2)}) collective-permute-start(bf16[320,128]{1,0:T(8,128)(2,1)S(1)} %get-tuple-element.51), channel_id=1, source_target_pairs={{0,12},{1,13},{2,14},{3,15},{4,8},{5,9},{6,10},{7,11},{8,4},{9,5},... | collective-permute-start | bytes 245768 | tf_op jit(solution)/shard_map/ppermute | solution.py:34
  30.5 6.3 %collective-permute-start.35 = (bf16[320,128]{1,0:T(8,128)(2,1)S(1)}, bf16[320,128]{1,0:T(8,128)(2,1)S(1)}, u32[]{:S(2)}, u32[]{:S(2)}) collective-permute-start(bf16[320,128]{1,0:T(8,128)(2,1)S(1)} %get-tuple-element.51), channel_id=1, source_target_pairs={{0,8},{1,9},{2,10},{3,11},{4,12},{5,13},{6,14},{7,15},{8,0},{9,1},... | collective-permute-start | bytes 245768 | tf_op jit(solution)/shard_map/ppermute | solution.py:34
  31.4 5.7 %collective-permute-start.34 = (bf16[320,128]{1,0:T(8,128)(2,1)S(1)}, bf16[320,128]{1,0:T(8,128)(2,1)S(1)}, u32[]{:S(2)}, u32[]{:S(2)}) collective-permute-start(bf16[320,128]{1,0:T(8,128)(2,1)S(1)} %get-tuple-element.51), channel_id=1, source_target_pairs={{0,4},{1,5},{2,6},{3,7},{4,0},{5,1},{6,2},{7,3},{8,12},{9,13},{10,... | collective-permute-start | bytes 245768 | tf_op jit(solution)/shard_map/ppermute | solution.py:34
  34.0 14.8 %collective-permute-start.55 = (bf16[1280,128]{1,0:T(8,128)(2,1)S(1)}, bf16[1280,128]{1,0:T(8,128)(2,1)S(1)}, u32[]{:S(2)}, u32[]{:S(2)}) collective-permute-start(bf16[1280,128]{1,0:T(8,128)(2,1)S(1)} %pad_maximum_fusion.6.qa), channel_id=1, source_target_pairs={{0,1},{1,0},{2,3},{3,2},{4,5},{5,4},{6,7},{7,6},{8,9},{9,8},{10,11... | collective-permute-start | bytes 983048 | tf_op jit(solution)/shard_map/ppermute | solution.py:34
  34.0 14.8 %collective-permute-start.20 = (bf16[1280,128]{1,0:T(8,128)(2,1)S(1)}, bf16[1280,128]{1,0:T(8,128)(2,1)S(1)}, u32[]{:S(2)}, u32[]{:S(2)}) collective-permute-start(bf16[1280,128]{1,0:T(8,128)(2,1)S(1)} %pad_maximum_fusion.2.qa), channel_id=1, source_target_pairs={{0,2},{1,3},{2,0},{3,1},{4,6},{5,7},{6,4},{7,5},{8,10},{9,11},{10,... | collective-permute-start | bytes 983048 | tf_op jit(solution)/shard_map/ppermute | solution.py:34
  34.6 15.5 %collective-permute-start.56 = (bf16[1280,128]{1,0:T(8,128)(2,1)S(1)}, bf16[1280,128]{1,0:T(8,128)(2,1)S(1)}, u32[]{:S(2)}, u32[]{:S(2)}) collective-permute-start(bf16[1280,128]{1,0:T(8,128)(2,1)S(1)} %collective-permute-done.54.qb), channel_id=1, source_target_pairs={{0,1},{1,0},{2,3},{3,2},{4,5},{5,4},{6,7},{7,6},{8,9},{9,8},{10,11... | collective-permute-start | bytes 983048 | tf_op jit(solution)/shard_map/ppermute | solution.py:34
  36.8 22.1 %collective-permute-start.3 = (bf16[1280,128]{1,0:T(8,128)(2,1)S(1)}, bf16[1280,128]{1,0:T(8,128)(2,1)}, u32[]{:S(2)}, u32[]{:S(2)}) collective-permute-start(bf16[1280,128]{1,0:T(8,128)(2,1)S(1)} %pad_maximum_fusion.qa), channel_id=1, source_target_pairs={{0,2},{1,3},{2,0},{3,1},{4,6},{5,7},{6,4},{7,5},{8,10},{9,11},{10,... | collective-permute-start | bytes 983048 | tf_op jit(solution)/shard_map/ppermute | solution.py:34
  37.2 22.2 %collective-permute-start.37 = (bf16[1280,128]{1,0:T(8,128)(2,1)S(1)}, bf16[1280,128]{1,0:T(8,128)(2,1)}, u32[]{:S(2)}, u32[]{:S(2)}) collective-permute-start(bf16[1280,128]{1,0:T(8,128)(2,1)S(1)} %pad_maximum_fusion.4.qa), channel_id=1, source_target_pairs={{0,2},{1,3},{2,0},{3,1},{4,6},{5,7},{6,4},{7,5},{8,10},{9,11},{10,... | collective-permute-start | bytes 983048 | tf_op jit(solution)/shard_map/ppermute | solution.py:34
  48.8 10.7 %collective-permute-start.21 = (bf16[1280,128]{1,0:T(8,128)(2,1)S(1)}, bf16[1280,128]{1,0:T(8,128)(2,1)S(1)}, u32[]{:S(2)}, u32[]{:S(2)}) collective-permute-start(bf16[1280,128]{1,0:T(8,128)(2,1)S(1)} %pad_maximum_fusion.2.qa), channel_id=1, source_target_pairs={{0,1},{1,0},{2,3},{3,2},{4,5},{5,4},{6,7},{7,6},{8,9},{9,8},{10,11... | collective-permute-start | bytes 983048 | tf_op jit(solution)/shard_map/ppermute | solution.py:34
  49.6 11.0 %collective-permute-start.22 = (bf16[1280,128]{1,0:T(8,128)(2,1)S(1)}, bf16[1280,128]{1,0:T(8,128)(2,1)S(1)}, u32[]{:S(2)}, u32[]{:S(2)}) collective-permute-start(bf16[1280,128]{1,0:T(8,128)(2,1)S(1)} %collective-permute-done.20.qb), channel_id=1, source_target_pairs={{0,1},{1,0},{2,3},{3,2},{4,5},{5,4},{6,7},{7,6},{8,9},{9,8},{10,11... | collective-permute-start | bytes 983048 | tf_op jit(solution)/shard_map/ppermute | solution.py:34
  58.9 29.4 %collective-permute-start.57 = (bf16[2560,128]{1,0:T(8,128)(2,1)}, bf16[2560,128]{1,0:T(8,128)(2,1)}, u32[]{:S(2)}, u32[]{:S(2)}) collective-permute-start(bf16[2560,128]{1,0:T(8,128)(2,1)} %get-tuple-element.27), channel_id=1, source_target_pairs={{0,1},{1,0},{2,3},{3,2},{4,5},{5,4},{6,7},{7,6},{8,9},{9,8},{10,11... | collective-permute-start | bytes 1966088 | tf_op jit(solution)/shard_map/ppermute | solution.py:34
  58.9 21.4 %collective-permute-start.38 = (bf16[1280,128]{1,0:T(8,128)(2,1)S(1)}, bf16[1280,128]{1,0:T(8,128)(2,1)}, u32[]{:S(2)}, u32[]{:S(2)}) collective-permute-start(bf16[1280,128]{1,0:T(8,128)(2,1)S(1)} %pad_maximum_fusion.4.qa), channel_id=1, source_target_pairs={{0,1},{1,0},{2,3},{3,2},{4,5},{5,4},{6,7},{7,6},{8,9},{9,8},{10,11... | collective-permute-start | bytes 983048 | tf_op jit(solution)/shard_map/ppermute | solution.py:34
  59.4 21.4 %collective-permute-start.39 = (bf16[1280,128]{1,0:T(8,128)(2,1)}, bf16[1280,128]{1,0:T(8,128)(2,1)}, u32[]{:S(2)}, u32[]{:S(2)}) collective-permute-start(bf16[1280,128]{1,0:T(8,128)(2,1)} %collective-permute-done.37.qb), channel_id=1, source_target_pairs={{0,1},{1,0},{2,3},{3,2},{4,5},{5,4},{6,7},{7,6},{8,9},{9,8},{10,11... | collective-permute-start | bytes 983048 | tf_op jit(solution)/shard_map/ppermute | solution.py:34
  60.2 24.6 %collective-permute-start.4 = (bf16[1280,128]{1,0:T(8,128)(2,1)S(1)}, bf16[1280,128]{1,0:T(8,128)(2,1)}, u32[]{:S(2)}, u32[]{:S(2)}) collective-permute-start(bf16[1280,128]{1,0:T(8,128)(2,1)S(1)} %pad_maximum_fusion.qa), channel_id=1, source_target_pairs={{0,1},{1,0},{2,3},{3,2},{4,5},{5,4},{6,7},{7,6},{8,9},{9,8},{10,11... | collective-permute-start | bytes 983048 | tf_op jit(solution)/shard_map/ppermute | solution.py:34
  61.3 23.4 %collective-permute-start.5 = (bf16[1280,128]{1,0:T(8,128)(2,1)}, bf16[1280,128]{1,0:T(8,128)(2,1)}, u32[]{:S(2)}, u32[]{:S(2)}) collective-permute-start(bf16[1280,128]{1,0:T(8,128)(2,1)} %collective-permute-done.3.qb), channel_id=1, source_target_pairs={{0,1},{1,0},{2,3},{3,2},{4,5},{5,4},{6,7},{7,6},{8,9},{9,8},{10,11... | collective-permute-start | bytes 983048 | tf_op jit(solution)/shard_map/ppermute | solution.py:34
  80.3 9.4 %collective-permute-start.23 = (bf16[2560,128]{1,0:T(8,128)(2,1)}, bf16[2560,128]{1,0:T(8,128)(2,1)S(1)}, u32[]{:S(2)}, u32[]{:S(2)}) collective-permute-start(bf16[2560,128]{1,0:T(8,128)(2,1)} %get-tuple-element.21), channel_id=1, source_target_pairs={{0,1},{1,0},{2,3},{3,2},{4,5},{5,4},{6,7},{7,6},{8,9},{9,8},{10,11... | collective-permute-start | bytes 1966088 | tf_op jit(solution)/shard_map/ppermute | solution.py:34
  84.2 7.3 %collective-permute-start.40 = (bf16[2560,128]{1,0:T(8,128)(2,1)S(1)}, bf16[2560,128]{1,0:T(8,128)(2,1)S(1)}, u32[]{:S(2)}, u32[]{:S(2)}) collective-permute-start(bf16[2560,128]{1,0:T(8,128)(2,1)S(1)} %get-tuple-element.24), channel_id=1, source_target_pairs={{0,1},{1,0},{2,3},{3,2},{4,5},{5,4},{6,7},{7,6},{8,9},{9,8},{10,11... | collective-permute-start | bytes 1966088 | tf_op jit(solution)/shard_map/ppermute | solution.py:34
  89.3 10.6 %collective-permute-start.58 = (bf16[1280,128]{1,0:T(8,128)(2,1)S(1)}, bf16[1280,128]{1,0:T(8,128)(2,1)S(1)}, u32[]{:S(2)}, u32[]{:S(2)}) collective-permute-start(bf16[1280,128]{1,0:T(8,128)(2,1)S(1)} %add_convert_fusion), channel_id=1, source_target_pairs={{0,2},{1,3},{2,0},{3,1},{4,6},{5,7},{6,4},{7,5},{8,10},{9,11},{10,... | collective-permute-start | bytes 983048 | tf_op jit(solution)/shard_map/ppermute | solution.py:34
  89.8 17.1 %collective-permute-start.24 = (bf16[1280,128]{1,0:T(8,128)(2,1)S(1)}, bf16[1280,128]{1,0:T(8,128)(2,1)S(1)}, u32[]{:S(2)}, u32[]{:S(2)}) collective-permute-start(bf16[1280,128]{1,0:T(8,128)(2,1)S(1)} %add_convert_fusion.2), channel_id=1, source_target_pairs={{0,2},{1,3},{2,0},{3,1},{4,6},{5,7},{6,4},{7,5},{8,10},{9,11},{10,... | collective-permute-start | bytes 983048 | tf_op jit(solution)/shard_map/ppermute | solution.py:34
  91.6 22.3 %collective-permute-start.41 = (bf16[1280,128]{1,0:T(8,128)(2,1)S(1)}, bf16[1280,128]{1,0:T(8,128)(2,1)S(1)}, u32[]{:S(2)}, u32[]{:S(2)}) collective-permute-start(bf16[1280,128]{1,0:T(8,128)(2,1)S(1)} %add_convert_fusion.1), channel_id=1, source_target_pairs={{0,2},{1,3},{2,0},{3,1},{4,6},{5,7},{6,4},{7,5},{8,10},{9,11},{10,... | collective-permute-start | bytes 983048 | tf_op jit(solution)/shard_map/ppermute | solution.py:34
  92.1 28.3 %collective-permute-start.7 = (bf16[1280,128]{1,0:T(8,128)(2,1)S(1)}, bf16[1280,128]{1,0:T(8,128)(2,1)S(1)}, u32[]{:S(2)}, u32[]{:S(2)}) collective-permute-start(bf16[1280,128]{1,0:T(8,128)(2,1)S(1)} %add_convert_fusion.3), channel_id=1, source_target_pairs={{0,2},{1,3},{2,0},{3,1},{4,6},{5,7},{6,4},{7,5},{8,10},{9,11},{10,... | collective-permute-start | bytes 983048 | tf_op jit(solution)/shard_map/ppermute | solution.py:34
  101.0 21.6 %collective-permute-start.59 = (bf16[320,128]{1,0:T(8,128)(2,1)S(1)}, bf16[320,128]{1,0:T(8,128)(2,1)S(1)}, u32[]{:S(2)}, u32[]{:S(2)}) collective-permute-start(bf16[320,128]{1,0:T(8,128)(2,1)S(1)} %get-tuple-element.37), channel_id=1, source_target_pairs={{0,4},{1,5},{2,6},{3,7},{4,0},{5,1},{6,2},{7,3},{8,12},{9,13},{10,... | collective-permute-start | bytes 245768 | tf_op jit(solution)/shard_map/ppermute | solution.py:34
  101.3 21.3 %collective-permute-start.61 = (bf16[320,128]{1,0:T(8,128)(2,1)S(1)}, bf16[320,128]{1,0:T(8,128)(2,1)S(1)}, u32[]{:S(2)}, u32[]{:S(2)}) collective-permute-start(bf16[320,128]{1,0:T(8,128)(2,1)S(1)} %get-tuple-element.38), channel_id=1, source_target_pairs={{0,12},{1,13},{2,14},{3,15},{4,8},{5,9},{6,10},{7,11},{8,4},{9,5},... | collective-permute-start | bytes 245768 | tf_op jit(solution)/shard_map/ppermute | solution.py:34
  106.9 18.2 %collective-permute-start.60 = (bf16[320,128]{1,0:T(8,128)(2,1)S(1)}, bf16[320,128]{1,0:T(8,128)(2,1)S(1)}, u32[]{:S(2)}, u32[]{:S(2)}) collective-permute-start(bf16[320,128]{1,0:T(8,128)(2,1)S(1)} %get-tuple-element.39), channel_id=1, source_target_pairs={{0,8},{1,9},{2,10},{3,11},{4,12},{5,13},{6,14},{7,15},{8,0},{9,1},... | collective-permute-start | bytes 245768 | tf_op jit(solution)/shard_map/ppermute | solution.py:34
  113.9 13.2 %collective-permute-start.25 = (bf16[320,128]{1,0:T(8,128)(2,1)S(1)}, bf16[320,128]{1,0:T(8,128)(2,1)S(1)}, u32[]{:S(2)}, u32[]{:S(2)}) collective-permute-start(bf16[320,128]{1,0:T(8,128)(2,1)S(1)} %get-tuple-element.43), channel_id=1, source_target_pairs={{0,4},{1,5},{2,6},{3,7},{4,0},{5,1},{6,2},{7,3},{8,12},{9,13},{10,... | collective-permute-start | bytes 245768 | tf_op jit(solution)/shard_map/ppermute | solution.py:34
  120.5 7.2 %collective-permute-start.27 = (bf16[320,128]{1,0:T(8,128)(2,1)S(1)}, bf16[320,128]{1,0:T(8,128)(2,1)S(1)}, u32[]{:S(2)}, u32[]{:S(2)}) collective-permute-start(bf16[320,128]{1,0:T(8,128)(2,1)S(1)} %get-tuple-element.44), channel_id=1, source_target_pairs={{0,12},{1,13},{2,14},{3,15},{4,8},{5,9},{6,10},{7,11},{8,4},{9,5},... | collective-permute-start | bytes 245768 | tf_op jit(solution)/shard_map/ppermute | solution.py:34
  122.6 9.8 %collective-permute-start.26 = (bf16[320,128]{1,0:T(8,128)(2,1)S(1)}, bf16[320,128]{1,0:T(8,128)(2,1)S(1)}, u32[]{:S(2)}, u32[]{:S(2)}) collective-permute-start(bf16[320,128]{1,0:T(8,128)(2,1)S(1)} %get-tuple-element.45), channel_id=1, source_target_pairs={{0,8},{1,9},{2,10},{3,11},{4,12},{5,13},{6,14},{7,15},{8,0},{9,1},... | collective-permute-start | bytes 245768 | tf_op jit(solution)/shard_map/ppermute | solution.py:34
  122.7 11.6 %collective-permute-start.42 = (bf16[320,128]{1,0:T(8,128)(2,1)S(1)}, bf16[320,128]{1,0:T(8,128)(2,1)S(1)}, u32[]{:S(2)}, u32[]{:S(2)}) collective-permute-start(bf16[320,128]{1,0:T(8,128)(2,1)S(1)} %get-tuple-element.40), channel_id=1, source_target_pairs={{0,4},{1,5},{2,6},{3,7},{4,0},{5,1},{6,2},{7,3},{8,12},{9,13},{10,... | collective-permute-start | bytes 245768 | tf_op jit(solution)/shard_map/ppermute | solution.py:34
  125.1 9.3 %collective-permute-start.44 = (bf16[320,128]{1,0:T(8,128)(2,1)S(1)}, bf16[320,128]{1,0:T(8,128)(2,1)S(1)}, u32[]{:S(2)}, u32[]{:S(2)}) collective-permute-start(bf16[320,128]{1,0:T(8,128)(2,1)S(1)} %get-tuple-element.41), channel_id=1, source_target_pairs={{0,12},{1,13},{2,14},{3,15},{4,8},{5,9},{6,10},{7,11},{8,4},{9,5},... | collective-permute-start | bytes 245768 | tf_op jit(solution)/shard_map/ppermute | solution.py:34
  127.1 15.2 %collective-permute-start.43 = (bf16[320,128]{1,0:T(8,128)(2,1)S(1)}, bf16[320,128]{1,0:T(8,128)(2,1)S(1)}, u32[]{:S(2)}, u32[]{:S(2)}) collective-permute-start(bf16[320,128]{1,0:T(8,128)(2,1)S(1)} %get-tuple-element.42), channel_id=1, source_target_pairs={{0,8},{1,9},{2,10},{3,11},{4,12},{5,13},{6,14},{7,15},{8,0},{9,1},... | collective-permute-start | bytes 245768 | tf_op jit(solution)/shard_map/ppermute | solution.py:34
  127.7 14.7 %collective-permute-start.8 = (bf16[320,128]{1,0:T(8,128)(2,1)S(1)}, bf16[320,128]{1,0:T(8,128)(2,1)S(1)}, u32[]{:S(2)}, u32[]{:S(2)}) collective-permute-start(bf16[320,128]{1,0:T(8,128)(2,1)S(1)} %get-tuple-element.46), channel_id=1, source_target_pairs={{0,4},{1,5},{2,6},{3,7},{4,0},{5,1},{6,2},{7,3},{8,12},{9,13},{10,... | collective-permute-start | bytes 245768 | tf_op jit(solution)/shard_map/ppermute | solution.py:34
  132.4 12.5 %collective-permute-start.10 = (bf16[320,128]{1,0:T(8,128)(2,1)S(1)}, bf16[320,128]{1,0:T(8,128)(2,1)S(1)}, u32[]{:S(2)}, u32[]{:S(2)}) collective-permute-start(bf16[320,128]{1,0:T(8,128)(2,1)S(1)} %get-tuple-element.47), channel_id=1, source_target_pairs={{0,12},{1,13},{2,14},{3,15},{4,8},{5,9},{6,10},{7,11},{8,4},{9,5},... | collective-permute-start | bytes 245768 | tf_op jit(solution)/shard_map/ppermute | solution.py:34
  134.3 13.3 %collective-permute-start.9 = (bf16[320,128]{1,0:T(8,128)(2,1)S(1)}, bf16[320,128]{1,0:T(8,128)(2,1)S(1)}, u32[]{:S(2)}, u32[]{:S(2)}) collective-permute-start(bf16[320,128]{1,0:T(8,128)(2,1)S(1)} %get-tuple-element.48), channel_id=1, source_target_pairs={{0,8},{1,9},{2,10},{3,11},{4,12},{5,13},{6,14},{7,15},{8,0},{9,1},... | collective-permute-start | bytes 245768 | tf_op jit(solution)/shard_map/ppermute | solution.py:34
  134.4 13.2 %collective-permute-start.64 = (bf16[320,128]{1,0:T(8,128)(2,1)S(1)}, bf16[320,128]{1,0:T(8,128)(2,1)S(1)}, u32[]{:S(2)}, u32[]{:S(2)}) collective-permute-start(bf16[320,128]{1,0:T(8,128)(2,1)S(1)} %fusion.2), channel_id=1, source_target_pairs={{0,12},{1,13},{2,14},{3,15},{4,8},{5,9},{6,10},{7,11},{8,4},{9,5},... | collective-permute-start | bytes 245768 | tf_op jit(solution)/shard_map/ppermute | solution.py:34
  142.3 12.3 %collective-permute-start.63 = (bf16[320,128]{1,0:T(8,128)(2,1)S(1)}, bf16[320,128]{1,0:T(8,128)(2,1)S(1)}, u32[]{:S(2)}, u32[]{:S(2)}) collective-permute-start(bf16[320,128]{1,0:T(8,128)(2,1)S(1)} %fusion.2), channel_id=1, source_target_pairs={{0,8},{1,9},{2,10},{3,11},{4,12},{5,13},{6,14},{7,15},{8,0},{9,1},... | collective-permute-start | bytes 245768 | tf_op jit(solution)/shard_map/ppermute | solution.py:34
  142.3 14.2 %collective-permute-start.62 = (bf16[320,128]{1,0:T(8,128)(2,1)S(1)}, bf16[320,128]{1,0:T(8,128)(2,1)S(1)}, u32[]{:S(2)}, u32[]{:S(2)}) collective-permute-start(bf16[320,128]{1,0:T(8,128)(2,1)S(1)} %fusion.2), channel_id=1, source_target_pairs={{0,4},{1,5},{2,6},{3,7},{4,0},{5,1},{6,2},{7,3},{8,12},{9,13},{10,... | collective-permute-start | bytes 245768 | tf_op jit(solution)/shard_map/ppermute | solution.py:34
  144.9 11.7 %collective-permute-start.30 = (bf16[320,128]{1,0:T(8,128)(2,1)S(1)}, bf16[320,128]{1,0:T(8,128)(2,1)S(1)}, u32[]{:S(2)}, u32[]{:S(2)}) collective-permute-start(bf16[320,128]{1,0:T(8,128)(2,1)S(1)} %fusion.8), channel_id=1, source_target_pairs={{0,12},{1,13},{2,14},{3,15},{4,8},{5,9},{6,10},{7,11},{8,4},{9,5},... | collective-permute-start | bytes 245768 | tf_op jit(solution)/shard_map/ppermute | solution.py:34
  147.6 11.6 %collective-permute-start.29 = (bf16[320,128]{1,0:T(8,128)(2,1)S(1)}, bf16[320,128]{1,0:T(8,128)(2,1)S(1)}, u32[]{:S(2)}, u32[]{:S(2)}) collective-permute-start(bf16[320,128]{1,0:T(8,128)(2,1)S(1)} %fusion.8), channel_id=1, source_target_pairs={{0,8},{1,9},{2,10},{3,11},{4,12},{5,13},{6,14},{7,15},{8,0},{9,1},... | collective-permute-start | bytes 245768 | tf_op jit(solution)/shard_map/ppermute | solution.py:34
  147.6 13.4 %collective-permute-start.28 = (bf16[320,128]{1,0:T(8,128)(2,1)S(1)}, bf16[320,128]{1,0:T(8,128)(2,1)S(1)}, u32[]{:S(2)}, u32[]{:S(2)}) collective-permute-start(bf16[320,128]{1,0:T(8,128)(2,1)S(1)} %fusion.8), channel_id=1, source_target_pairs={{0,4},{1,5},{2,6},{3,7},{4,0},{5,1},{6,2},{7,3},{8,12},{9,13},{10,... | collective-permute-start | bytes 245768 | tf_op jit(solution)/shard_map/ppermute | solution.py:34
  154.6 7.1 %collective-permute-start.47 = (bf16[320,128]{1,0:T(8,128)(2,1)S(1)}, bf16[320,128]{1,0:T(8,128)(2,1)S(1)}, u32[]{:S(2)}, u32[]{:S(2)}) collective-permute-start(bf16[320,128]{1,0:T(8,128)(2,1)S(1)} %fusion.5), channel_id=1, source_target_pairs={{0,12},{1,13},{2,14},{3,15},{4,8},{5,9},{6,10},{7,11},{8,4},{9,5},... | collective-permute-start | bytes 245768 | tf_op jit(solution)/shard_map/ppermute | solution.py:34
  156.5 12.1 %collective-permute-start.46 = (bf16[320,128]{1,0:T(8,128)(2,1)S(1)}, bf16[320,128]{1,0:T(8,128)(2,1)S(1)}, u32[]{:S(2)}, u32[]{:S(2)}) collective-permute-start(bf16[320,128]{1,0:T(8,128)(2,1)S(1)} %fusion.5), channel_id=1, source_target_pairs={{0,8},{1,9},{2,10},{3,11},{4,12},{5,13},{6,14},{7,15},{8,0},{9,1},... | collective-permute-start | bytes 245768 | tf_op jit(solution)/shard_map/ppermute | solution.py:34
  156.6 12.1 %collective-permute-start.45 = (bf16[320,128]{1,0:T(8,128)(2,1)S(1)}, bf16[320,128]{1,0:T(8,128)(2,1)S(1)}, u32[]{:S(2)}, u32[]{:S(2)}) collective-permute-start(bf16[320,128]{1,0:T(8,128)(2,1)S(1)} %fusion.5), channel_id=1, source_target_pairs={{0,4},{1,5},{2,6},{3,7},{4,0},{5,1},{6,2},{7,3},{8,12},{9,13},{10,... | collective-permute-start | bytes 245768 | tf_op jit(solution)/shard_map/ppermute | solution.py:34
  159.1 11.1 %collective-permute-start.13 = (bf16[320,128]{1,0:T(8,128)(2,1)S(1)}, bf16[320,128]{1,0:T(8,128)(2,1)S(1)}, u32[]{:S(2)}, u32[]{:S(2)}) collective-permute-start(bf16[320,128]{1,0:T(8,128)(2,1)S(1)} %fusion.11), channel_id=1, source_target_pairs={{0,12},{1,13},{2,14},{3,15},{4,8},{5,9},{6,10},{7,11},{8,4},{9,5},... | collective-permute-start | bytes 245768 | tf_op jit(solution)/shard_map/ppermute | solution.py:34
  161.0 11.0 %collective-permute-start.12 = (bf16[320,128]{1,0:T(8,128)(2,1)S(1)}, bf16[320,128]{1,0:T(8,128)(2,1)S(1)}, u32[]{:S(2)}, u32[]{:S(2)}) collective-permute-start(bf16[320,128]{1,0:T(8,128)(2,1)S(1)} %fusion.11), channel_id=1, source_target_pairs={{0,8},{1,9},{2,10},{3,11},{4,12},{5,13},{6,14},{7,15},{8,0},{9,1},... | collective-permute-start | bytes 245768 | tf_op jit(solution)/shard_map/ppermute | solution.py:34
  161.7 11.4 %collective-permute-start.11 = (bf16[320,128]{1,0:T(8,128)(2,1)S(1)}, bf16[320,128]{1,0:T(8,128)(2,1)S(1)}, u32[]{:S(2)}, u32[]{:S(2)}) collective-permute-start(bf16[320,128]{1,0:T(8,128)(2,1)S(1)} %fusion.11), channel_id=1, source_target_pairs={{0,4},{1,5},{2,6},{3,7},{4,0},{5,1},{6,2},{7,3},{8,12},{9,13},{10,... | collective-permute-start | bytes 245768 | tf_op jit(solution)/shard_map/ppermute | solution.py:34
  168.7 10.5 %collective-permute-start.65 = (bf16[1280,128]{1,0:T(8,128)(2,1)S(1)}, bf16[1280,128]{1,0:T(8,128)(2,1)S(1)}, u32[]{:S(2)}, u32[]{:S(2)}) collective-permute-start(bf16[1280,128]{1,0:T(8,128)(2,1)S(1)} %pad_maximum_fusion.7.pa), channel_id=1, source_target_pairs={{0,2},{1,3},{2,0},{3,1},{4,6},{5,7},{6,4},{7,5},{8,10},{9,11},{10,... | collective-permute-start | bytes 983048 | tf_op jit(solution)/shard_map/ppermute | solution.py:34
  170.2 16.0 %collective-permute-start.32 = (bf16[1280,128]{1,0:T(8,128)(2,1)S(1)}, bf16[1280,128]{1,0:T(8,128)(2,1)S(1)}, u32[]{:S(2)}, u32[]{:S(2)}) collective-permute-start(bf16[1280,128]{1,0:T(8,128)(2,1)S(1)} %pad_maximum_fusion.3.pa), channel_id=1, source_target_pairs={{0,1},{1,0},{2,3},{3,2},{4,5},{5,4},{6,7},{7,6},{8,9},{9,8},{10,11... | collective-permute-start | bytes 983048 | tf_op jit(solution)/shard_map/ppermute | solution.py:34
  172.1 14.1 %collective-permute-start.31 = (bf16[1280,128]{1,0:T(8,128)(2,1)S(1)}, bf16[1280,128]{1,0:T(8,128)(2,1)S(1)}, u32[]{:S(2)}, u32[]{:S(2)}) collective-permute-start(bf16[1280,128]{1,0:T(8,128)(2,1)S(1)} %pad_maximum_fusion.3.pa), channel_id=1, source_target_pairs={{0,2},{1,3},{2,0},{3,1},{4,6},{5,7},{6,4},{7,5},{8,10},{9,11},{10,... | collective-permute-start | bytes 983048 | tf_op jit(solution)/shard_map/ppermute | solution.py:34
  173.1 20.1 %collective-permute-start.48 = (bf16[1280,128]{1,0:T(8,128)(2,1)S(1)}, bf16[1280,128]{1,0:T(8,128)(2,1)S(1)}, u32[]{:S(2)}, u32[]{:S(2)}) collective-permute-start(bf16[1280,128]{1,0:T(8,128)(2,1)S(1)} %pad_maximum_fusion.5.pa), channel_id=1, source_target_pairs={{0,2},{1,3},{2,0},{3,1},{4,6},{5,7},{6,4},{7,5},{8,10},{9,11},{10,... | collective-permute-start | bytes 983048 | tf_op jit(solution)/shard_map/ppermute | solution.py:34
  174.1 25.7 %collective-permute-start.14 = (bf16[1280,128]{1,0:T(8,128)(2,1)S(1)}, bf16[1280,128]{1,0:T(8,128)(2,1)S(1)}, u32[]{:S(2)}, u32[]{:S(2)}) collective-permute-start(bf16[1280,128]{1,0:T(8,128)(2,1)S(1)} %pad_maximum_fusion.1.pa), channel_id=1, source_target_pairs={{0,2},{1,3},{2,0},{3,1},{4,6},{5,7},{6,4},{7,5},{8,10},{9,11},{10,... | collective-permute-start | bytes 983048 | tf_op jit(solution)/shard_map/ppermute | solution.py:34
  179.2 20.7 %collective-permute-start.67 = (bf16[1280,128]{1,0:T(8,128)(2,1)S(1)}, bf16[1280,128]{1,0:T(8,128)(2,1)S(1)}, u32[]{:S(2)}, u32[]{:S(2)}) collective-permute-start(bf16[1280,128]{1,0:T(8,128)(2,1)S(1)} %collective-permute-done.65.pb), channel_id=1, source_target_pairs={{0,1},{1,0},{2,3},{3,2},{4,5},{5,4},{6,7},{7,6},{8,9},{9,8},{10,11... | collective-permute-start | bytes 983048 | tf_op jit(solution)/shard_map/ppermute | solution.py:34
  186.2 14.9 %collective-permute-start.33 = (bf16[1280,128]{1,0:T(8,128)(2,1)S(1)}, bf16[1280,128]{1,0:T(8,128)(2,1)S(1)}, u32[]{:S(2)}, u32[]{:S(2)}) collective-permute-start(bf16[1280,128]{1,0:T(8,128)(2,1)S(1)} %collective-permute-done.31.pb), channel_id=1, source_target_pairs={{0,1},{1,0},{2,3},{3,2},{4,5},{5,4},{6,7},{7,6},{8,9},{9,8},{10,11... | collective-permute-start | bytes 983048 | tf_op jit(solution)/shard_map/ppermute | solution.py:34
  186.2 15.7 %collective-permute-start.49 = (bf16[1280,128]{1,0:T(8,128)(2,1)S(1)}, bf16[1280,128]{1,0:T(8,128)(2,1)S(1)}, u32[]{:S(2)}, u32[]{:S(2)}) collective-permute-start(bf16[1280,128]{1,0:T(8,128)(2,1)S(1)} %pad_maximum_fusion.5.pa), channel_id=1, source_target_pairs={{0,1},{1,0},{2,3},{3,2},{4,5},{5,4},{6,7},{7,6},{8,9},{9,8},{10,11... | collective-permute-start | bytes 983048 | tf_op jit(solution)/shard_map/ppermute | solution.py:34
  193.2 8.7 %collective-permute-start.50 = (bf16[1280,128]{1,0:T(8,128)(2,1)S(1)}, bf16[1280,128]{1,0:T(8,128)(2,1)S(1)}, u32[]{:S(2)}, u32[]{:S(2)}) collective-permute-start(bf16[1280,128]{1,0:T(8,128)(2,1)S(1)} %collective-permute-done.48.pb), channel_id=1, source_target_pairs={{0,1},{1,0},{2,3},{3,2},{4,5},{5,4},{6,7},{7,6},{8,9},{9,8},{10,11... | collective-permute-start | bytes 983048 | tf_op jit(solution)/shard_map/ppermute | solution.py:34
  (22 other events, 216.4 us)

commit v2 on v0

v2 whole, which is shorter than its diff:
```python
import functools

import jax
import jax.numpy as jnp
from jax import lax
from jax.experimental import pallas as pl
from jax.experimental.pallas import tpu as pltpu
from jax.sharding import PartitionSpec as P

R = 32
QUERIES = 4
DAMP = 0.5
TOGETHER = 2
SPREAD = 2
PIECES = 4
TERMS_VMEM = 20 * 2**20
AXIS = "train"
F32 = jnp.float32
BF16 = jnp.bfloat16


def far_stages(n, most):
    stages, bit = [], 4
    while bit < n:
        bits = min(most, (n // bit).bit_length() - 1)
        stages.append((bit, bits))
        bit <<= bits
    return stages


def swap(x, n, mask):
    return lax.ppermute(x, AXIS, [(t, t ^ mask) for t in range(n)])


def spread(block, n):
    ks = [0]
    for bit, bits in far_stages(n, SPREAD):
        masks = [bit * j for j in range(1, 1 << bits)]
        block = jnp.concatenate([block] + [swap(block, n, m) for m in masks], axis=1)
        ks = [k ^ m for m in [0] + masks for k in ks]
    return block, ks


def fold(total, me, n):
    result = total.astype(BF16)
    for bit, bits in far_stages(n, 2):
        if bits == 1:
            total = total + swap(result, n, bit).astype(F32)
            result = total.astype(BF16)
            continue
        place = lambda t: (t // bit) % 4
        inward = [(t, t ^ bit) for t in range(n) if place(t) in (0, 3)]
        outward = [(b, a) for a, b in inward]
        middle = [(t, t ^ (3 * bit)) for t in range(n) if place(t) in (1, 2)]
        total = total + lax.ppermute(result, AXIS, inward).astype(F32)
        total = total + lax.ppermute(total.astype(BF16), AXIS, middle).astype(F32)
        result = total.astype(BF16)
        inner = (place(me) == 1) | (place(me) == 2)
        result = jnp.where(inner, result, lax.ppermute(result, AXIS, outward))
        total = result.astype(F32)
    return result


def after(x, earlier):
    return lax.optimization_barrier((x, earlier))[0] if earlier else x


def gather_near(block, n):
    across = swap(block, n, 2)
    return block, across, swap(block, n, 1), swap(across, n, 1)


def term_kernel(n, column, first, offsets, me_ref, *refs):
    *arrays, basis, eig, send, keep, full, held, pair, sems = refs
    me = me_ref[0]
    layers, _, width = held.shape
    rows = width // n
    piece = width // PIECES
    copies = {}
    for l in range(layers):
        for p in range(PIECES):
            part = (slice(None), pl.ds(p * piece, piece))
            copies[l, p] = pltpu.make_async_copy(
                basis.at[first + l].at[part], held.at[l].at[part], sems.at[l, p]
            )
            copies[l, p].start()
    mine = me & 1
    above = (me >> 1) & 1
    for l in range(layers):
        for array, ks in zip(arrays, offsets):
            for i, k in enumerate(ks):
                at = pl.multiple_of((me ^ k) * rows, rows)
                full[pl.ds(at, rows), :] = array[l, i * rows : (i + 1) * rows, :]
        coeff = [0.0, 0.0]
        split = held.shape[1] // 2
        for p in range(PIECES):
            copies[l, p].wait()
            for h in range(2):
                coeff[h] = coeff[h] + jnp.dot(
                    held[l, h * split : (h + 1) * split, p * piece : (p + 1) * piece],
                    full[p * piece : (p + 1) * piece, :],
                    preferred_element_type=F32,
                )
        coeff = jnp.concatenate(coeff, axis=0)
        scale = eig[:, column + l : column + l + 1] + DAMP
        scaled = (coeff / scale).astype(BF16).T
        term = jnp.dot(scaled, held[l], preferred_element_type=F32)
        for p in range(n // 2):
            pair[...] = term[:, 2 * p * rows : 2 * (p + 1) * rows].T
            at = pl.multiple_of(((above ^ (p & 1)) * (n // 4) + p // 2) * rows, rows)
            kept = pl.multiple_of(mine * rows, rows)
            sent = pl.multiple_of((1 - mine) * rows, rows)
            keep[l, pl.ds(at, rows), :] = pair[pl.ds(kept, rows), :]
            send[l, pl.ds(at, rows), :] = pair[pl.ds(sent, rows), :].astype(BF16)


def terms(me, arrays, offsets, basis, eig, first, column, n):
    _, cols, width = basis.shape
    layers, _, q = arrays[0].shape
    vmem = pl.BlockSpec(memory_space=pltpu.VMEM)
    half = (layers, width // 2, q)
    return pl.pallas_call(
        functools.partial(term_kernel, n, column, first, offsets),
        in_specs=[pl.BlockSpec(memory_space=pltpu.SMEM)]
        + [vmem] * len(arrays)
        + [pl.BlockSpec(memory_space=pltpu.HBM), vmem],
        out_specs=[vmem, vmem],
        scratch_shapes=[
            pltpu.VMEM((width, q), BF16),
            pltpu.VMEM((layers, cols, width), BF16),
            pltpu.VMEM((2 * width // n, q), F32),
            pltpu.SemaphoreType.DMA((layers, PIECES)),
        ],
        out_shape=[jax.ShapeDtypeStruct(half, BF16), jax.ShapeDtypeStruct(half, F32)],
        compiler_params=pltpu.CompilerParams(vmem_limit_bytes=TERMS_VMEM),
        cost_estimate=pl.CostEstimate(
            flops=layers * 4 * width * cols * q,
            bytes_accessed=layers * 2 * width * (cols + 2 * q),
            transcendentals=0,
        ),
        name="terms",
    )(me, *arrays, pltpu.with_memory_space_constraint(basis, pltpu.HBM), eig)


def proj_kernel(n, first, me_ref, pa, pb, pc, pd, train, *rest):
    *other, out, full, held, sems = rest
    layers, tables, s, width = held.shape
    rows = width // n
    copies = []
    for l in range(layers):
        copies.append(pltpu.make_async_copy(train.at[:, first + l], held.at[l], sems.at[l]))
        copies[l].start()
    total = 0.0
    for l in range(layers):
        for quarter, mask in zip((pa, pb, pc, pd), (0, 2, 1, 3)):
            for i in range(n // 4):
                at = pl.multiple_of((4 * i + ((me_ref[0] & 3) ^ mask)) * rows, rows)
                full[pl.ds(at, rows), :] = quarter[l, i * rows : (i + 1) * rows, :]
        copies[l].wait()
        proj = jnp.dot(
            held[l].reshape(tables * s, width), full[...], preferred_element_type=F32
        )
        if other:
            product = (proj * other[0][l]).reshape(tables, s, proj.shape[1])
            total = total + jnp.sum(product, axis=1)
        else:
            out[l] = proj
    if other:
        out[...] = total


def project(me, quarters, train, first, n, other=()):
    tables, _, s, width = train.shape
    layers, _, q = quarters[0].shape
    vmem = pl.BlockSpec(memory_space=pltpu.VMEM)
    shape = (tables, q) if other else (layers, tables * s, q)
    return pl.pallas_call(
        functools.partial(proj_kernel, n, first),
        in_specs=[pl.BlockSpec(memory_space=pltpu.SMEM)]
        + [vmem] * 4
        + [pl.BlockSpec(memory_space=pltpu.HBM)]
        + [vmem] * len(other),
        out_specs=vmem,
        scratch_shapes=[
            pltpu.VMEM((width, q), BF16),
            pltpu.VMEM((layers, tables, s, width), BF16),
            pltpu.SemaphoreType.DMA((layers,)),
        ],
        out_shape=jax.ShapeDtypeStruct(shape, F32),
        compiler_params=pltpu.CompilerParams(vmem_limit_bytes=TERMS_VMEM),
        cost_estimate=pl.CostEstimate(
            flops=layers * 2 * width * tables * s * q,
            bytes_accessed=layers * 2 * width * (tables * s + q),
            transcendentals=0,
        ),
        name="project",
    )(me, *quarters, train, *other)


def on_device(
    n, q_left, q_right, left_basis, right_basis, left_eig, right_eig, train_left, train_right, seq_ids
):
    layers = q_left.shape[0]
    tables = train_left.shape[0]
    me = lax.axis_index(AXIS).astype(jnp.int32).reshape(1)
    eig = jnp.concatenate((left_eig, right_eig), axis=0).T
    sides = (
        (q_left, jnp.swapaxes(left_basis, 1, 2), train_left),
        (q_right, jnp.swapaxes(right_basis, 1, 2), train_right),
    )
    chunks = [(first, side) for first in range(0, layers, TOGETHER) for side in range(2)]
    blocks = [spread(sides[side][0][first : first + TOGETHER], n) for first, side in chunks]
    gathered = [gather_near(block, n) for block, _ in blocks]
    aways, halves, quarters = [], [], []
    for i, (first, side) in enumerate(chunks):
        ks = blocks[i][1]
        offsets = [[k ^ m for k in ks] for m in (0, 2, 1, 3)]
        earlier = []
        arrays = after(gathered[i], earlier)
        send, keep = terms(me, arrays, offsets, sides[side][1], eig, first, side * layers + first, n)
        half = keep + swap(send, n, 1).astype(F32)
        quarter = half.shape[1] // 2
        aways.append(half[:, quarter:].astype(BF16))
        halves.append(half[:, :quarter] + swap(aways[i], n, 2).astype(F32))
    total, left = 0.0, ()
    for i, (first, side) in enumerate(chunks):
        precond = gather_near(fold(halves[i], me[0], n), n)
        left = (project(me, precond, sides[side][2], first, n, left),)
        if side:
            total, left = total + left[0], ()
    table_scores = jnp.sum(total.reshape(tables, QUERIES, R), axis=2).T
    match = (seq_ids[None, :] == jnp.arange(tables, dtype=jnp.int32)[:, None]).astype(F32)
    return jnp.dot(table_scores, match, precision=lax.Precision.HIGHEST, preferred_element_type=F32)


def solution(mesh):
    placed = (
        P(None, "train", "groups"),
        P(None, "train", "groups"),
        P(None, None, "train"),
        P(None, None, "train"),
        P(None, "train"),
        P(None, "train"),
        P(("groups", "train"), None, None, None),
        P(("groups", "train"), None, None, None),
        P(("groups", "train")),
    )
    return jax.shard_map(
        functools.partial(on_device, mesh.shape[AXIS]),
        mesh=mesh,
        in_specs=placed,
        out_specs=P("groups", "train"),
        check_vma=False,
    )
```

time: 436 us -> 168 us (0.39)
  blocking collectives: 221 us -> 0 us
  starting transfers between devices: 0.08 us -> 35.6 us
  waiting for transfers between devices: 138 us -> 107 us
  matrix products: 25.6 us -> 0.78 us
  local copies, waits for them, and re-layouts: 26.2 us -> 1.6 us
  Pallas kernels: 0 us -> 20.5 us
  between operations: 13.8 us -> 0.35 us
  other arithmetic: 10.7 us -> 1.96 us
    unnamed x1 -> x0, blocking collectives: 221 us -> none
    all_gather x3 -> x0, waiting for transfers between devices: 137 us -> none  [the longest x1 59.4 us: on_device(): piece = lax.all_gather(precond, 'train', axis=0, tiled=True)]
    ppermute x0 -> x28, waiting for transfers between devices: none -> 107 us  [the longest x22 63.2 us: swap(): return lax.ppermute(x, AXIS, [(t, t ^ mask) for t in range(n)])]
    ppermute x0 -> x28, starting transfers between devices: none -> 35.6 us  [the longest x22 18.9 us: swap(): return lax.ppermute(x, AXIS, [(t, t ^ mask) for t in range(n)])]
    dot_general x4 -> x0, matrix products: 24.9 us -> none  [the longest x1 11.3 us: on_device(): jnp.einsum('ldc,lcq->dlq', right_part, scaled_right, preferred_element_ty...]
    pallas_call x0 -> x4, Pallas kernels: none -> 20.5 us  [the longest x2 16.6 us: terms(): pl.pallas_call(functools.partial(term_kernel, n, column, first, offsets),...]
    another operation x1 -> x0, local copies, waits for them, and re-layouts: 16.1 us -> none  [on_device(): jnp.stack((term_left, term_right), axis=1)]
    another operation x1 -> x0, other arithmetic: 9.26 us -> none  [on_device(): jnp.stack((term_left, term_right), axis=1)]
  transfers between devices with their start and end apart: 3 -> 28, of which waited for: 3 -> 16; matrix products, arithmetic and copies ran while one was open for 3% -> 2% of each run, Pallas kernels for 0% -> 11%
where the time goes in v2:
time: 168 us; the launch traced here: 167 us
  waiting for transfers between devices  107 us (64%)
  starting transfers between devices  35.6 us (21%)
  Pallas kernels  20.5 us (12%)
  other arithmetic  1.96 us (1%)
    ppermute x22, waiting for transfers between devices, swap(): return lax.ppermute(x, AXIS, [(t, t ^ mask) for t in range(n)])  63.2 us
    ppermute x2, waiting for transfers between devices, fold(): result = jnp.where(inner, result, lax.ppermute(result, AXIS, outward))  30.8 us
    ppermute x22, starting transfers between devices, swap(): return lax.ppermute(x, AXIS, [(t, t ^ mask) for t in range(n)])  18.9 us
    pallas_call x2, Pallas kernels, terms(): pl.pallas_call(functools.partial(term_kernel, n, column, first, offsets),...  16.6 us
    ppermute x2, waiting for transfers between devices, fold(): total = total + lax.ppermute(result, AXIS, inward).astype(F32)  12.7 us
    ppermute x2, starting transfers between devices, fold(): total = total + lax.ppermute(result, AXIS, inward).astype(F32)  12.7 us
    pallas_call x2, Pallas kernels, project(): pl.pallas_call(functools.partial(proj_kernel, n, first), in_specs=[pl.Blo...  3.9 us
  transfers between devices with their start and end apart: 28, of which 16 were waited for; matrix products, arithmetic and copies ran while one was open for 2% of the time, Pallas kernels for 11%

profile of v2, /device:TPU:0, one launch (start us, length us, event | category | flops | bytes accessed | tf_op | source)
XLA Modules:
  0.0 167.4 jit_solution(12108971226982538334)
XLA Ops:
  0.0 3.1 %collective-permute-start.14 = (bf16[2,320,128]{2,1,0:T(8,128)(2,1)}, bf16[2,320,128]{2,1,0:T(8,128)(2,1)S(1)}, u32[]{:S(2)}, u32[]{:S(2)}) collective-permute-start(bf16[2,320,128]{2,1,0:T(8,128)(2,1)} %param.9), channel_id=1, source_target_pairs={{0,4},{1,5},{2,6},{3,7},{4,0},{5,1},{6,2},{7,3},{8,12},{9,13},{10,... | collective-permute-start | bytes 491528 | tf_op jit(solution)/shard_map/ppermute | solution.py:32
  3.1 2.6 %collective-permute-start.15 = (bf16[2,320,128]{2,1,0:T(8,128)(2,1)}, bf16[2,320,128]{2,1,0:T(8,128)(2,1)S(1)}, u32[]{:S(2)}, u32[]{:S(2)}) collective-permute-start(bf16[2,320,128]{2,1,0:T(8,128)(2,1)} %param.9), channel_id=1, source_target_pairs={{0,8},{1,9},{2,10},{3,11},{4,12},{5,13},{6,14},{7,15},{8,0},{9,1},... | collective-permute-start | bytes 491528 | tf_op jit(solution)/shard_map/ppermute | solution.py:32
  5.7 1.0 constant_dynamic-update-slice_fusion.7
  6.7 3.3 %collective-permute-done.14 = bf16[2,320,128]{2,1,0:T(8,128)(2,1)S(1)} collective-permute-done((bf16[2,320,128]{2,1,0:T(8,128)(2,1)}, bf16[2,320,128]{2,1,0:T(8,128)(2,1)S(1)}, u32[]{:S(2)}, u32[]{:S(2)}) %collective-permute-start.14) | collective-permute-done | bytes 163872 | tf_op jit(solution)/shard_map/ppermute | solution.py:32
  10.0 8.3 %collective-permute-done.15 = bf16[2,320,128]{2,1,0:T(8,128)(2,1)S(1)} collective-permute-done((bf16[2,320,128]{2,1,0:T(8,128)(2,1)}, bf16[2,320,128]{2,1,0:T(8,128)(2,1)S(1)}, u32[]{:S(2)}, u32[]{:S(2)}) %collective-permute-start.15) | collective-permute-done | bytes 163872 | tf_op jit(solution)/shard_map/ppermute | solution.py:32
  18.4 1.6 collective-permute-start.17
  20.0 2.6 %collective-permute-start = (bf16[2,320,128]{2,1,0:T(8,128)(2,1)}, bf16[2,320,128]{2,1,0:T(8,128)(2,1)S(1)}, u32[]{:S(2)}, u32[]{:S(2)}) collective-permute-start(bf16[2,320,128]{2,1,0:T(8,128)(2,1)} %param.10), channel_id=1, source_target_pairs={{0,4},{1,5},{2,6},{3,7},{4,0},{5,1},{6,2},{7,3},{8,12},{9,13},{10,... | collective-permute-start | bytes 491528 | tf_op jit(solution)/shard_map/ppermute | solution.py:32
  22.6 1.0 collective-permute-start.1
  23.6 1.5 collective-permute-start.2
  25.1 0.1 collective-permute-start.18
  25.2 2.9 %collective-permute-done = bf16[2,320,128]{2,1,0:T(8,128)(2,1)S(1)} collective-permute-done((bf16[2,320,128]{2,1,0:T(8,128)(2,1)}, bf16[2,320,128]{2,1,0:T(8,128)(2,1)S(1)}, u32[]{:S(2)}, u32[]{:S(2)}) %collective-permute-start) | collective-permute-done | bytes 163872 | tf_op jit(solution)/shard_map/ppermute | solution.py:32
  28.1 4.4 %collective-permute-done.17.refs_1_ = bf16[2,1280,128]{2,1,0:T(8,128)(2,1)S(1)} collective-permute-done((bf16[2,1280,128]{2,1,0:T(8,128)(2,1)S(1)}, bf16[2,1280,128]{2,1,0:T(8,128)(2,1)S(1)}, u32[]{:S(2)}, u32[]{:S(2)}) %collective-permute-start.17) | collective-permute-done | bytes 655392 | tf_op jit(solution)/shard_map/ppermute | solution.py:32
  32.5 4.4 %collective-permute-done.1 = bf16[2,320,128]{2,1,0:T(8,128)(2,1)S(1)} collective-permute-done((bf16[2,320,128]{2,1,0:T(8,128)(2,1)}, bf16[2,320,128]{2,1,0:T(8,128)(2,1)S(1)}, u32[]{:S(2)}, u32[]{:S(2)}) %collective-permute-start.1) | collective-permute-done | bytes 163872 | tf_op jit(solution)/shard_map/ppermute | solution.py:32
  36.8 0.0 collective-permute-done.2
  36.9 0.6 collective-permute-start.3
  37.5 0.1 copy.12
  37.6 8.7 %terms.3 = (bf16[2,2560,128]{2,1,0:T(8,128)(2,1)S(1)}, f32[2,2560,128]{2,1,0:T(8,128)S(1)}) custom-call(s32[1]{0:T(128)} %bitcast.me_ref, bf16[2,1280,128]{2,1,0:T(8,128)(2,1)S(1)} %constant_dynamic-update-slice_fusion.4.refs_0_, bf16[2,1280,128]{2,1,0:T(8,128)(2,1)S(1)} %collective-permute-done.17.refs_1_, ...), custom_call_target="tpu_custom_call" | custom-call | flops 1677721600 | bytes 11796480 | tf_op jit(solution)/shard_map/terms/pallas_call | solution.py:122
  46.4 0.1 collective-permute-start.20
  46.5 0.5 collective-permute-start.4
  47.0 2.8 %collective-permute-done.3.refs_1_ = bf16[2,1280,128]{2,1,0:T(8,128)(2,1)S(1)} collective-permute-done((bf16[2,1280,128]{2,1,0:T(8,128)(2,1)S(1)}, bf16[2,1280,128]{2,1,0:T(8,128)(2,1)S(1)}, u32[]{:S(2)}, u32[]{:S(2)}) %collective-permute-start.3) | collective-permute-done | bytes 655392 | tf_op jit(solution)/shard_map/ppermute | solution.py:32
  49.7 0.7 collective-permute-done.4.refs_2_
  50.4 1.4 collective-permute-done.5.refs_3_
  51.8 7.8 %terms.2 = (bf16[2,2560,128]{2,1,0:T(8,128)(2,1)S(1)}, f32[2,2560,128]{2,1,0:T(8,128)S(1)}) custom-call(s32[1]{0:T(128)} %bitcast.me_ref, bf16[2,1280,128]{2,1,0:T(8,128)(2,1)S(1)} %constant_dynamic-update-slice_fusion.refs_0_, bf16[2,1280,128]{2,1,0:T(8,128)(2,1)S(1)} %collective-permute-done.3.refs_1_, ...), custom_call_target="tpu_custom_call" | custom-call | flops 1677721600 | bytes 11796480 | tf_op jit(solution)/shard_map/terms/pallas_call | solution.py:122
  59.7 0.2 collective-permute-start.6
  59.9 0.2 convert_add_fusion
  60.1 0.1 slice.38
  60.2 1.6 collective-permute-start.21
  61.8 1.0 collective-permute-done.6
  62.8 0.2 convert_add_fusion.1
  63.0 0.1 slice.39
  63.1 1.6 collective-permute-start.7
  64.7 13.2 %collective-permute-done.21 = bf16[2,1280,128]{2,1,0:T(8,128)(2,1)S(1)} collective-permute-done((bf16[2,1280,128]{2,1,0:T(8,128)(2,1)S(1)}, bf16[2,1280,128]{2,1,0:T(8,128)(2,1)S(1)}, u32[]{:S(2)}, u32[]{:S(2)}) %collective-permute-start.21) | collective-permute-done | bytes 655392 | tf_op jit(solution)/shard_map/ppermute | solution.py:32
  77.8 0.1 fusion.3
  78.0 6.3 %collective-permute-start.22 = (bf16[2,1280,128]{2,1,0:T(8,128)(2,1)S(1)}, bf16[2,1280,128]{2,1,0:T(8,128)(2,1)S(1)}, u32[]{:S(2)}, u32[]{:S(2)}) collective-permute-start(bf16[2,1280,128]{2,1,0:T(8,128)(2,1)S(1)} %fusion.3), channel_id=1, source_target_pairs={{0,4},{1,5},{2,6},{3,7},{12,8},{13,9},{14,10},{15,11},{16,20},{17,... | collective-permute-start | bytes 1966088 | tf_op jit(solution)/shard_map/ppermute | solution.py:55
  84.3 7.0 %collective-permute-done.7 = bf16[2,1280,128]{2,1,0:T(8,128)(2,1)S(1)} collective-permute-done((bf16[2,1280,128]{2,1,0:T(8,128)(2,1)S(1)}, bf16[2,1280,128]{2,1,0:T(8,128)(2,1)S(1)}, u32[]{:S(2)}, u32[]{:S(2)}) %collective-permute-start.7) | collective-permute-done | bytes 655392 | tf_op jit(solution)/shard_map/ppermute | solution.py:32
  91.3 0.1 fusion.2
  91.4 6.3 %collective-permute-start.8 = (bf16[2,1280,128]{2,1,0:T(8,128)(2,1)S(1)}, bf16[2,1280,128]{2,1,0:T(8,128)(2,1)S(1)}, u32[]{:S(2)}, u32[]{:S(2)}) collective-permute-start(bf16[2,1280,128]{2,1,0:T(8,128)(2,1)S(1)} %fusion.2), channel_id=1, source_target_pairs={{0,4},{1,5},{2,6},{3,7},{12,8},{13,9},{14,10},{15,11},{16,20},{17,... | collective-permute-start | bytes 1966088 | tf_op jit(solution)/shard_map/ppermute | solution.py:55
  97.8 0.2 fusion.1
  98.0 0.7 collective-permute-start.23
  98.7 12.7 %collective-permute-done.8 = bf16[2,1280,128]{2,1,0:T(8,128)(2,1)S(1)} collective-permute-done((bf16[2,1280,128]{2,1,0:T(8,128)(2,1)S(1)}, bf16[2,1280,128]{2,1,0:T(8,128)(2,1)S(1)}, u32[]{:S(2)}, u32[]{:S(2)}) %collective-permute-start.8) | collective-permute-done | bytes 655392 | tf_op jit(solution)/shard_map/ppermute | solution.py:55
  111.4 0.2 fusion
  111.7 0.7 collective-permute-start.9
  112.4 0.3 add_convert_fusion
  112.7 1.3 collective-permute-start.24
  114.0 0.3 add_convert_fusion.1
  114.3 1.3 collective-permute-start.10
  115.6 18.5 %collective-permute-done.24 = bf16[2,1280,128]{2,1,0:T(8,128)(2,1)S(1)} collective-permute-done((bf16[2,1280,128]{2,1,0:T(8,128)(2,1)S(1)}, bf16[2,1280,128]{2,1,0:T(8,128)(2,1)S(1)}, u32[]{:S(2)}, u32[]{:S(2)}) %collective-permute-start.24) | collective-permute-done | bytes 655392 | tf_op jit(solution)/shard_map/ppermute | solution.py:59
  134.1 0.1 broadcast_select_fusion.pa
  134.2 0.8 collective-permute-start.25
  135.0 12.3 %collective-permute-done.10 = bf16[2,1280,128]{2,1,0:T(8,128)(2,1)S(1)} collective-permute-done((bf16[2,1280,128]{2,1,0:T(8,128)(2,1)S(1)}, bf16[2,1280,128]{2,1,0:T(8,128)(2,1)S(1)}, u32[]{:S(2)}, u32[]{:S(2)}) %collective-permute-start.10) | collective-permute-done | bytes 655392 | tf_op jit(solution)/shard_map/ppermute | solution.py:59
  147.3 0.1 broadcast_select_fusion.1.pa
  147.4 0.6 collective-permute-start.11
  148.0 0.5 collective-permute-start.27
  148.5 0.0 collective-permute-start.12
  148.5 13.9 %collective-permute-done.11.pb = bf16[2,1280,128]{2,1,0:T(8,128)(2,1)S(1)} collective-permute-done((bf16[2,1280,128]{2,1,0:T(8,128)(2,1)S(1)}, bf16[2,1280,128]{2,1,0:T(8,128)(2,1)S(1)}, u32[]{:S(2)}, u32[]{:S(2)}) %collective-permute-start.11) | collective-permute-done | bytes 655392 | tf_op jit(solution)/shard_map/ppermute | solution.py:32
  162.4 0.0 copy-start.1
  162.4 1.9 %project.2.rest_0_ = f32[2,192,128]{2,1,0:T(8,128)S(1)} custom-call(s32[1]{0:T(128)} %bitcast.me_ref, bf16[2,1280,128]{2,1,0:T(8,128)(2,1)S(1)} %broadcast_select_fusion.pa, bf16[2,1280,128]{2,1,0:T(8,128)(2,1)S(1)} %collective-permute-done.25.pb, bf16[2,1280,128]{2,1,0:T(8,128)(2,1)S(1)} %collective-permute-done.26.pc, ...), custom_call_target="tpu_custom_call" | custom-call | flops 503316480 | bytes 6553600 | tf_op jit(solution)/shard_map/project/pallas_call | solution.py:177
  164.4 0.0 copy-start.5
  164.4 0.1 collective-permute-done.13.pd
  164.5 0.0 copy-done.1
  164.5 1.9 %project.3 = f32[6,128]{1,0:T(8,128)S(1)} custom-call(s32[1]{0:T(128)} %bitcast.me_ref, bf16[2,1280,128]{2,1,0:T(8,128)(2,1)S(1)} %broadcast_select_fusion.1.pa, bf16[2,1280,128]{2,1,0:T(8,128)(2,1)S(1)} %collective-permute-done.11.pb, bf16[2,1280,128]{2,1,0:T(8,128)(2,1)S(1)} %collective-permute-done.12.pc, ...), custom_call_target="tpu_custom_call" | custom-call | flops 503316480 | bytes 6553600 | tf_op jit(solution)/shard_map/project/pallas_call | solution.py:177
  166.5 0.1 reshape.8
  166.5 0.1 reduce_sum.9
  166.6 0.8 fusion.4
  (33 shorter events, 0.2 us)
Async XLA Ops:
  0.0 25.1 %copy-start.2 = (bf16[2,320,128]{2,1,0:T(8,128)(2,1)S(1)}, bf16[2,320,128]{2,1,0:T(8,128)(2,1)}, u32[]{:S(2)}) copy-start(bf16[2,320,128]{2,1,0:T(8,128)(2,1)} %param.10) | copy-start | bytes 491524
  0.0 37.5 %copy-start.4 = (f32[2,320]{1,0:T(2,128)S(1)}, f32[2,320]{1,0:T(2,128)}, u32[]{:S(2)}) copy-start(f32[2,320]{1,0:T(2,128)} %param.13) | copy-start | bytes 7684
  0.0 37.5 %copy-start.3 = (f32[2,320]{1,0:T(2,128)S(1)}, f32[2,320]{1,0:T(2,128)}, u32[]{:S(2)}) copy-start(f32[2,320]{1,0:T(2,128)} %param.14) | copy-start | bytes 7684
  0.0 10.0 %collective-permute-start.14 = (bf16[2,320,128]{2,1,0:T(8,128)(2,1)}, bf16[2,320,128]{2,1,0:T(8,128)(2,1)S(1)}, u32[]{:S(2)}, u32[]{:S(2)}) collective-permute-start(bf16[2,320,128]{2,1,0:T(8,128)(2,1)} %param.9), channel_id=1, source_target_pairs={{0,4},{1,5},{2,6},{3,7},{4,0},{5,1},{6,2},{7,3},{8,12},{9,13},{10,... | collective-permute-start | bytes 491528 | tf_op jit(solution)/shard_map/ppermute | solution.py:32
  3.1 15.3 %collective-permute-start.15 = (bf16[2,320,128]{2,1,0:T(8,128)(2,1)}, bf16[2,320,128]{2,1,0:T(8,128)(2,1)S(1)}, u32[]{:S(2)}, u32[]{:S(2)}) collective-permute-start(bf16[2,320,128]{2,1,0:T(8,128)(2,1)} %param.9), channel_id=1, source_target_pairs={{0,8},{1,9},{2,10},{3,11},{4,12},{5,13},{6,14},{7,15},{8,0},{9,1},... | collective-permute-start | bytes 491528 | tf_op jit(solution)/shard_map/ppermute | solution.py:32
  5.7 12.7 %collective-permute-start.16 = (bf16[2,320,128]{2,1,0:T(8,128)(2,1)}, bf16[2,320,128]{2,1,0:T(8,128)(2,1)S(1)}, u32[]{:S(2)}, u32[]{:S(2)}) collective-permute-start(bf16[2,320,128]{2,1,0:T(8,128)(2,1)} %param.9), channel_id=1, source_target_pairs={{0,12},{1,13},{2,14},{3,15},{4,8},{5,9},{6,10},{7,11},{8,4},{9,5},... | collective-permute-start | bytes 491528 | tf_op jit(solution)/shard_map/ppermute | solution.py:32
  18.4 14.0 %collective-permute-start.17 = (bf16[2,1280,128]{2,1,0:T(8,128)(2,1)S(1)}, bf16[2,1280,128]{2,1,0:T(8,128)(2,1)S(1)}, u32[]{:S(2)}, u32[]{:S(2)}) collective-permute-start(bf16[2,1280,128]{2,1,0:T(8,128)(2,1)S(1)} %constant_dynamic-update-slice_fusion.4.refs_0_), channel_id=1, source_target_pairs={{0,2},{1,3},{2,0},{3,1},{4,6},{5,7},{6,4},{7,5},{8,10},{9,11},{10,... | collective-permute-start | bytes 1966088 | tf_op jit(solution)/shard_map/ppermute | solution.py:32
  20.0 8.0 %collective-permute-start = (bf16[2,320,128]{2,1,0:T(8,128)(2,1)}, bf16[2,320,128]{2,1,0:T(8,128)(2,1)S(1)}, u32[]{:S(2)}, u32[]{:S(2)}) collective-permute-start(bf16[2,320,128]{2,1,0:T(8,128)(2,1)} %param.10), channel_id=1, source_target_pairs={{0,4},{1,5},{2,6},{3,7},{4,0},{5,1},{6,2},{7,3},{8,12},{9,13},{10,... | collective-permute-start | bytes 491528 | tf_op jit(solution)/shard_map/ppermute | solution.py:32
  22.6 14.2 %collective-permute-start.1 = (bf16[2,320,128]{2,1,0:T(8,128)(2,1)}, bf16[2,320,128]{2,1,0:T(8,128)(2,1)S(1)}, u32[]{:S(2)}, u32[]{:S(2)}) collective-permute-start(bf16[2,320,128]{2,1,0:T(8,128)(2,1)} %param.10), channel_id=1, source_target_pairs={{0,8},{1,9},{2,10},{3,11},{4,12},{5,13},{6,14},{7,15},{8,0},{9,1},... | collective-permute-start | bytes 491528 | tf_op jit(solution)/shard_map/ppermute | solution.py:32
  23.6 13.2 %collective-permute-start.2 = (bf16[2,320,128]{2,1,0:T(8,128)(2,1)}, bf16[2,320,128]{2,1,0:T(8,128)(2,1)S(1)}, u32[]{:S(2)}, u32[]{:S(2)}) collective-permute-start(bf16[2,320,128]{2,1,0:T(8,128)(2,1)} %param.10), channel_id=1, source_target_pairs={{0,12},{1,13},{2,14},{3,15},{4,8},{5,9},{6,10},{7,11},{8,4},{9,5},... | collective-permute-start | bytes 491528 | tf_op jit(solution)/shard_map/ppermute | solution.py:32
  25.1 12.5 %collective-permute-start.18 = (bf16[2,1280,128]{2,1,0:T(8,128)(2,1)S(1)}, bf16[2,1280,128]{2,1,0:T(8,128)(2,1)S(1)}, u32[]{:S(2)}, u32[]{:S(2)}) collective-permute-start(bf16[2,1280,128]{2,1,0:T(8,128)(2,1)S(1)} %constant_dynamic-update-slice_fusion.4.refs_0_), channel_id=1, source_target_pairs={{0,1},{1,0},{2,3},{3,2},{4,5},{5,4},{6,7},{7,6},{8,9},{9,8},{10,11... | collective-permute-start | bytes 1966088 | tf_op jit(solution)/shard_map/ppermute | solution.py:32
  32.5 5.2 %collective-permute-start.19 = (bf16[2,1280,128]{2,1,0:T(8,128)(2,1)S(1)}, bf16[2,1280,128]{2,1,0:T(8,128)(2,1)}, u32[]{:S(2)}, u32[]{:S(2)}) collective-permute-start(bf16[2,1280,128]{2,1,0:T(8,128)(2,1)S(1)} %collective-permute-done.17.refs_1_), channel_id=1, source_target_pairs={{0,1},{1,0},{2,3},{3,2},{4,5},{5,4},{6,7},{7,6},{8,9},{9,8},{10,11... | collective-permute-start | bytes 1966088 | tf_op jit(solution)/shard_map/ppermute | solution.py:32
  36.9 12.9 %collective-permute-start.3 = (bf16[2,1280,128]{2,1,0:T(8,128)(2,1)S(1)}, bf16[2,1280,128]{2,1,0:T(8,128)(2,1)S(1)}, u32[]{:S(2)}, u32[]{:S(2)}) collective-permute-start(bf16[2,1280,128]{2,1,0:T(8,128)(2,1)S(1)} %constant_dynamic-update-slice_fusion.refs_0_), channel_id=1, source_target_pairs={{0,2},{1,3},{2,0},{3,1},{4,6},{5,7},{6,4},{7,5},{8,10},{9,11},{10,... | collective-permute-start | bytes 1966088 | tf_op jit(solution)/shard_map/ppermute | solution.py:32
  46.4 13.5 %collective-permute-start.20 = (bf16[2,2560,128]{2,1,0:T(8,128)(2,1)S(1)}, bf16[2,2560,128]{2,1,0:T(8,128)(2,1)S(1)}, u32[]{:S(2)}, u32[]{:S(2)}) collective-permute-start(bf16[2,2560,128]{2,1,0:T(8,128)(2,1)S(1)} %get-tuple-element.12), channel_id=1, source_target_pairs={{0,1},{1,0},{2,3},{3,2},{4,5},{5,4},{6,7},{7,6},{8,9},{9,8},{10,11... | collective-permute-start | bytes 3932168 | tf_op jit(solution)/shard_map/ppermute | solution.py:32
  46.5 4.0 %collective-permute-start.4 = (bf16[2,1280,128]{2,1,0:T(8,128)(2,1)S(1)}, bf16[2,1280,128]{2,1,0:T(8,128)(2,1)S(1)}, u32[]{:S(2)}, u32[]{:S(2)}) collective-permute-start(bf16[2,1280,128]{2,1,0:T(8,128)(2,1)S(1)} %constant_dynamic-update-slice_fusion.refs_0_), channel_id=1, source_target_pairs={{0,1},{1,0},{2,3},{3,2},{4,5},{5,4},{6,7},{7,6},{8,9},{9,8},{10,11... | collective-permute-start | bytes 1966088 | tf_op jit(solution)/shard_map/ppermute | solution.py:32
  49.7 2.1 %collective-permute-start.5 = (bf16[2,1280,128]{2,1,0:T(8,128)(2,1)S(1)}, bf16[2,1280,128]{2,1,0:T(8,128)(2,1)S(1)}, u32[]{:S(2)}, u32[]{:S(2)}) collective-permute-start(bf16[2,1280,128]{2,1,0:T(8,128)(2,1)S(1)} %collective-permute-done.3.refs_1_), channel_id=1, source_target_pairs={{0,1},{1,0},{2,3},{3,2},{4,5},{5,4},{6,7},{7,6},{8,9},{9,8},{10,11... | collective-permute-start | bytes 1966088 | tf_op jit(solution)/shard_map/ppermute | solution.py:32
  59.7 3.1 %collective-permute-start.6 = (bf16[2,2560,128]{2,1,0:T(8,128)(2,1)S(1)}, bf16[2,2560,128]{2,1,0:T(8,128)(2,1)S(1)}, u32[]{:S(2)}, u32[]{:S(2)}) collective-permute-start(bf16[2,2560,128]{2,1,0:T(8,128)(2,1)S(1)} %get-tuple-element.10), channel_id=1, source_target_pairs={{0,1},{1,0},{2,3},{3,2},{4,5},{5,4},{6,7},{7,6},{8,9},{9,8},{10,11... | collective-permute-start | bytes 3932168 | tf_op jit(solution)/shard_map/ppermute | solution.py:32
  60.2 17.6 %collective-permute-start.21 = (bf16[2,1280,128]{2,1,0:T(8,128)(2,1)S(1)}, bf16[2,1280,128]{2,1,0:T(8,128)(2,1)S(1)}, u32[]{:S(2)}, u32[]{:S(2)}) collective-permute-start(bf16[2,1280,128]{2,1,0:T(8,128)(2,1)S(1)} %slice.38), channel_id=1, source_target_pairs={{0,2},{1,3},{2,0},{3,1},{4,6},{5,7},{6,4},{7,5},{8,10},{9,11},{10,... | collective-permute-start | bytes 1966088 | tf_op jit(solution)/shard_map/ppermute | solution.py:32
  63.1 28.2 %collective-permute-start.7 = (bf16[2,1280,128]{2,1,0:T(8,128)(2,1)S(1)}, bf16[2,1280,128]{2,1,0:T(8,128)(2,1)S(1)}, u32[]{:S(2)}, u32[]{:S(2)}) collective-permute-start(bf16[2,1280,128]{2,1,0:T(8,128)(2,1)S(1)} %slice.39), channel_id=1, source_target_pairs={{0,2},{1,3},{2,0},{3,1},{4,6},{5,7},{6,4},{7,5},{8,10},{9,11},{10,... | collective-permute-start | bytes 1966088 | tf_op jit(solution)/shard_map/ppermute | solution.py:32
  78.0 19.8 %collective-permute-start.22 = (bf16[2,1280,128]{2,1,0:T(8,128)(2,1)S(1)}, bf16[2,1280,128]{2,1,0:T(8,128)(2,1)S(1)}, u32[]{:S(2)}, u32[]{:S(2)}) collective-permute-start(bf16[2,1280,128]{2,1,0:T(8,128)(2,1)S(1)} %fusion.3), channel_id=1, source_target_pairs={{0,4},{1,5},{2,6},{3,7},{12,8},{13,9},{14,10},{15,11},{16,20},{17,... | collective-permute-start | bytes 1966088 | tf_op jit(solution)/shard_map/ppermute | solution.py:55
  91.4 20.0 %collective-permute-start.8 = (bf16[2,1280,128]{2,1,0:T(8,128)(2,1)S(1)}, bf16[2,1280,128]{2,1,0:T(8,128)(2,1)S(1)}, u32[]{:S(2)}, u32[]{:S(2)}) collective-permute-start(bf16[2,1280,128]{2,1,0:T(8,128)(2,1)S(1)} %fusion.2), channel_id=1, source_target_pairs={{0,4},{1,5},{2,6},{3,7},{12,8},{13,9},{14,10},{15,11},{16,20},{17,... | collective-permute-start | bytes 1966088 | tf_op jit(solution)/shard_map/ppermute | solution.py:55
  98.0 14.3 %collective-permute-start.23 = (bf16[2,1280,128]{2,1,0:T(8,128)(2,1)S(1)}, bf16[2,1280,128]{2,1,0:T(8,128)(2,1)S(1)}, u32[]{:S(2)}, u32[]{:S(2)}) collective-permute-start(bf16[2,1280,128]{2,1,0:T(8,128)(2,1)S(1)} %fusion.1), channel_id=1, source_target_pairs={{4,8},{5,9},{6,10},{7,11},{8,4},{9,5},{10,6},{11,7},{20,24},{21,25... | collective-permute-start | bytes 1966088 | tf_op jit(solution)/shard_map/ppermute | solution.py:56
  111.7 2.3 %collective-permute-start.9 = (bf16[2,1280,128]{2,1,0:T(8,128)(2,1)S(1)}, bf16[2,1280,128]{2,1,0:T(8,128)(2,1)S(1)}, u32[]{:S(2)}, u32[]{:S(2)}) collective-permute-start(bf16[2,1280,128]{2,1,0:T(8,128)(2,1)S(1)} %fusion), channel_id=1, source_target_pairs={{4,8},{5,9},{6,10},{7,11},{8,4},{9,5},{10,6},{11,7},{20,24},{21,25... | collective-permute-start | bytes 1966088 | tf_op jit(solution)/shard_map/ppermute | solution.py:56
  112.7 21.4 %collective-permute-start.24 = (bf16[2,1280,128]{2,1,0:T(8,128)(2,1)S(1)}, bf16[2,1280,128]{2,1,0:T(8,128)(2,1)S(1)}, u32[]{:S(2)}, u32[]{:S(2)}) collective-permute-start(bf16[2,1280,128]{2,1,0:T(8,128)(2,1)S(1)} %add_convert_fusion), channel_id=1, source_target_pairs={{4,0},{5,1},{6,2},{7,3},{8,12},{9,13},{10,14},{11,15},{20,16},{21,... | collective-permute-start | bytes 1966088 | tf_op jit(solution)/shard_map/ppermute | solution.py:59
  114.3 33.0 %collective-permute-start.10 = (bf16[2,1280,128]{2,1,0:T(8,128)(2,1)S(1)}, bf16[2,1280,128]{2,1,0:T(8,128)(2,1)S(1)}, u32[]{:S(2)}, u32[]{:S(2)}) collective-permute-start(bf16[2,1280,128]{2,1,0:T(8,128)(2,1)S(1)} %add_convert_fusion.1), channel_id=1, source_target_pairs={{4,0},{5,1},{6,2},{7,3},{8,12},{9,13},{10,14},{11,15},{20,16},{21,... | collective-permute-start | bytes 1966088 | tf_op jit(solution)/shard_map/ppermute | solution.py:59
  134.1 28.3 %copy-start = (bf16[6,2,32,5120]{3,2,1,0:T(8,128)(2,1)S(1)}, bf16[6,2,32,5120]{3,2,1,0:T(8,128)(2,1)}, u32[]{:S(2)}) copy-start(bf16[6,2,32,5120]{3,2,1,0:T(8,128)(2,1)} %train.2) | copy-start | bytes 11796484
  134.2 13.8 %collective-permute-start.25 = (bf16[2,1280,128]{2,1,0:T(8,128)(2,1)S(1)}, bf16[2,1280,128]{2,1,0:T(8,128)(2,1)S(1)}, u32[]{:S(2)}, u32[]{:S(2)}) collective-permute-start(bf16[2,1280,128]{2,1,0:T(8,128)(2,1)S(1)} %broadcast_select_fusion.pa), channel_id=1, source_target_pairs={{0,2},{1,3},{2,0},{3,1},{4,6},{5,7},{6,4},{7,5},{8,10},{9,11},{10,... | collective-permute-start | bytes 1966088 | tf_op jit(solution)/shard_map/ppermute | solution.py:32
  147.4 15.0 %collective-permute-start.11 = (bf16[2,1280,128]{2,1,0:T(8,128)(2,1)S(1)}, bf16[2,1280,128]{2,1,0:T(8,128)(2,1)S(1)}, u32[]{:S(2)}, u32[]{:S(2)}) collective-permute-start(bf16[2,1280,128]{2,1,0:T(8,128)(2,1)S(1)} %broadcast_select_fusion.1.pa), channel_id=1, source_target_pairs={{0,2},{1,3},{2,0},{3,1},{4,6},{5,7},{6,4},{7,5},{8,10},{9,11},{10,... | collective-permute-start | bytes 1966088 | tf_op jit(solution)/shard_map/ppermute | solution.py:32
  148.0 14.4 %collective-permute-start.26 = (bf16[2,1280,128]{2,1,0:T(8,128)(2,1)S(1)}, bf16[2,1280,128]{2,1,0:T(8,128)(2,1)S(1)}, u32[]{:S(2)}, u32[]{:S(2)}) collective-permute-start(bf16[2,1280,128]{2,1,0:T(8,128)(2,1)S(1)} %broadcast_select_fusion.pa), channel_id=1, source_target_pairs={{0,1},{1,0},{2,3},{3,2},{4,5},{5,4},{6,7},{7,6},{8,9},{9,8},{10,11... | collective-permute-start | bytes 1966088 | tf_op jit(solution)/shard_map/ppermute | solution.py:32
  148.0 14.4 %collective-permute-start.27 = (bf16[2,1280,128]{2,1,0:T(8,128)(2,1)S(1)}, bf16[2,1280,128]{2,1,0:T(8,128)(2,1)S(1)}, u32[]{:S(2)}, u32[]{:S(2)}) collective-permute-start(bf16[2,1280,128]{2,1,0:T(8,128)(2,1)S(1)} %collective-permute-done.25.pb), channel_id=1, source_target_pairs={{0,1},{1,0},{2,3},{3,2},{4,5},{5,4},{6,7},{7,6},{8,9},{9,8},{10,11... | collective-permute-start | bytes 1966088 | tf_op jit(solution)/shard_map/ppermute | solution.py:32
  148.5 15.9 %collective-permute-start.12 = (bf16[2,1280,128]{2,1,0:T(8,128)(2,1)S(1)}, bf16[2,1280,128]{2,1,0:T(8,128)(2,1)S(1)}, u32[]{:S(2)}, u32[]{:S(2)}) collective-permute-start(bf16[2,1280,128]{2,1,0:T(8,128)(2,1)S(1)} %broadcast_select_fusion.1.pa), channel_id=1, source_target_pairs={{0,1},{1,0},{2,3},{3,2},{4,5},{5,4},{6,7},{7,6},{8,9},{9,8},{10,11... | collective-permute-start | bytes 1966088 | tf_op jit(solution)/shard_map/ppermute | solution.py:32
  162.4 2.1 %collective-permute-start.13 = (bf16[2,1280,128]{2,1,0:T(8,128)(2,1)S(1)}, bf16[2,1280,128]{2,1,0:T(8,128)(2,1)S(1)}, u32[]{:S(2)}, u32[]{:S(2)}) collective-permute-start(bf16[2,1280,128]{2,1,0:T(8,128)(2,1)S(1)} %collective-permute-done.11.pb), channel_id=1, source_target_pairs={{0,1},{1,0},{2,3},{3,2},{4,5},{5,4},{6,7},{7,6},{8,9},{9,8},{10,11... | collective-permute-start | bytes 1966088 | tf_op jit(solution)/shard_map/ppermute | solution.py:32
  162.4 2.1 %copy-start.1 = (bf16[6,2,32,5120]{3,2,1,0:T(8,128)(2,1)S(1)}, bf16[6,2,32,5120]{3,2,1,0:T(8,128)(2,1)}, u32[]{:S(2)}) copy-start(bf16[6,2,32,5120]{3,2,1,0:T(8,128)(2,1)} %train.3) | copy-start | bytes 11796484
  164.4 2.3 %copy-start.5 = (s32[128]{0:T(128)S(1)}, s32[128]{0:T(128)}, u32[]{:S(2)}) copy-start(s32[128]{0:T(128)} %param.17) | copy-start | bytes 1540

commit v3 on v2

--- a/solution.py
+++ b/solution.py
@@ -41,22 +41,26 @@
     return block, ks
 
 
-def fold(total, me, n):
+def sum_far(total, me, n):
     result = total.astype(BF16)
     for bit, bits in far_stages(n, 2):
         if bits == 1:
             total = total + swap(result, n, bit).astype(F32)
             result = total.astype(BF16)
             continue
-        place = lambda t: (t // bit) % 4
-        inward = [(t, t ^ bit) for t in range(n) if place(t) in (0, 3)]
-        outward = [(b, a) for a, b in inward]
-        middle = [(t, t ^ (3 * bit)) for t in range(n) if place(t) in (1, 2)]
-        total = total + lax.ppermute(result, AXIS, inward).astype(F32)
-        total = total + lax.ppermute(total.astype(BF16), AXIS, middle).astype(F32)
-        result = total.astype(BF16)
-        inner = (place(me) == 1) | (place(me) == 2)
-        result = jnp.where(inner, result, lax.ppermute(result, AXIS, outward))
+        place = (me // bit) % 4
+        first = (place == 0) | (place == 3)
+        half = total.shape[1] // 2
+        low, high = total[:, :half], total[:, half:]
+        mine = jnp.where(first, low, high)
+        theirs = jnp.where(first, high, low).astype(BF16)
+        mine = mine + swap(theirs, n, bit).astype(F32)
+        mine = mine + swap(mine.astype(BF16), n, 3 * bit).astype(F32)
+        mine = mine.astype(BF16)
+        theirs = swap(mine, n, bit)
+        result = jnp.concatenate(
+            [jnp.where(first, mine, theirs), jnp.where(first, theirs, mine)], axis=1
+        )
         total = result.astype(F32)
     return result
 
@@ -224,8 +228,10 @@
         halves.append(half[:, :quarter] + swap(aways[i], n, 2).astype(F32))
     total, left = 0.0, ()
     for i, (first, side) in enumerate(chunks):
-        precond = gather_near(fold(halves[i], me[0], n), n)
-        left = (project(me, precond, sides[side][2], first, n, left),)
+        block = sum_far(halves[i], me[0], n)
+        across = swap(block, n, 2)
+        corner = swap(after(across, left), n, 1)
+        left = (project(me, (block, across, swap(block, n, 1), corner), sides[side][2], first, n, left),)
         if side:
             total, left = total + left[0], ()
     table_scores = jnp.sum(total.reshape(tables, QUERIES, R), axis=2).T

time: 168 us -> 162 us (0.964)
  waiting for transfers between devices: 107 us -> 87.8 us
  local copies, waits for them, and re-layouts: 1.6 us -> 9.06 us
  other arithmetic: 1.96 us -> 4.49 us
  Pallas kernels: 20.5 us -> 22.6 us
    ppermute x6 -> x0, waiting for transfers between devices: 43.5 us -> none  [the longest x2 30.8 us: fold(): result = jnp.where(inner, result, lax.ppermute(result, AXIS, outward))]
    ppermute x22 -> x28, waiting for transfers between devices: 63.2 us -> 87.8 us  [swap(): return lax.ppermute(x, AXIS, [(t, t ^ mask) for t in range(n)])]
    ppermute x22 -> x28, starting transfers between devices: 18.9 us -> 36.5 us  [swap(): return lax.ppermute(x, AXIS, [(t, t ^ mask) for t in range(n)])]
    ppermute x6 -> x0, starting transfers between devices: 16.7 us -> none  [the longest x2 12.7 us: fold(): total = total + lax.ppermute(result, AXIS, inward).astype(F32)]
    unnamed x18 -> x38, local copies, waits for them, and re-layouts: 1.16 us -> 8.62 us
    add x2, other arithmetic: 0.43 us -> 3.27 us  [on_device(): half = keep + swap(send, n, 1).astype(F32)]
    pallas_call x2, Pallas kernels: 16.6 us -> 18.7 us  [terms(): pl.pallas_call(functools.partial(term_kernel, n, column, first, offsets),...]
  transfers between devices with their start and end apart: 28 -> 28, of which waited for: 16 -> 18; matrix products, arithmetic and copies ran while one was open for 2% -> 4% of each run, Pallas kernels for 11% -> 13%
where the time goes in v3:
time: 162 us; the launch traced here: 161 us
  waiting for transfers between devices  87.8 us (54%)
  starting transfers between devices  36.5 us (23%)
  Pallas kernels  22.6 us (14%)
  local copies, waits for them, and re-layouts  9.06 us (6%)
  other arithmetic  4.49 us (3%)
    ppermute x28, waiting for transfers between devices, swap(): return lax.ppermute(x, AXIS, [(t, t ^ mask) for t in range(n)])  87.8 us
    ppermute x28, starting transfers between devices, swap(): return lax.ppermute(x, AXIS, [(t, t ^ mask) for t in range(n)])  36.5 us
    pallas_call x2, Pallas kernels, terms(): pl.pallas_call(functools.partial(term_kernel, n, column, first, offsets),...  18.7 us
    unnamed x38, local copies, waits for them, and re-layouts  8.62 us
    pallas_call x2, Pallas kernels, project(): pl.pallas_call(functools.partial(proj_kernel, n, first), in_specs=[pl.Blo...  3.87 us
    add x2, other arithmetic, on_device(): half = keep + swap(send, n, 1).astype(F32)  3.27 us
  transfers between devices with their start and end apart: 28, of which 18 were waited for; matrix products, arithmetic and copies ran while one was open for 4% of the time, Pallas kernels for 13%

profile of v3, /device:TPU:0, one launch (start us, length us, event | category | flops | bytes accessed | tf_op | source)
XLA Modules:
  0.0 161.5 jit_solution(8675263455694208720)
XLA Ops:
  0.0 3.1 %collective-permute-start.13 = (bf16[2,320,128]{2,1,0:T(8,128)(2,1)}, bf16[2,320,128]{2,1,0:T(8,128)(2,1)S(1)}, u32[]{:S(2)}, u32[]{:S(2)}) collective-permute-start(bf16[2,320,128]{2,1,0:T(8,128)(2,1)} %param.9), channel_id=1, source_target_pairs={{0,4},{1,5},{2,6},{3,7},{4,0},{5,1},{6,2},{7,3},{8,12},{9,13},{10,... | collective-permute-start | bytes 491528 | tf_op jit(solution)/shard_map/ppermute | solution.py:32
  3.1 2.6 %collective-permute-start.14 = (bf16[2,320,128]{2,1,0:T(8,128)(2,1)}, bf16[2,320,128]{2,1,0:T(8,128)(2,1)S(1)}, u32[]{:S(2)}, u32[]{:S(2)}) collective-permute-start(bf16[2,320,128]{2,1,0:T(8,128)(2,1)} %param.9), channel_id=1, source_target_pairs={{0,8},{1,9},{2,10},{3,11},{4,12},{5,13},{6,14},{7,15},{8,0},{9,1},... | collective-permute-start | bytes 491528 | tf_op jit(solution)/shard_map/ppermute | solution.py:32
  5.7 1.0 constant_dynamic-update-slice_fusion.7
  6.7 3.3 %collective-permute-done.13 = bf16[2,320,128]{2,1,0:T(8,128)(2,1)S(1)} collective-permute-done((bf16[2,320,128]{2,1,0:T(8,128)(2,1)}, bf16[2,320,128]{2,1,0:T(8,128)(2,1)S(1)}, u32[]{:S(2)}, u32[]{:S(2)}) %collective-permute-start.13) | collective-permute-done | bytes 163872 | tf_op jit(solution)/shard_map/ppermute | solution.py:32
  10.0 8.4 %collective-permute-done.14 = bf16[2,320,128]{2,1,0:T(8,128)(2,1)S(1)} collective-permute-done((bf16[2,320,128]{2,1,0:T(8,128)(2,1)}, bf16[2,320,128]{2,1,0:T(8,128)(2,1)S(1)}, u32[]{:S(2)}, u32[]{:S(2)}) %collective-permute-start.14) | collective-permute-done | bytes 163872 | tf_op jit(solution)/shard_map/ppermute | solution.py:32
  18.4 1.6 collective-permute-start.16
  20.0 2.6 %collective-permute-start = (bf16[2,320,128]{2,1,0:T(8,128)(2,1)}, bf16[2,320,128]{2,1,0:T(8,128)(2,1)S(1)}, u32[]{:S(2)}, u32[]{:S(2)}) collective-permute-start(bf16[2,320,128]{2,1,0:T(8,128)(2,1)} %param.10), channel_id=1, source_target_pairs={{0,4},{1,5},{2,6},{3,7},{4,0},{5,1},{6,2},{7,3},{8,12},{9,13},{10,... | collective-permute-start | bytes 491528 | tf_op jit(solution)/shard_map/ppermute | solution.py:32
  22.7 1.0 collective-permute-start.1
  23.6 1.5 collective-permute-start.2
  25.2 2.9 %collective-permute-done = bf16[2,320,128]{2,1,0:T(8,128)(2,1)S(1)} collective-permute-done((bf16[2,320,128]{2,1,0:T(8,128)(2,1)}, bf16[2,320,128]{2,1,0:T(8,128)(2,1)S(1)}, u32[]{:S(2)}, u32[]{:S(2)}) %collective-permute-start) | collective-permute-done | bytes 163872 | tf_op jit(solution)/shard_map/ppermute | solution.py:32
  28.1 4.4 %collective-permute-done.16.refs_1_ = bf16[2,1280,128]{2,1,0:T(8,128)(2,1)S(1)} collective-permute-done((bf16[2,1280,128]{2,1,0:T(8,128)(2,1)S(1)}, bf16[2,1280,128]{2,1,0:T(8,128)(2,1)S(1)}, u32[]{:S(2)}, u32[]{:S(2)}) %collective-permute-start.16) | collective-permute-done | bytes 655392 | tf_op jit(solution)/shard_map/ppermute | solution.py:32
  32.5 4.4 %collective-permute-done.1 = bf16[2,320,128]{2,1,0:T(8,128)(2,1)S(1)} collective-permute-done((bf16[2,320,128]{2,1,0:T(8,128)(2,1)}, bf16[2,320,128]{2,1,0:T(8,128)(2,1)S(1)}, u32[]{:S(2)}, u32[]{:S(2)}) %collective-permute-start.1) | collective-permute-done | bytes 163872 | tf_op jit(solution)/shard_map/ppermute | solution.py:32
  36.9 0.6 collective-permute-start.3
  37.5 0.1 copy.12
  37.7 0.8 copy-done.8
  38.5 0.8 copy-done.10
  39.3 1.1 copy-done.5
  40.4 1.1 copy-done.7
  41.5 1.1 copy-done.9
  42.6 1.1 copy-done.11
  43.7 8.7 %terms.3 = (bf16[2,2560,128]{2,1,0:T(8,128)(2,1)}, f32[2,2560,128]{2,1,0:T(8,128)S(1)}) custom-call(s32[1]{0:T(128)} %bitcast.me_ref, bf16[2,1280,128]{2,1,0:T(8,128)(2,1)S(1)} %copy-done.5, bf16[2,1280,128]{2,1,0:T(8,128)(2,1)S(1)} %copy-done.7, bf16[2,1280,128]{2,1,0:T(8,128)(2,1)S(1)} %copy-done.9, bf16[2,1280,128]{2,1,0:T(8,128)(2,1)S(1)} %copy-done.11, ...), custom_call_target="tpu_custom_call" | custom-call | flops 1677721600 | bytes 11796480 | tf_op jit(solution)/shard_map/terms/pallas_call | solution.py:126
  52.5 0.5 collective-permute-start.4
  53.0 0.1 collective-permute-start.5
  53.1 3.9 %collective-permute-done.4.refs_2_ = bf16[2,1280,128]{2,1,0:T(8,128)(2,1)S(1)} collective-permute-done((bf16[2,1280,128]{2,1,0:T(8,128)(2,1)S(1)}, bf16[2,1280,128]{2,1,0:T(8,128)(2,1)S(1)}, u32[]{:S(2)}, u32[]{:S(2)}) %collective-permute-start.4) | collective-permute-done | bytes 655392 | tf_op jit(solution)/shard_map/ppermute | solution.py:32
  57.1 0.6 collective-permute-done.5.refs_3_
  57.6 10.0 %terms.2 = (bf16[2,2560,128]{2,1,0:T(8,128)(2,1)}, f32[2,2560,128]{2,1,0:T(8,128)S(1)}) custom-call(s32[1]{0:T(128)} %bitcast.me_ref, bf16[2,1280,128]{2,1,0:T(8,128)(2,1)S(1)} %constant_dynamic-update-slice_fusion.refs_0_, bf16[2,1280,128]{2,1,0:T(8,128)(2,1)} %collective-permute-done.3.refs_1_, bf16[2,1280,128]{2,1,0:T(8,128)(2,1)S(1)} %collective-permute-done.4.refs_2_, ...), custom_call_target="tpu_custom_call" | custom-call | flops 1677721600 | bytes 11796480 | tf_op jit(solution)/shard_map/terms/pallas_call | solution.py:126
  67.6 1.5 copy-done.2
  69.1 0.1 collective-permute-start.6
  69.2 1.7 %convert_add_fusion = f32[2,2560,128]{2,1,0:T(8,128)S(1)} fusion(f32[2,2560,128]{2,1,0:T(8,128)S(1)} %get-tuple-element.12, bf16[2,2560,128]{2,1,0:T(8,128)(2,1)} %collective-permute-done.19), kind=kLoop, calls=%fused_computation | loop fusion | flops 1310720 | bytes 6553600 | tf_op jit(solution)/shard_map/add | solution.py:225
  70.9 0.1 slice.70
  71.0 1.6 collective-permute-start.20
  72.6 1.6 convert_add_fusion.1
  74.2 0.1 slice.71
  74.3 1.4 collective-permute-start.7
  75.7 12.9 %collective-permute-done.20 = bf16[2,1280,128]{2,1,0:T(8,128)(2,1)S(1)} collective-permute-done((bf16[2,1280,128]{2,1,0:T(8,128)(2,1)S(1)}, bf16[2,1280,128]{2,1,0:T(8,128)(2,1)S(1)}, u32[]{:S(2)}, u32[]{:S(2)}) %collective-permute-start.20) | collective-permute-done | bytes 655392 | tf_op jit(solution)/shard_map/ppermute | solution.py:32
  88.6 0.1 slice_add_fusion
  88.8 2.3 %collective-permute-start.21 = (bf16[2,640,128]{2,1,0:T(8,128)(2,1)S(1)}, bf16[2,640,128]{2,1,0:T(8,128)(2,1)S(1)}, u32[]{:S(2)}, u32[]{:S(2)}) collective-permute-start(bf16[2,640,128]{2,1,0:T(8,128)(2,1)S(1)} %select_convert_fusion), channel_id=1, source_target_pairs={{0,4},{1,5},{2,6},{3,7},{4,0},{5,1},{6,2},{7,3},{8,12},{9,13},{10,... | collective-permute-start | bytes 983048 | tf_op jit(solution)/shard_map/ppermute | solution.py:32
  91.2 6.9 %collective-permute-done.21 = bf16[2,640,128]{2,1,0:T(8,128)(2,1)S(1)} collective-permute-done((bf16[2,640,128]{2,1,0:T(8,128)(2,1)S(1)}, bf16[2,640,128]{2,1,0:T(8,128)(2,1)S(1)}, u32[]{:S(2)}, u32[]{:S(2)}) %collective-permute-start.21) | collective-permute-done | bytes 327712 | tf_op jit(solution)/shard_map/ppermute | solution.py:32
  98.0 0.1 fusion.1
  98.1 2.6 %collective-permute-start.22 = (bf16[2,640,128]{2,1,0:T(8,128)(2,1)S(1)}, bf16[2,640,128]{2,1,0:T(8,128)(2,1)S(1)}, u32[]{:S(2)}, u32[]{:S(2)}) collective-permute-start(bf16[2,640,128]{2,1,0:T(8,128)(2,1)S(1)} %fusion.1), channel_id=1, source_target_pairs={{0,12},{1,13},{2,14},{3,15},{4,8},{5,9},{6,10},{7,11},{8,4},{9,5},... | collective-permute-start | bytes 983048 | tf_op jit(solution)/shard_map/ppermute | solution.py:32
  100.8 1.3 collective-permute-done.7
  102.1 0.2 slice_add_fusion.1
  102.3 2.3 %collective-permute-start.8 = (bf16[2,640,128]{2,1,0:T(8,128)(2,1)S(1)}, bf16[2,640,128]{2,1,0:T(8,128)(2,1)S(1)}, u32[]{:S(2)}, u32[]{:S(2)}) collective-permute-start(bf16[2,640,128]{2,1,0:T(8,128)(2,1)S(1)} %select_convert_fusion.1), channel_id=1, source_target_pairs={{0,4},{1,5},{2,6},{3,7},{4,0},{5,1},{6,2},{7,3},{8,12},{9,13},{10,... | collective-permute-start | bytes 983048 | tf_op jit(solution)/shard_map/ppermute | solution.py:32
  104.7 3.9 %collective-permute-done.22 = bf16[2,640,128]{2,1,0:T(8,128)(2,1)S(1)} collective-permute-done((bf16[2,640,128]{2,1,0:T(8,128)(2,1)S(1)}, bf16[2,640,128]{2,1,0:T(8,128)(2,1)S(1)}, u32[]{:S(2)}, u32[]{:S(2)}) %collective-permute-start.22) | collective-permute-done | bytes 327712 | tf_op jit(solution)/shard_map/ppermute | solution.py:32
  108.6 0.2 add_convert_fusion
  108.8 6.1 %collective-permute-start.23 = (bf16[2,640,128]{2,1,0:T(8,128)(2,1)S(1)}, bf16[2,640,128]{2,1,0:T(8,128)(2,1)S(1)}, u32[]{:S(2)}, u32[]{:S(2)}) collective-permute-start(bf16[2,640,128]{2,1,0:T(8,128)(2,1)S(1)} %add_convert_fusion), channel_id=1, source_target_pairs={{0,4},{1,5},{2,6},{3,7},{4,0},{5,1},{6,2},{7,3},{8,12},{9,13},{10,... | collective-permute-start | bytes 983048 | tf_op jit(solution)/shard_map/ppermute | solution.py:32
  114.9 0.3 collective-permute-done.8
  115.2 0.1 fusion
  115.3 2.6 %collective-permute-start.9 = (bf16[2,640,128]{2,1,0:T(8,128)(2,1)S(1)}, bf16[2,640,128]{2,1,0:T(8,128)(2,1)S(1)}, u32[]{:S(2)}, u32[]{:S(2)}) collective-permute-start(bf16[2,640,128]{2,1,0:T(8,128)(2,1)S(1)} %fusion), channel_id=1, source_target_pairs={{0,12},{1,13},{2,14},{3,15},{4,8},{5,9},{6,10},{7,11},{8,4},{9,5},... | collective-permute-start | bytes 983048 | tf_op jit(solution)/shard_map/ppermute | solution.py:32
  117.9 5.1 %collective-permute-done.23 = bf16[2,640,128]{2,1,0:T(8,128)(2,1)S(1)} collective-permute-done((bf16[2,640,128]{2,1,0:T(8,128)(2,1)S(1)}, bf16[2,640,128]{2,1,0:T(8,128)(2,1)S(1)}, u32[]{:S(2)}, u32[]{:S(2)}) %collective-permute-start.23) | collective-permute-done | bytes 327712 | tf_op jit(solution)/shard_map/ppermute | solution.py:32
  123.2 1.6 collective-permute-start.24
  124.7 6.4 %collective-permute-done.9 = bf16[2,640,128]{2,1,0:T(8,128)(2,1)S(1)} collective-permute-done((bf16[2,640,128]{2,1,0:T(8,128)(2,1)S(1)}, bf16[2,640,128]{2,1,0:T(8,128)(2,1)S(1)}, u32[]{:S(2)}, u32[]{:S(2)}) %collective-permute-start.9) | collective-permute-done | bytes 327712 | tf_op jit(solution)/shard_map/ppermute | solution.py:32
  131.1 0.1 add_convert_fusion.1
  131.4 7.6 %collective-permute-done.10 = bf16[2,640,128]{2,1,0:T(8,128)(2,1)S(1)} collective-permute-done((bf16[2,640,128]{2,1,0:T(8,128)(2,1)S(1)}, bf16[2,640,128]{2,1,0:T(8,128)(2,1)S(1)}, u32[]{:S(2)}, u32[]{:S(2)}) %collective-permute-start.10) | collective-permute-done | bytes 327712 | tf_op jit(solution)/shard_map/ppermute | solution.py:32
  139.3 1.6 collective-permute-start.11
  140.8 0.2 collective-permute-start.12
  141.1 0.2 collective-permute-done.26.pd
  141.3 1.9 %project.2.rest_0_ = f32[2,192,128]{2,1,0:T(8,128)S(1)} custom-call(s32[1]{0:T(128)} %bitcast.me_ref, bf16[2,1280,128]{2,1,0:T(8,128)(2,1)S(1)} %pad_maximum_fusion.1.pa, bf16[2,1280,128]{2,1,0:T(8,128)(2,1)S(1)} %collective-permute-done.24.pb, bf16[2,1280,128]{2,1,0:T(8,128)(2,1)S(1)} %collective-permute-done.25.pc, ...), custom_call_target="tpu_custom_call" | custom-call | flops 503316480 | bytes 6553600 | tf_op jit(solution)/shard_map/project/pallas_call | solution.py:181
  143.3 13.2 %collective-permute-done.11.pb = bf16[2,1280,128]{2,1,0:T(8,128)(2,1)S(1)} collective-permute-done((bf16[2,1280,128]{2,1,0:T(8,128)(2,1)S(1)}, bf16[2,1280,128]{2,1,0:T(8,128)(2,1)S(1)}, u32[]{:S(2)}, u32[]{:S(2)}) %collective-permute-start.11) | collective-permute-done | bytes 655392 | tf_op jit(solution)/shard_map/ppermute | solution.py:32
  156.5 2.1 %collective-permute-done.27.pd = bf16[2,1280,128]{2,1,0:T(8,128)(2,1)S(1)} collective-permute-done((bf16[2,1280,128]{2,1,0:T(8,128)(2,1)S(1)}, bf16[2,1280,128]{2,1,0:T(8,128)(2,1)S(1)}, u32[]{:S(2)}, u32[]{:S(2)}) %collective-permute-start.27) | collective-permute-done | bytes 655392 | tf_op jit(solution)/shard_map/ppermute | solution.py:32
  158.6 1.9 %project.3 = f32[6,128]{1,0:T(8,128)S(1)} custom-call(s32[1]{0:T(128)} %bitcast.me_ref, bf16[2,1280,128]{2,1,0:T(8,128)(2,1)S(1)} %pad_maximum_fusion.pa, bf16[2,1280,128]{2,1,0:T(8,128)(2,1)S(1)} %collective-permute-done.11.pb, bf16[2,1280,128]{2,1,0:T(8,128)(2,1)S(1)} %collective-permute-done.12.pc, bf16[2,1280,128]{2,1,0:T(8,128)(2,1)S(1)} %collective-permute-done.27.pd, ...), custom_call_target="tpu_custom_call" | custom-call | flops 503316480 | bytes 6553600 | tf_op jit(solution)/shard_map/project/pallas_call | solution.py:181
  160.5 0.1 reshape.8
  160.6 0.1 reduce_sum.9
  160.7 0.8 fusion.2
  (57 shorter events, 0.9 us)
Async XLA Ops:
  0.0 25.1 %copy-start.12 = (bf16[2,320,128]{2,1,0:T(8,128)(2,1)S(1)}, bf16[2,320,128]{2,1,0:T(8,128)(2,1)}, u32[]{:S(2)}) copy-start(bf16[2,320,128]{2,1,0:T(8,128)(2,1)} %param.10) | copy-start | bytes 491524
  0.0 37.5 %copy-start.14 = (f32[2,320]{1,0:T(2,128)S(1)}, f32[2,320]{1,0:T(2,128)}, u32[]{:S(2)}) copy-start(f32[2,320]{1,0:T(2,128)} %param.13) | copy-start | bytes 7684
  0.0 37.5 %copy-start.13 = (f32[2,320]{1,0:T(2,128)S(1)}, f32[2,320]{1,0:T(2,128)}, u32[]{:S(2)}) copy-start(f32[2,320]{1,0:T(2,128)} %param.14) | copy-start | bytes 7684
  0.0 10.0 %collective-permute-start.13 = (bf16[2,320,128]{2,1,0:T(8,128)(2,1)}, bf16[2,320,128]{2,1,0:T(8,128)(2,1)S(1)}, u32[]{:S(2)}, u32[]{:S(2)}) collective-permute-start(bf16[2,320,128]{2,1,0:T(8,128)(2,1)} %param.9), channel_id=1, source_target_pairs={{0,4},{1,5},{2,6},{3,7},{4,0},{5,1},{6,2},{7,3},{8,12},{9,13},{10,... | collective-permute-start | bytes 491528 | tf_op jit(solution)/shard_map/ppermute | solution.py:32
  3.1 15.3 %collective-permute-start.14 = (bf16[2,320,128]{2,1,0:T(8,128)(2,1)}, bf16[2,320,128]{2,1,0:T(8,128)(2,1)S(1)}, u32[]{:S(2)}, u32[]{:S(2)}) collective-permute-start(bf16[2,320,128]{2,1,0:T(8,128)(2,1)} %param.9), channel_id=1, source_target_pairs={{0,8},{1,9},{2,10},{3,11},{4,12},{5,13},{6,14},{7,15},{8,0},{9,1},... | collective-permute-start | bytes 491528 | tf_op jit(solution)/shard_map/ppermute | solution.py:32
  5.7 12.7 %collective-permute-start.15 = (bf16[2,320,128]{2,1,0:T(8,128)(2,1)}, bf16[2,320,128]{2,1,0:T(8,128)(2,1)S(1)}, u32[]{:S(2)}, u32[]{:S(2)}) collective-permute-start(bf16[2,320,128]{2,1,0:T(8,128)(2,1)} %param.9), channel_id=1, source_target_pairs={{0,12},{1,13},{2,14},{3,15},{4,8},{5,9},{6,10},{7,11},{8,4},{9,5},... | collective-permute-start | bytes 491528 | tf_op jit(solution)/shard_map/ppermute | solution.py:32
  18.4 20.9 %copy-start.4 = (bf16[2,1280,128]{2,1,0:T(8,128)(2,1)}, bf16[2,1280,128]{2,1,0:T(8,128)(2,1)S(1)}, u32[]{:S(2)}) copy-start(bf16[2,1280,128]{2,1,0:T(8,128)(2,1)S(1)} %constant_dynamic-update-slice_fusion.4.refs_0_) | copy-start | bytes 1966084
  18.4 14.0 %collective-permute-start.16 = (bf16[2,1280,128]{2,1,0:T(8,128)(2,1)S(1)}, bf16[2,1280,128]{2,1,0:T(8,128)(2,1)S(1)}, u32[]{:S(2)}, u32[]{:S(2)}) collective-permute-start(bf16[2,1280,128]{2,1,0:T(8,128)(2,1)S(1)} %constant_dynamic-update-slice_fusion.4.refs_0_), channel_id=1, source_target_pairs={{0,2},{1,3},{2,0},{3,1},{4,6},{5,7},{6,4},{7,5},{8,10},{9,11},{10,... | collective-permute-start | bytes 1966088 | tf_op jit(solution)/shard_map/ppermute | solution.py:32
  20.0 8.0 %collective-permute-start = (bf16[2,320,128]{2,1,0:T(8,128)(2,1)}, bf16[2,320,128]{2,1,0:T(8,128)(2,1)S(1)}, u32[]{:S(2)}, u32[]{:S(2)}) collective-permute-start(bf16[2,320,128]{2,1,0:T(8,128)(2,1)} %param.10), channel_id=1, source_target_pairs={{0,4},{1,5},{2,6},{3,7},{4,0},{5,1},{6,2},{7,3},{8,12},{9,13},{10,... | collective-permute-start | bytes 491528 | tf_op jit(solution)/shard_map/ppermute | solution.py:32
  22.7 14.2 %collective-permute-start.1 = (bf16[2,320,128]{2,1,0:T(8,128)(2,1)}, bf16[2,320,128]{2,1,0:T(8,128)(2,1)S(1)}, u32[]{:S(2)}, u32[]{:S(2)}) collective-permute-start(bf16[2,320,128]{2,1,0:T(8,128)(2,1)} %param.10), channel_id=1, source_target_pairs={{0,8},{1,9},{2,10},{3,11},{4,12},{5,13},{6,14},{7,15},{8,0},{9,1},... | collective-permute-start | bytes 491528 | tf_op jit(solution)/shard_map/ppermute | solution.py:32
  23.6 13.2 %collective-permute-start.2 = (bf16[2,320,128]{2,1,0:T(8,128)(2,1)}, bf16[2,320,128]{2,1,0:T(8,128)(2,1)S(1)}, u32[]{:S(2)}, u32[]{:S(2)}) collective-permute-start(bf16[2,320,128]{2,1,0:T(8,128)(2,1)} %param.10), channel_id=1, source_target_pairs={{0,12},{1,13},{2,14},{3,15},{4,8},{5,9},{6,10},{7,11},{8,4},{9,5},... | collective-permute-start | bytes 491528 | tf_op jit(solution)/shard_map/ppermute | solution.py:32
  25.1 12.5 %collective-permute-start.17 = (bf16[2,1280,128]{2,1,0:T(8,128)(2,1)S(1)}, bf16[2,1280,128]{2,1,0:T(8,128)(2,1)S(1)}, u32[]{:S(2)}, u32[]{:S(2)}) collective-permute-start(bf16[2,1280,128]{2,1,0:T(8,128)(2,1)S(1)} %constant_dynamic-update-slice_fusion.4.refs_0_), channel_id=1, source_target_pairs={{0,1},{1,0},{2,3},{3,2},{4,5},{5,4},{6,7},{7,6},{8,9},{9,8},{10,11... | collective-permute-start | bytes 1966088 | tf_op jit(solution)/shard_map/ppermute | solution.py:32
  32.5 6.9 %copy-start.6 = (bf16[2,1280,128]{2,1,0:T(8,128)(2,1)}, bf16[2,1280,128]{2,1,0:T(8,128)(2,1)S(1)}, u32[]{:S(2)}) copy-start(bf16[2,1280,128]{2,1,0:T(8,128)(2,1)S(1)} %collective-permute-done.16.refs_1_) | copy-start | bytes 1966084
  32.5 6.0 %collective-permute-start.18 = (bf16[2,1280,128]{2,1,0:T(8,128)(2,1)S(1)}, bf16[2,1280,128]{2,1,0:T(8,128)(2,1)S(1)}, u32[]{:S(2)}, u32[]{:S(2)}) collective-permute-start(bf16[2,1280,128]{2,1,0:T(8,128)(2,1)S(1)} %collective-permute-done.16.refs_1_), channel_id=1, source_target_pairs={{0,1},{1,0},{2,3},{3,2},{4,5},{5,4},{6,7},{7,6},{8,9},{9,8},{10,11... | collective-permute-start | bytes 1966088 | tf_op jit(solution)/shard_map/ppermute | solution.py:32
  36.9 16.1 %collective-permute-start.3 = (bf16[2,1280,128]{2,1,0:T(8,128)(2,1)S(1)}, bf16[2,1280,128]{2,1,0:T(8,128)(2,1)}, u32[]{:S(2)}, u32[]{:S(2)}) collective-permute-start(bf16[2,1280,128]{2,1,0:T(8,128)(2,1)S(1)} %constant_dynamic-update-slice_fusion.refs_0_), channel_id=1, source_target_pairs={{0,2},{1,3},{2,0},{3,1},{4,6},{5,7},{6,4},{7,5},{8,10},{9,11},{10,... | collective-permute-start | bytes 1966088 | tf_op jit(solution)/shard_map/ppermute | solution.py:32
  37.6 0.8 copy-start.8
  38.5 0.8 copy-start.10
  39.3 1.1 copy-start.5
  40.4 1.1 copy-start.7
  41.5 1.1 copy-start.9
  42.6 1.1 copy-start.11
  52.4 16.8 %collective-permute-start.19 = (bf16[2,2560,128]{2,1,0:T(8,128)(2,1)}, bf16[2,2560,128]{2,1,0:T(8,128)(2,1)}, u32[]{:S(2)}, u32[]{:S(2)}) collective-permute-start(bf16[2,2560,128]{2,1,0:T(8,128)(2,1)} %get-tuple-element.13), channel_id=1, source_target_pairs={{0,1},{1,0},{2,3},{3,2},{4,5},{5,4},{6,7},{7,6},{8,9},{9,8},{10,11... | collective-permute-start | bytes 3932168 | tf_op jit(solution)/shard_map/ppermute | solution.py:32
  52.5 4.5 %collective-permute-start.4 = (bf16[2,1280,128]{2,1,0:T(8,128)(2,1)S(1)}, bf16[2,1280,128]{2,1,0:T(8,128)(2,1)S(1)}, u32[]{:S(2)}, u32[]{:S(2)}) collective-permute-start(bf16[2,1280,128]{2,1,0:T(8,128)(2,1)S(1)} %constant_dynamic-update-slice_fusion.refs_0_), channel_id=1, source_target_pairs={{0,1},{1,0},{2,3},{3,2},{4,5},{5,4},{6,7},{7,6},{8,9},{9,8},{10,11... | collective-permute-start | bytes 1966088 | tf_op jit(solution)/shard_map/ppermute | solution.py:32
  53.0 4.6 %collective-permute-start.5 = (bf16[2,1280,128]{2,1,0:T(8,128)(2,1)}, bf16[2,1280,128]{2,1,0:T(8,128)(2,1)S(1)}, u32[]{:S(2)}, u32[]{:S(2)}) collective-permute-start(bf16[2,1280,128]{2,1,0:T(8,128)(2,1)} %collective-permute-done.3.refs_1_), channel_id=1, source_target_pairs={{0,1},{1,0},{2,3},{3,2},{4,5},{5,4},{6,7},{7,6},{8,9},{9,8},{10,11... | collective-permute-start | bytes 1966088 | tf_op jit(solution)/shard_map/ppermute | solution.py:32
  67.6 1.5 copy-start.2
  69.1 3.5 %collective-permute-start.6 = (bf16[2,2560,128]{2,1,0:T(8,128)(2,1)}, bf16[2,2560,128]{2,1,0:T(8,128)(2,1)}, u32[]{:S(2)}, u32[]{:S(2)}) collective-permute-start(bf16[2,2560,128]{2,1,0:T(8,128)(2,1)} %get-tuple-element.11), channel_id=1, source_target_pairs={{0,1},{1,0},{2,3},{3,2},{4,5},{5,4},{6,7},{7,6},{8,9},{9,8},{10,11... | collective-permute-start | bytes 3932168 | tf_op jit(solution)/shard_map/ppermute | solution.py:32
  69.2 3.4 %copy-start.3 = (f32[2,2560,128]{2,1,0:T(8,128)S(1)}, f32[2,2560,128]{2,1,0:T(8,128)}, u32[]{:S(2)}) copy-start(f32[2,2560,128]{2,1,0:T(8,128)} %copy-done.2) | copy-start | bytes 7864324
  71.0 17.6 %collective-permute-start.20 = (bf16[2,1280,128]{2,1,0:T(8,128)(2,1)S(1)}, bf16[2,1280,128]{2,1,0:T(8,128)(2,1)S(1)}, u32[]{:S(2)}, u32[]{:S(2)}) collective-permute-start(bf16[2,1280,128]{2,1,0:T(8,128)(2,1)S(1)} %slice.70), channel_id=1, source_target_pairs={{0,2},{1,3},{2,0},{3,1},{4,6},{5,7},{6,4},{7,5},{8,10},{9,11},{10,... | collective-permute-start | bytes 1966088 | tf_op jit(solution)/shard_map/ppermute | solution.py:32
  74.3 27.8 %collective-permute-start.7 = (bf16[2,1280,128]{2,1,0:T(8,128)(2,1)S(1)}, bf16[2,1280,128]{2,1,0:T(8,128)(2,1)S(1)}, u32[]{:S(2)}, u32[]{:S(2)}) collective-permute-start(bf16[2,1280,128]{2,1,0:T(8,128)(2,1)S(1)} %slice.71), channel_id=1, source_target_pairs={{0,2},{1,3},{2,0},{3,1},{4,6},{5,7},{6,4},{7,5},{8,10},{9,11},{10,... | collective-permute-start | bytes 1966088 | tf_op jit(solution)/shard_map/ppermute | solution.py:32
  88.8 9.2 %collective-permute-start.21 = (bf16[2,640,128]{2,1,0:T(8,128)(2,1)S(1)}, bf16[2,640,128]{2,1,0:T(8,128)(2,1)S(1)}, u32[]{:S(2)}, u32[]{:S(2)}) collective-permute-start(bf16[2,640,128]{2,1,0:T(8,128)(2,1)S(1)} %select_convert_fusion), channel_id=1, source_target_pairs={{0,4},{1,5},{2,6},{3,7},{4,0},{5,1},{6,2},{7,3},{8,12},{9,13},{10,... | collective-permute-start | bytes 983048 | tf_op jit(solution)/shard_map/ppermute | solution.py:32
  98.1 10.4 %collective-permute-start.22 = (bf16[2,640,128]{2,1,0:T(8,128)(2,1)S(1)}, bf16[2,640,128]{2,1,0:T(8,128)(2,1)S(1)}, u32[]{:S(2)}, u32[]{:S(2)}) collective-permute-start(bf16[2,640,128]{2,1,0:T(8,128)(2,1)S(1)} %fusion.1), channel_id=1, source_target_pairs={{0,12},{1,13},{2,14},{3,15},{4,8},{5,9},{6,10},{7,11},{8,4},{9,5},... | collective-permute-start | bytes 983048 | tf_op jit(solution)/shard_map/ppermute | solution.py:32
  102.3 12.8 %collective-permute-start.8 = (bf16[2,640,128]{2,1,0:T(8,128)(2,1)S(1)}, bf16[2,640,128]{2,1,0:T(8,128)(2,1)S(1)}, u32[]{:S(2)}, u32[]{:S(2)}) collective-permute-start(bf16[2,640,128]{2,1,0:T(8,128)(2,1)S(1)} %select_convert_fusion.1), channel_id=1, source_target_pairs={{0,4},{1,5},{2,6},{3,7},{4,0},{5,1},{6,2},{7,3},{8,12},{9,13},{10,... | collective-permute-start | bytes 983048 | tf_op jit(solution)/shard_map/ppermute | solution.py:32
  108.8 14.3 %collective-permute-start.23 = (bf16[2,640,128]{2,1,0:T(8,128)(2,1)S(1)}, bf16[2,640,128]{2,1,0:T(8,128)(2,1)S(1)}, u32[]{:S(2)}, u32[]{:S(2)}) collective-permute-start(bf16[2,640,128]{2,1,0:T(8,128)(2,1)S(1)} %add_convert_fusion), channel_id=1, source_target_pairs={{0,4},{1,5},{2,6},{3,7},{4,0},{5,1},{6,2},{7,3},{8,12},{9,13},{10,... | collective-permute-start | bytes 983048 | tf_op jit(solution)/shard_map/ppermute | solution.py:32
  115.3 15.8 %collective-permute-start.9 = (bf16[2,640,128]{2,1,0:T(8,128)(2,1)S(1)}, bf16[2,640,128]{2,1,0:T(8,128)(2,1)S(1)}, u32[]{:S(2)}, u32[]{:S(2)}) collective-permute-start(bf16[2,640,128]{2,1,0:T(8,128)(2,1)S(1)} %fusion), channel_id=1, source_target_pairs={{0,12},{1,13},{2,14},{3,15},{4,8},{5,9},{6,10},{7,11},{8,4},{9,5},... | collective-permute-start | bytes 983048 | tf_op jit(solution)/shard_map/ppermute | solution.py:32
  123.2 16.0 %collective-permute-start.24 = (bf16[2,1280,128]{2,1,0:T(8,128)(2,1)S(1)}, bf16[2,1280,128]{2,1,0:T(8,128)(2,1)S(1)}, u32[]{:S(2)}, u32[]{:S(2)}) collective-permute-start(bf16[2,1280,128]{2,1,0:T(8,128)(2,1)S(1)} %pad_maximum_fusion.1.pa), channel_id=1, source_target_pairs={{0,2},{1,3},{2,0},{3,1},{4,6},{5,7},{6,4},{7,5},{8,10},{9,11},{10,... | collective-permute-start | bytes 1966088 | tf_op jit(solution)/shard_map/ppermute | solution.py:32
  131.1 10.2 %copy-start = (bf16[6,2,32,5120]{3,2,1,0:T(8,128)(2,1)S(1)}, bf16[6,2,32,5120]{3,2,1,0:T(8,128)(2,1)}, u32[]{:S(2)}) copy-start(bf16[6,2,32,5120]{3,2,1,0:T(8,128)(2,1)} %train.2) | copy-start | bytes 11796484
  131.3 7.8 %collective-permute-start.10 = (bf16[2,640,128]{2,1,0:T(8,128)(2,1)S(1)}, bf16[2,640,128]{2,1,0:T(8,128)(2,1)S(1)}, u32[]{:S(2)}, u32[]{:S(2)}) collective-permute-start(bf16[2,640,128]{2,1,0:T(8,128)(2,1)S(1)} %add_convert_fusion.1), channel_id=1, source_target_pairs={{0,4},{1,5},{2,6},{3,7},{4,0},{5,1},{6,2},{7,3},{8,12},{9,13},{10,... | collective-permute-start | bytes 983048 | tf_op jit(solution)/shard_map/ppermute | solution.py:32
  131.3 9.7 %collective-permute-start.25 = (bf16[2,1280,128]{2,1,0:T(8,128)(2,1)S(1)}, bf16[2,1280,128]{2,1,0:T(8,128)(2,1)S(1)}, u32[]{:S(2)}, u32[]{:S(2)}) collective-permute-start(bf16[2,1280,128]{2,1,0:T(8,128)(2,1)S(1)} %pad_maximum_fusion.1.pa), channel_id=1, source_target_pairs={{0,1},{1,0},{2,3},{3,2},{4,5},{5,4},{6,7},{7,6},{8,9},{9,8},{10,11... | collective-permute-start | bytes 1966088 | tf_op jit(solution)/shard_map/ppermute | solution.py:32
  139.1 2.2 %collective-permute-start.26 = (bf16[2,1280,128]{2,1,0:T(8,128)(2,1)S(1)}, bf16[2,1280,128]{2,1,0:T(8,128)(2,1)S(1)}, u32[]{:S(2)}, u32[]{:S(2)}) collective-permute-start(bf16[2,1280,128]{2,1,0:T(8,128)(2,1)S(1)} %collective-permute-done.24.pb), channel_id=1, source_target_pairs={{0,1},{1,0},{2,3},{3,2},{4,5},{5,4},{6,7},{7,6},{8,9},{9,8},{10,11... | collective-permute-start | bytes 1966088 | tf_op jit(solution)/shard_map/ppermute | solution.py:32
  139.3 17.2 %collective-permute-start.11 = (bf16[2,1280,128]{2,1,0:T(8,128)(2,1)S(1)}, bf16[2,1280,128]{2,1,0:T(8,128)(2,1)S(1)}, u32[]{:S(2)}, u32[]{:S(2)}) collective-permute-start(bf16[2,1280,128]{2,1,0:T(8,128)(2,1)S(1)} %pad_maximum_fusion.pa), channel_id=1, source_target_pairs={{0,2},{1,3},{2,0},{3,1},{4,6},{5,7},{6,4},{7,5},{8,10},{9,11},{10,... | collective-permute-start | bytes 1966088 | tf_op jit(solution)/shard_map/ppermute | solution.py:32
  140.8 15.6 %collective-permute-start.12 = (bf16[2,1280,128]{2,1,0:T(8,128)(2,1)S(1)}, bf16[2,1280,128]{2,1,0:T(8,128)(2,1)S(1)}, u32[]{:S(2)}, u32[]{:S(2)}) collective-permute-start(bf16[2,1280,128]{2,1,0:T(8,128)(2,1)S(1)} %pad_maximum_fusion.pa), channel_id=1, source_target_pairs={{0,1},{1,0},{2,3},{3,2},{4,5},{5,4},{6,7},{7,6},{8,9},{9,8},{10,11... | collective-permute-start | bytes 1966088 | tf_op jit(solution)/shard_map/ppermute | solution.py:32
  141.3 17.3 %copy-start.1 = (bf16[6,2,32,5120]{3,2,1,0:T(8,128)(2,1)S(1)}, bf16[6,2,32,5120]{3,2,1,0:T(8,128)(2,1)}, u32[]{:S(2)}) copy-start(bf16[6,2,32,5120]{3,2,1,0:T(8,128)(2,1)} %train.3) | copy-start | bytes 11796484
  143.2 17.4 %copy-start.15 = (s32[128]{0:T(128)S(1)}, s32[128]{0:T(128)}, u32[]{:S(2)}) copy-start(s32[128]{0:T(128)} %param.17) | copy-start | bytes 1540
  156.5 2.1 %collective-permute-start.27 = (bf16[2,1280,128]{2,1,0:T(8,128)(2,1)S(1)}, bf16[2,1280,128]{2,1,0:T(8,128)(2,1)S(1)}, u32[]{:S(2)}, u32[]{:S(2)}) collective-permute-start(bf16[2,1280,128]{2,1,0:T(8,128)(2,1)S(1)} %collective-permute-done.11.pb), channel_id=1, source_target_pairs={{0,1},{1,0},{2,3},{3,2},{4,5},{5,4},{6,7},{7,6},{8,9},{9,8},{10,11... | collective-permute-start | bytes 1966088 | tf_op jit(solution)/shard_map/ppermute | solution.py:32

commit v4 on v3

--- a/solution.py
+++ b/solution.py
@@ -41,9 +41,9 @@
     return block, ks
 
 
-def sum_far(total, me, n):
+def sum_far(total, me, n, stages):
     result = total.astype(BF16)
-    for bit, bits in far_stages(n, 2):
+    for bit, bits in stages:
         if bits == 1:
             total = total + swap(result, n, bit).astype(F32)
             result = total.astype(BF16)
@@ -74,14 +74,42 @@
     return block, across, swap(block, n, 1), swap(across, n, 1)
 
 
+def sum_near(half, me, n):
+    quarter = half.shape[1] // 2
+    near, away = half[:, :quarter], half[:, quarter:].astype(BF16)
+    stages = far_stages(n, 2)
+    if not stages or stages[0][1] == 1:
+        total = near + swap(away, n, 2).astype(F32)
+        block = sum_far(total, me, n, stages)
+        return block, swap(block, n, 2)
+    bit = stages[0][0]
+    place = (me // bit) % 4
+    first = (place == 0) | (place == 3)
+    low, high = slice(0, quarter // 2), slice(quarter // 2, quarter)
+    pick = lambda x, y: jnp.where(first, x, y)
+    theirs = pick(near[:, high], near[:, low]) + swap(pick(away[:, high], away[:, low]), n, 2).astype(F32)
+    mine = pick(near[:, low], near[:, high]) + swap(pick(away[:, low], away[:, high]), n, 2).astype(F32)
+    mine = mine + swap(theirs.astype(BF16), n, bit).astype(F32)
+    mine = mine + swap(mine.astype(BF16), n, 3 * bit).astype(F32)
+    mine = sum_far(mine, me, n, stages[1:])
+    theirs = swap(mine, n, bit)
+    join = lambda x, y: jnp.concatenate([pick(x, y), pick(y, x)], axis=1)
+    return join(mine, theirs), join(swap(mine, n, 2), swap(theirs, n, 2))
+
+
 def term_kernel(n, column, first, offsets, me_ref, *refs):
-    *arrays, basis, eig, send, keep, full, held, pair, sems = refs
+    count = len(offsets)
+    arrays, rest = refs[:count], refs[count:]
+    basis, eig, send, keep, full, held, pair, sems, *stages, in_sems = rest
     me = me_ref[0]
     layers, _, width = held.shape
     rows = width // n
     piece = width // PIECES
     copies = {}
     for l in range(layers):
+        for i, (array, stage) in enumerate(zip(arrays, stages)):
+            copies[l, -1 - i] = pltpu.make_async_copy(array.at[l], stage.at[l], in_sems.at[l, i])
+            copies[l, -1 - i].start()
         for p in range(PIECES):
             part = (slice(None), pl.ds(p * piece, piece))
             copies[l, p] = pltpu.make_async_copy(
@@ -91,10 +119,11 @@
     mine = me & 1
     above = (me >> 1) & 1
     for l in range(layers):
-        for array, ks in zip(arrays, offsets):
+        for j, (stage, ks) in enumerate(zip(stages, offsets)):
+            copies[l, -1 - j].wait()
             for i, k in enumerate(ks):
                 at = pl.multiple_of((me ^ k) * rows, rows)
-                full[pl.ds(at, rows), :] = array[l, i * rows : (i + 1) * rows, :]
+                full[pl.ds(at, rows), :] = stage[l, i * rows : (i + 1) * rows, :]
         coeff = [0.0, 0.0]
         split = held.shape[1] // 2
         for p in range(PIECES):
@@ -114,7 +143,7 @@
             at = pl.multiple_of(((above ^ (p & 1)) * (n // 4) + p // 2) * rows, rows)
             kept = pl.multiple_of(mine * rows, rows)
             sent = pl.multiple_of((1 - mine) * rows, rows)
-            keep[l, pl.ds(at, rows), :] = pair[pl.ds(kept, rows), :]
+            keep[l, pl.ds(at, rows), :] = pair[pl.ds(kept, rows), :].astype(BF16)
             send[l, pl.ds(at, rows), :] = pair[pl.ds(sent, rows), :].astype(BF16)
 
 
@@ -126,16 +155,18 @@
     return pl.pallas_call(
         functools.partial(term_kernel, n, column, first, offsets),
         in_specs=[pl.BlockSpec(memory_space=pltpu.SMEM)]
-        + [vmem] * len(arrays)
-        + [pl.BlockSpec(memory_space=pltpu.HBM), vmem],
+        + [pl.BlockSpec(memory_space=pl.ANY)] * (len(arrays) + 1)
+        + [vmem],
         out_specs=[vmem, vmem],
         scratch_shapes=[
             pltpu.VMEM((width, q), BF16),
             pltpu.VMEM((layers, cols, width), BF16),
             pltpu.VMEM((2 * width // n, q), F32),
             pltpu.SemaphoreType.DMA((layers, PIECES)),
+            *[pltpu.VMEM(a.shape, BF16) for a in arrays],
+            pltpu.SemaphoreType.DMA((layers, len(arrays))),
         ],
-        out_shape=[jax.ShapeDtypeStruct(half, BF16), jax.ShapeDtypeStruct(half, F32)],
+        out_shape=[jax.ShapeDtypeStruct(half, BF16)] * 2,
         compiler_params=pltpu.CompilerParams(vmem_limit_bytes=TERMS_VMEM),
         cost_estimate=pl.CostEstimate(
             flops=layers * 4 * width * cols * q,
@@ -143,7 +174,7 @@
             transcendentals=0,
         ),
         name="terms",
-    )(me, *arrays, pltpu.with_memory_space_constraint(basis, pltpu.HBM), eig)
+    )(me, *[pltpu.with_memory_space_constraint(a, pltpu.HBM) for a in arrays], pltpu.with_memory_space_constraint(basis, pltpu.HBM), eig)
 
 
 def proj_kernel(n, first, me_ref, pa, pb, pc, pd, train, *rest):
@@ -214,22 +245,23 @@
     )
     chunks = [(first, side) for first in range(0, layers, TOGETHER) for side in range(2)]
     blocks = [spread(sides[side][0][first : first + TOGETHER], n) for first, side in chunks]
-    gathered = [gather_near(block, n) for block, _ in blocks]
-    aways, halves, quarters = [], [], []
+    gathered = []
+    for i, (block, _) in enumerate(blocks):
+        across = swap(block, n, 2)
+        ready = after(across, [other for other, _ in blocks[i + 1 : i + 2]])
+        gathered.append((block, across, swap(block, n, 1), swap(ready, n, 1)))
+    halves = []
     for i, (first, side) in enumerate(chunks):
         ks = blocks[i][1]
         offsets = [[k ^ m for k in ks] for m in (0, 2, 1, 3)]
         earlier = []
         arrays = after(gathered[i], earlier)
         send, keep = terms(me, arrays, offsets, sides[side][1], eig, first, side * layers + first, n)
-        half = keep + swap(send, n, 1).astype(F32)
-        quarter = half.shape[1] // 2
-        aways.append(half[:, quarter:].astype(BF16))
-        halves.append(half[:, :quarter] + swap(aways[i], n, 2).astype(F32))
+        half = keep.astype(F32) + swap(send, n, 1).astype(F32)
+        halves.append(sum_near(half, me[0], n))
     total, left = 0.0, ()
     for i, (first, side) in enumerate(chunks):
-        block = sum_far(halves[i], me[0], n)
-        across = swap(block, n, 2)
+        block, across = halves[i]
         corner = swap(after(across, left), n, 1)
         left = (project(me, (block, across, swap(block, n, 1), corner), sides[side][2], first, n, left),)
         if side:

time: 162 us -> 155 us (0.957)
  starting transfers between devices: 36.5 us -> 48.7 us
  waiting for transfers between devices: 87.8 us -> 75.7 us
  local copies, waits for them, and re-layouts: 9.06 us -> 3.1 us
    ppermute x28 -> x32, starting transfers between devices: 36.5 us -> 48.7 us  [swap(): return lax.ppermute(x, AXIS, [(t, t ^ mask) for t in range(n)])]
    ppermute x28 -> x32, waiting for transfers between devices: 87.8 us -> 75.7 us  [swap(): return lax.ppermute(x, AXIS, [(t, t ^ mask) for t in range(n)])]
    unnamed x38 -> x32, local copies, waits for them, and re-layouts: 8.62 us -> 2.84 us
    add x4 -> x2, other arithmetic: 3.53 us -> 3.31 us  [on_device(): half = keep.astype(F32) + swap(send, n, 1).astype(F32)]
  transfers between devices with their start and end apart: 28 -> 32, of which waited for: 18 -> 17; matrix products, arithmetic and copies ran while one was open for 4% -> 4% of each run, Pallas kernels for 13% -> 13%
where the time goes in v4:
time: 155 us
  waiting for transfers between devices  75.7 us (49%)
  starting transfers between devices  48.7 us (31%)
  Pallas kernels  21.7 us (14%)
  other arithmetic  4.58 us (3%)
  local copies, waits for them, and re-layouts  3.1 us (2%)
    ppermute x32, waiting for transfers between devices, swap(): return lax.ppermute(x, AXIS, [(t, t ^ mask) for t in range(n)])  75.7 us
    ppermute x32, starting transfers between devices, swap(): return lax.ppermute(x, AXIS, [(t, t ^ mask) for t in range(n)])  48.7 us
    pallas_call x2, Pallas kernels, terms(): pl.pallas_call(functools.partial(term_kernel, n, column, first, offsets),...  17.8 us
    pallas_call x2, Pallas kernels, project(): pl.pallas_call(functools.partial(proj_kernel, n, first), in_specs=[pl.Blo...  3.89 us
    add x2, other arithmetic, on_device(): half = keep.astype(F32) + swap(send, n, 1).astype(F32)  3.31 us
  transfers between devices with their start and end apart: 32, of which 17 were waited for; matrix products, arithmetic and copies ran while one was open for 4% of the time, Pallas kernels for 13%

profile of v4, /device:TPU:0, one launch (start us, length us, event | category | flops | bytes accessed | tf_op | source)
XLA Modules:
  0.0 154.9 jit_solution(6353966439373596774)
XLA Ops:
  0.0 3.1 %collective-permute-start.15 = (bf16[2,320,128]{2,1,0:T(8,128)(2,1)}, bf16[2,320,128]{2,1,0:T(8,128)(2,1)S(1)}, u32[]{:S(2)}, u32[]{:S(2)}) collective-permute-start(bf16[2,320,128]{2,1,0:T(8,128)(2,1)} %param.9), channel_id=1, source_target_pairs={{0,4},{1,5},{2,6},{3,7},{4,0},{5,1},{6,2},{7,3},{8,12},{9,13},{10,... | collective-permute-start | bytes 491528 | tf_op jit(solution)/shard_map/ppermute | solution.py:32
  3.1 2.6 %collective-permute-start.16 = (bf16[2,320,128]{2,1,0:T(8,128)(2,1)}, bf16[2,320,128]{2,1,0:T(8,128)(2,1)S(1)}, u32[]{:S(2)}, u32[]{:S(2)}) collective-permute-start(bf16[2,320,128]{2,1,0:T(8,128)(2,1)} %param.9), channel_id=1, source_target_pairs={{0,8},{1,9},{2,10},{3,11},{4,12},{5,13},{6,14},{7,15},{8,0},{9,1},... | collective-permute-start | bytes 491528 | tf_op jit(solution)/shard_map/ppermute | solution.py:32
  5.7 1.0 constant_dynamic-update-slice_fusion.7
  6.7 3.3 %collective-permute-done.15 = bf16[2,320,128]{2,1,0:T(8,128)(2,1)S(1)} collective-permute-done((bf16[2,320,128]{2,1,0:T(8,128)(2,1)}, bf16[2,320,128]{2,1,0:T(8,128)(2,1)S(1)}, u32[]{:S(2)}, u32[]{:S(2)}) %collective-permute-start.15) | collective-permute-done | bytes 163872 | tf_op jit(solution)/shard_map/ppermute | solution.py:32
  10.0 8.4 %collective-permute-done.16 = bf16[2,320,128]{2,1,0:T(8,128)(2,1)S(1)} collective-permute-done((bf16[2,320,128]{2,1,0:T(8,128)(2,1)}, bf16[2,320,128]{2,1,0:T(8,128)(2,1)S(1)}, u32[]{:S(2)}, u32[]{:S(2)}) %collective-permute-start.16) | collective-permute-done | bytes 163872 | tf_op jit(solution)/shard_map/ppermute | solution.py:32
  18.4 1.6 %collective-permute-start.18 = (bf16[2,1280,128]{2,1,0:T(8,128)(2,1)S(1)}, bf16[2,1280,128]{2,1,0:T(8,128)(2,1)S(1)}, u32[]{:S(2)}, u32[]{:S(2)}) collective-permute-start(bf16[2,1280,128]{2,1,0:T(8,128)(2,1)S(1)} %constant_dynamic-update-slice_fusion.4.refs_0_), channel_id=1, source_target_pairs={{0,2},{1,3},{2,0},{3,1},{4,6},{5,7},{6,4},{7,5},{8,10},{9,11},{10,... | collective-permute-start | bytes 1966088 | tf_op jit(solution)/shard_map/ppermute | solution.py:32
  20.0 2.6 %collective-permute-start = (bf16[2,320,128]{2,1,0:T(8,128)(2,1)}, bf16[2,320,128]{2,1,0:T(8,128)(2,1)S(1)}, u32[]{:S(2)}, u32[]{:S(2)}) collective-permute-start(bf16[2,320,128]{2,1,0:T(8,128)(2,1)} %param.10), channel_id=1, source_target_pairs={{0,4},{1,5},{2,6},{3,7},{4,0},{5,1},{6,2},{7,3},{8,12},{9,13},{10,... | collective-permute-start | bytes 491528 | tf_op jit(solution)/shard_map/ppermute | solution.py:32
  22.7 1.0 collective-permute-start.1
  23.6 1.5 collective-permute-start.2
  25.2 2.9 %collective-permute-done = bf16[2,320,128]{2,1,0:T(8,128)(2,1)S(1)} collective-permute-done((bf16[2,320,128]{2,1,0:T(8,128)(2,1)}, bf16[2,320,128]{2,1,0:T(8,128)(2,1)S(1)}, u32[]{:S(2)}, u32[]{:S(2)}) %collective-permute-start) | collective-permute-done | bytes 163872 | tf_op jit(solution)/shard_map/ppermute | solution.py:32
  28.1 8.7 %collective-permute-done.1 = bf16[2,320,128]{2,1,0:T(8,128)(2,1)S(1)} collective-permute-done((bf16[2,320,128]{2,1,0:T(8,128)(2,1)}, bf16[2,320,128]{2,1,0:T(8,128)(2,1)S(1)}, u32[]{:S(2)}, u32[]{:S(2)}) %collective-permute-start.1) | collective-permute-done | bytes 163872 | tf_op jit(solution)/shard_map/ppermute | solution.py:32
  36.9 0.1 collective-permute-start.20
  37.0 0.6 collective-permute-start.3
  37.6 0.1 copy.12
  37.8 1.3 collective-permute-done.20.refs_3_
  39.1 0.8 copy-done.6
  39.9 8.9 %terms.3 = (bf16[2,2560,128]{2,1,0:T(8,128)(2,1)}, bf16[2,2560,128]{2,1,0:T(8,128)(2,1)S(1)}) custom-call(s32[1]{0:T(128)} %bitcast.me_ref, bf16[2,1280,128]{2,1,0:T(8,128)(2,1)} %copy-done.3, bf16[2,1280,128]{2,1,0:T(8,128)(2,1)} %copy-done.4, bf16[2,1280,128]{2,1,0:T(8,128)(2,1)} %copy-done.5, bf16[2,1280,128]{2,1,0:T(8,128)(2,1)} %copy-done.6, ...), custom_call_target="tpu_custom_call" | custom-call | flops 1677721600 | bytes 11796480 | tf_op jit(solution)/shard_map/terms/pallas_call | solution.py:155
  48.9 0.2 collective-permute-start.21
  49.1 0.3 collective-permute-start.4
  49.5 4.8 %collective-permute-done.3.refs_1_ = bf16[2,1280,128]{2,1,0:T(8,128)(2,1)} collective-permute-done((bf16[2,1280,128]{2,1,0:T(8,128)(2,1)S(1)}, bf16[2,1280,128]{2,1,0:T(8,128)(2,1)}, u32[]{:S(2)}, u32[]{:S(2)}) %collective-permute-start.3) | collective-permute-done | bytes 655392 | tf_op jit(solution)/shard_map/ppermute | solution.py:32
  54.3 2.3 %collective-permute-done.5.refs_3_ = bf16[2,1280,128]{2,1,0:T(8,128)(2,1)S(1)} collective-permute-done((bf16[2,1280,128]{2,1,0:T(8,128)(2,1)}, bf16[2,1280,128]{2,1,0:T(8,128)(2,1)S(1)}, u32[]{:S(2)}, u32[]{:S(2)}) %collective-permute-start.5) | collective-permute-done | bytes 655392 | tf_op jit(solution)/shard_map/ppermute | solution.py:32
  56.6 0.8 copy-done.8
  57.4 8.9 %terms.2 = (bf16[2,2560,128]{2,1,0:T(8,128)(2,1)}, bf16[2,2560,128]{2,1,0:T(8,128)(2,1)S(1)}) custom-call(s32[1]{0:T(128)} %bitcast.me_ref, bf16[2,1280,128]{2,1,0:T(8,128)(2,1)} %copy-done.2, bf16[2,1280,128]{2,1,0:T(8,128)(2,1)} %collective-permute-done.3.refs_1_, bf16[2,1280,128]{2,1,0:T(8,128)(2,1)} %copy-done.7, bf16[2,1280,128]{2,1,0:T(8,128)(2,1)} %copy-done.8, ...), custom_call_target="tpu_custom_call" | custom-call | flops 1677721600 | bytes 11796480 | tf_op jit(solution)/shard_map/terms/pallas_call | solution.py:155
  66.3 0.2 collective-permute-start.6
  66.5 1.7 %convert_add_fusion = (f32[2,2560,128]{2,1,0:T(8,128)S(1)}, bf16[2,2560,128]{2,1,0:T(8,128)(2,1)S(1)}) fusion(bf16[2,2560,128]{2,1,0:T(8,128)(2,1)} %collective-permute-done.21, bf16[2,2560,128]{2,1,0:T(8,128)(2,1)S(1)} %get-tuple-element.14), kind=kLoop, calls=%fused_computation | loop fusion | flops 2621440 | bytes 6553600 | tf_op jit(solution)/shard_map/add | solution.py:260
  68.3 0.8 collective-permute-start.23
  69.0 0.7 collective-permute-done.6
  69.7 1.7 %convert_add_fusion.1 = (f32[2,2560,128]{2,1,0:T(8,128)S(1)}, bf16[2,2560,128]{2,1,0:T(8,128)(2,1)S(1)}) fusion(bf16[2,2560,128]{2,1,0:T(8,128)(2,1)} %collective-permute-done.6, bf16[2,2560,128]{2,1,0:T(8,128)(2,1)S(1)} %get-tuple-element.11), kind=kLoop, calls=%fused_computation.1 | loop fusion | flops 2621440 | bytes 6553600 | tf_op jit(solution)/shard_map/add | solution.py:260
  71.5 0.9 collective-permute-start.8
  72.3 1.2 collective-permute-start.22
  73.5 5.5 %collective-permute-done.23 = bf16[2,640,128]{2,1,0:T(8,128)(2,1)S(1)} collective-permute-done((bf16[2,640,128]{2,1,0:T(8,128)(2,1)S(1)}, bf16[2,640,128]{2,1,0:T(8,128)(2,1)S(1)}, u32[]{:S(2)}, u32[]{:S(2)}) %collective-permute-start.23) | collective-permute-done | bytes 327712 | tf_op jit(solution)/shard_map/ppermute | solution.py:32
  79.0 0.1 add_convert_fusion.1
  79.1 2.3 %collective-permute-start.24 = (bf16[2,640,128]{2,1,0:T(8,128)(2,1)S(1)}, bf16[2,640,128]{2,1,0:T(8,128)(2,1)S(1)}, u32[]{:S(2)}, u32[]{:S(2)}) collective-permute-start(bf16[2,640,128]{2,1,0:T(8,128)(2,1)S(1)} %add_convert_fusion.1), channel_id=1, source_target_pairs={{0,4},{1,5},{2,6},{3,7},{4,0},{5,1},{6,2},{7,3},{8,12},{9,13},{10,... | collective-permute-start | bytes 983048 | tf_op jit(solution)/shard_map/ppermute | solution.py:32
  81.5 0.5 collective-permute-start.7
  82.0 4.1 %collective-permute-done.8 = bf16[2,640,128]{2,1,0:T(8,128)(2,1)S(1)} collective-permute-done((bf16[2,640,128]{2,1,0:T(8,128)(2,1)S(1)}, bf16[2,640,128]{2,1,0:T(8,128)(2,1)S(1)}, u32[]{:S(2)}, u32[]{:S(2)}) %collective-permute-start.8) | collective-permute-done | bytes 327712 | tf_op jit(solution)/shard_map/ppermute | solution.py:32
  86.1 0.1 add_convert_fusion.3
  86.2 2.3 %collective-permute-start.9 = (bf16[2,640,128]{2,1,0:T(8,128)(2,1)S(1)}, bf16[2,640,128]{2,1,0:T(8,128)(2,1)S(1)}, u32[]{:S(2)}, u32[]{:S(2)}) collective-permute-start(bf16[2,640,128]{2,1,0:T(8,128)(2,1)S(1)} %add_convert_fusion.3), channel_id=1, source_target_pairs={{0,4},{1,5},{2,6},{3,7},{4,0},{5,1},{6,2},{7,3},{8,12},{9,13},{10,... | collective-permute-start | bytes 983048 | tf_op jit(solution)/shard_map/ppermute | solution.py:32
  88.5 4.6 %collective-permute-done.22 = bf16[2,640,128]{2,1,0:T(8,128)(2,1)S(1)} collective-permute-done((bf16[2,640,128]{2,1,0:T(8,128)(2,1)S(1)}, bf16[2,640,128]{2,1,0:T(8,128)(2,1)S(1)}, u32[]{:S(2)}, u32[]{:S(2)}) %collective-permute-start.22) | collective-permute-done | bytes 327712 | tf_op jit(solution)/shard_map/ppermute | solution.py:32
  93.1 0.2 fusion.4
  93.2 2.0 %collective-permute-start.25 = (bf16[2,640,128]{2,1,0:T(8,128)(2,1)S(1)}, bf16[2,640,128]{2,1,0:T(8,128)(2,1)S(1)}, u32[]{:S(2)}, u32[]{:S(2)}) collective-permute-start(bf16[2,640,128]{2,1,0:T(8,128)(2,1)S(1)} %get-tuple-element.17), channel_id=1, source_target_pairs={{0,12},{1,13},{2,14},{3,15},{4,8},{5,9},{6,10},{7,11},{8,4},{9,5},... | collective-permute-start | bytes 983048 | tf_op jit(solution)/shard_map/ppermute | solution.py:32
  95.3 4.3 %collective-permute-done.7 = bf16[2,640,128]{2,1,0:T(8,128)(2,1)S(1)} collective-permute-done((bf16[2,640,128]{2,1,0:T(8,128)(2,1)S(1)}, bf16[2,640,128]{2,1,0:T(8,128)(2,1)S(1)}, u32[]{:S(2)}, u32[]{:S(2)}) %collective-permute-start.7) | collective-permute-done | bytes 327712 | tf_op jit(solution)/shard_map/ppermute | solution.py:32
  99.5 0.2 fusion.5
  99.7 2.0 %collective-permute-start.10 = (bf16[2,640,128]{2,1,0:T(8,128)(2,1)S(1)}, bf16[2,640,128]{2,1,0:T(8,128)(2,1)S(1)}, u32[]{:S(2)}, u32[]{:S(2)}) collective-permute-start(bf16[2,640,128]{2,1,0:T(8,128)(2,1)S(1)} %get-tuple-element.19), channel_id=1, source_target_pairs={{0,12},{1,13},{2,14},{3,15},{4,8},{5,9},{6,10},{7,11},{8,4},{9,5},... | collective-permute-start | bytes 983048 | tf_op jit(solution)/shard_map/ppermute | solution.py:32
  101.7 4.0 %collective-permute-done.25 = bf16[2,640,128]{2,1,0:T(8,128)(2,1)S(1)} collective-permute-done((bf16[2,640,128]{2,1,0:T(8,128)(2,1)S(1)}, bf16[2,640,128]{2,1,0:T(8,128)(2,1)S(1)}, u32[]{:S(2)}, u32[]{:S(2)}) %collective-permute-start.25) | collective-permute-done | bytes 327712 | tf_op jit(solution)/shard_map/ppermute | solution.py:32
  105.8 13.7 %collective-permute-start.26 = (bf16[2,640,128]{2,1,0:T(8,128)(2,1)S(1)}, bf16[2,640,128]{2,1,0:T(8,128)(2,1)S(1)}, u32[]{:S(2)}, u32[]{:S(2)}) collective-permute-start(bf16[2,640,128]{2,1,0:T(8,128)(2,1)S(1)} %add_convert_fusion), channel_id=1, source_target_pairs={{0,4},{1,5},{2,6},{3,7},{4,0},{5,1},{6,2},{7,3},{8,12},{9,13},{10,... | collective-permute-start | bytes 983048 | tf_op jit(solution)/shard_map/ppermute | solution.py:32
  119.5 0.5 collective-permute-start.27
  120.1 5.3 %collective-permute-start.11 = (bf16[2,640,128]{2,1,0:T(8,128)(2,1)S(1)}, bf16[2,640,128]{2,1,0:T(8,128)(2,1)S(1)}, u32[]{:S(2)}, u32[]{:S(2)}) collective-permute-start(bf16[2,640,128]{2,1,0:T(8,128)(2,1)S(1)} %add_convert_fusion.2), channel_id=1, source_target_pairs={{0,4},{1,5},{2,6},{3,7},{4,0},{5,1},{6,2},{7,3},{8,12},{9,13},{10,... | collective-permute-start | bytes 983048 | tf_op jit(solution)/shard_map/ppermute | solution.py:32
  125.3 0.5 collective-permute-start.12
  125.8 1.5 collective-permute-start.28
  127.4 0.1 broadcast_select_fusion.3
  127.5 0.1 collective-permute-start.29
  127.6 4.6 %collective-permute-done.11 = bf16[2,640,128]{2,1,0:T(8,128)(2,1)S(1)} collective-permute-done((bf16[2,640,128]{2,1,0:T(8,128)(2,1)S(1)}, bf16[2,640,128]{2,1,0:T(8,128)(2,1)S(1)}, u32[]{:S(2)}, u32[]{:S(2)}) %collective-permute-start.11) | collective-permute-done | bytes 327712 | tf_op jit(solution)/shard_map/ppermute | solution.py:32
  132.2 0.5 collective-permute-start.13
  132.6 0.1 broadcast_select_fusion.9
  132.7 10.3 %collective-permute-done.28 = bf16[2,640,128]{2,1,0:T(8,128)(2,1)S(1)} collective-permute-done((bf16[2,640,128]{2,1,0:T(8,128)(2,1)S(1)}, bf16[2,640,128]{2,1,0:T(8,128)(2,1)S(1)}, u32[]{:S(2)}, u32[]{:S(2)}) %collective-permute-start.28) | collective-permute-done | bytes 327712 | tf_op jit(solution)/shard_map/ppermute | solution.py:32
  143.1 0.1 collective-permute-start.30
  143.3 0.5 collective-permute-start.14
  143.8 3.9 %collective-permute-done.13 = bf16[2,640,128]{2,1,0:T(8,128)(2,1)S(1)} collective-permute-done((bf16[2,640,128]{2,1,0:T(8,128)(2,1)S(1)}, bf16[2,640,128]{2,1,0:T(8,128)(2,1)S(1)}, u32[]{:S(2)}, u32[]{:S(2)}) %collective-permute-start.13) | collective-permute-done | bytes 327712 | tf_op jit(solution)/shard_map/ppermute | solution.py:32
  147.8 1.9 %project.2.rest_0_ = f32[2,192,128]{2,1,0:T(8,128)S(1)} custom-call(s32[1]{0:T(128)} %bitcast.me_ref, bf16[2,1280,128]{2,1,0:T(8,128)(2,1)S(1)} %pad_maximum_fusion.2.pa, bf16[2,1280,128]{2,1,0:T(8,128)(2,1)S(1)} %pad_maximum_fusion.3.pb, bf16[2,1280,128]{2,1,0:T(8,128)(2,1)S(1)} %collective-permute-done.29.pc, ...), custom_call_target="tpu_custom_call" | custom-call | flops 503316480 | bytes 6553600 | tf_op jit(solution)/shard_map/project/pallas_call | solution.py:212
  149.9 2.1 %collective-permute-done.31.pd = bf16[2,1280,128]{2,1,0:T(8,128)(2,1)S(1)} collective-permute-done((bf16[2,1280,128]{2,1,0:T(8,128)(2,1)S(1)}, bf16[2,1280,128]{2,1,0:T(8,128)(2,1)S(1)}, u32[]{:S(2)}, u32[]{:S(2)}) %collective-permute-start.31) | collective-permute-done | bytes 655392 | tf_op jit(solution)/shard_map/ppermute | solution.py:32
  152.0 1.9 %project.3 = f32[6,128]{1,0:T(8,128)S(1)} custom-call(s32[1]{0:T(128)} %bitcast.me_ref, bf16[2,1280,128]{2,1,0:T(8,128)(2,1)S(1)} %pad_maximum_fusion.pa, bf16[2,1280,128]{2,1,0:T(8,128)(2,1)S(1)} %pad_maximum_fusion.1.pb, bf16[2,1280,128]{2,1,0:T(8,128)(2,1)S(1)} %collective-permute-done.14.pc, bf16[2,1280,128]{2,1,0:T(8,128)(2,1)S(1)} %collective-permute-done.31.pd, ...), custom_call_target="tpu_custom_call" | custom-call | flops 503316480 | bytes 6553600 | tf_op jit(solution)/shard_map/project/pallas_call | solution.py:212
  153.9 0.1 reshape.8
  154.0 0.1 reduce_sum.9
  154.1 0.8 fusion
  (61 shorter events, 0.9 us)
Async XLA Ops:
  0.0 25.1 %copy-start.9 = (bf16[2,320,128]{2,1,0:T(8,128)(2,1)S(1)}, bf16[2,320,128]{2,1,0:T(8,128)(2,1)}, u32[]{:S(2)}) copy-start(bf16[2,320,128]{2,1,0:T(8,128)(2,1)} %param.10) | copy-start | bytes 491524
  0.0 37.6 %copy-start.11 = (f32[2,320]{1,0:T(2,128)S(1)}, f32[2,320]{1,0:T(2,128)}, u32[]{:S(2)}) copy-start(f32[2,320]{1,0:T(2,128)} %param.13) | copy-start | bytes 7684
  0.0 37.6 %copy-start.10 = (f32[2,320]{1,0:T(2,128)S(1)}, f32[2,320]{1,0:T(2,128)}, u32[]{:S(2)}) copy-start(f32[2,320]{1,0:T(2,128)} %param.14) | copy-start | bytes 7684
  0.0 10.0 %collective-permute-start.15 = (bf16[2,320,128]{2,1,0:T(8,128)(2,1)}, bf16[2,320,128]{2,1,0:T(8,128)(2,1)S(1)}, u32[]{:S(2)}, u32[]{:S(2)}) collective-permute-start(bf16[2,320,128]{2,1,0:T(8,128)(2,1)} %param.9), channel_id=1, source_target_pairs={{0,4},{1,5},{2,6},{3,7},{4,0},{5,1},{6,2},{7,3},{8,12},{9,13},{10,... | collective-permute-start | bytes 491528 | tf_op jit(solution)/shard_map/ppermute | solution.py:32
  3.1 15.3 %collective-permute-start.16 = (bf16[2,320,128]{2,1,0:T(8,128)(2,1)}, bf16[2,320,128]{2,1,0:T(8,128)(2,1)S(1)}, u32[]{:S(2)}, u32[]{:S(2)}) collective-permute-start(bf16[2,320,128]{2,1,0:T(8,128)(2,1)} %param.9), channel_id=1, source_target_pairs={{0,8},{1,9},{2,10},{3,11},{4,12},{5,13},{6,14},{7,15},{8,0},{9,1},... | collective-permute-start | bytes 491528 | tf_op jit(solution)/shard_map/ppermute | solution.py:32
  5.7 12.7 %collective-permute-start.17 = (bf16[2,320,128]{2,1,0:T(8,128)(2,1)}, bf16[2,320,128]{2,1,0:T(8,128)(2,1)S(1)}, u32[]{:S(2)}, u32[]{:S(2)}) collective-permute-start(bf16[2,320,128]{2,1,0:T(8,128)(2,1)} %param.9), channel_id=1, source_target_pairs={{0,12},{1,13},{2,14},{3,15},{4,8},{5,9},{6,10},{7,11},{8,4},{9,5},... | collective-permute-start | bytes 491528 | tf_op jit(solution)/shard_map/ppermute | solution.py:32
  18.4 21.5 %copy-start.3 = (bf16[2,1280,128]{2,1,0:T(8,128)(2,1)}, bf16[2,1280,128]{2,1,0:T(8,128)(2,1)S(1)}, u32[]{:S(2)}) copy-start(bf16[2,1280,128]{2,1,0:T(8,128)(2,1)S(1)} %constant_dynamic-update-slice_fusion.4.refs_0_) | copy-start | bytes 1966084
  18.4 18.5 %collective-permute-start.18 = (bf16[2,1280,128]{2,1,0:T(8,128)(2,1)S(1)}, bf16[2,1280,128]{2,1,0:T(8,128)(2,1)S(1)}, u32[]{:S(2)}, u32[]{:S(2)}) collective-permute-start(bf16[2,1280,128]{2,1,0:T(8,128)(2,1)S(1)} %constant_dynamic-update-slice_fusion.4.refs_0_), channel_id=1, source_target_pairs={{0,2},{1,3},{2,0},{3,1},{4,6},{5,7},{6,4},{7,5},{8,10},{9,11},{10,... | collective-permute-start | bytes 1966088 | tf_op jit(solution)/shard_map/ppermute | solution.py:32
  20.0 8.0 %collective-permute-start = (bf16[2,320,128]{2,1,0:T(8,128)(2,1)}, bf16[2,320,128]{2,1,0:T(8,128)(2,1)S(1)}, u32[]{:S(2)}, u32[]{:S(2)}) collective-permute-start(bf16[2,320,128]{2,1,0:T(8,128)(2,1)} %param.10), channel_id=1, source_target_pairs={{0,4},{1,5},{2,6},{3,7},{4,0},{5,1},{6,2},{7,3},{8,12},{9,13},{10,... | collective-permute-start | bytes 491528 | tf_op jit(solution)/shard_map/ppermute | solution.py:32
  22.7 14.2 %collective-permute-start.1 = (bf16[2,320,128]{2,1,0:T(8,128)(2,1)}, bf16[2,320,128]{2,1,0:T(8,128)(2,1)S(1)}, u32[]{:S(2)}, u32[]{:S(2)}) collective-permute-start(bf16[2,320,128]{2,1,0:T(8,128)(2,1)} %param.10), channel_id=1, source_target_pairs={{0,8},{1,9},{2,10},{3,11},{4,12},{5,13},{6,14},{7,15},{8,0},{9,1},... | collective-permute-start | bytes 491528 | tf_op jit(solution)/shard_map/ppermute | solution.py:32
  23.6 13.2 %collective-permute-start.2 = (bf16[2,320,128]{2,1,0:T(8,128)(2,1)}, bf16[2,320,128]{2,1,0:T(8,128)(2,1)S(1)}, u32[]{:S(2)}, u32[]{:S(2)}) collective-permute-start(bf16[2,320,128]{2,1,0:T(8,128)(2,1)} %param.10), channel_id=1, source_target_pairs={{0,12},{1,13},{2,14},{3,15},{4,8},{5,9},{6,10},{7,11},{8,4},{9,5},... | collective-permute-start | bytes 491528 | tf_op jit(solution)/shard_map/ppermute | solution.py:32
  25.1 12.6 %collective-permute-start.19 = (bf16[2,1280,128]{2,1,0:T(8,128)(2,1)S(1)}, bf16[2,1280,128]{2,1,0:T(8,128)(2,1)S(1)}, u32[]{:S(2)}, u32[]{:S(2)}) collective-permute-start(bf16[2,1280,128]{2,1,0:T(8,128)(2,1)S(1)} %constant_dynamic-update-slice_fusion.4.refs_0_), channel_id=1, source_target_pairs={{0,1},{1,0},{2,3},{3,2},{4,5},{5,4},{6,7},{7,6},{8,9},{9,8},{10,11... | collective-permute-start | bytes 1966088 | tf_op jit(solution)/shard_map/ppermute | solution.py:32
  36.9 12.2 %copy-start.2 = (bf16[2,1280,128]{2,1,0:T(8,128)(2,1)}, bf16[2,1280,128]{2,1,0:T(8,128)(2,1)S(1)}, u32[]{:S(2)}) copy-start(bf16[2,1280,128]{2,1,0:T(8,128)(2,1)S(1)} %constant_dynamic-update-slice_fusion.refs_0_) | copy-start | bytes 1966084
  36.9 3.0 %copy-start.4 = (bf16[2,1280,128]{2,1,0:T(8,128)(2,1)}, bf16[2,1280,128]{2,1,0:T(8,128)(2,1)S(1)}, u32[]{:S(2)}) copy-start(bf16[2,1280,128]{2,1,0:T(8,128)(2,1)S(1)} %collective-permute-done.18.refs_1_) | copy-start | bytes 1966084
  36.9 2.2 %collective-permute-start.20 = (bf16[2,1280,128]{2,1,0:T(8,128)(2,1)S(1)}, bf16[2,1280,128]{2,1,0:T(8,128)(2,1)S(1)}, u32[]{:S(2)}, u32[]{:S(2)}) collective-permute-start(bf16[2,1280,128]{2,1,0:T(8,128)(2,1)S(1)} %collective-permute-done.18.refs_1_), channel_id=1, source_target_pairs={{0,1},{1,0},{2,3},{3,2},{4,5},{5,4},{6,7},{7,6},{8,9},{9,8},{10,11... | collective-permute-start | bytes 1966088 | tf_op jit(solution)/shard_map/ppermute | solution.py:32
  37.0 17.3 %collective-permute-start.3 = (bf16[2,1280,128]{2,1,0:T(8,128)(2,1)S(1)}, bf16[2,1280,128]{2,1,0:T(8,128)(2,1)}, u32[]{:S(2)}, u32[]{:S(2)}) collective-permute-start(bf16[2,1280,128]{2,1,0:T(8,128)(2,1)S(1)} %constant_dynamic-update-slice_fusion.refs_0_), channel_id=1, source_target_pairs={{0,2},{1,3},{2,0},{3,1},{4,6},{5,7},{6,4},{7,5},{8,10},{9,11},{10,... | collective-permute-start | bytes 1966088 | tf_op jit(solution)/shard_map/ppermute | solution.py:32
  37.8 1.3 copy-start.5
  39.1 0.8 copy-start.6
  48.9 17.7 %collective-permute-start.21 = (bf16[2,2560,128]{2,1,0:T(8,128)(2,1)}, bf16[2,2560,128]{2,1,0:T(8,128)(2,1)}, u32[]{:S(2)}, u32[]{:S(2)}) collective-permute-start(bf16[2,2560,128]{2,1,0:T(8,128)(2,1)} %get-tuple-element.15), channel_id=1, source_target_pairs={{0,1},{1,0},{2,3},{3,2},{4,5},{5,4},{6,7},{7,6},{8,9},{9,8},{10,11... | collective-permute-start | bytes 3932168 | tf_op jit(solution)/shard_map/ppermute | solution.py:32
  49.1 5.1 %collective-permute-start.4 = (bf16[2,1280,128]{2,1,0:T(8,128)(2,1)S(1)}, bf16[2,1280,128]{2,1,0:T(8,128)(2,1)S(1)}, u32[]{:S(2)}, u32[]{:S(2)}) collective-permute-start(bf16[2,1280,128]{2,1,0:T(8,128)(2,1)S(1)} %constant_dynamic-update-slice_fusion.refs_0_), channel_id=1, source_target_pairs={{0,1},{1,0},{2,3},{3,2},{4,5},{5,4},{6,7},{7,6},{8,9},{9,8},{10,11... | collective-permute-start | bytes 1966088 | tf_op jit(solution)/shard_map/ppermute | solution.py:32
  54.3 2.3 %collective-permute-start.5 = (bf16[2,1280,128]{2,1,0:T(8,128)(2,1)}, bf16[2,1280,128]{2,1,0:T(8,128)(2,1)S(1)}, u32[]{:S(2)}, u32[]{:S(2)}) collective-permute-start(bf16[2,1280,128]{2,1,0:T(8,128)(2,1)} %collective-permute-done.3.refs_1_), channel_id=1, source_target_pairs={{0,1},{1,0},{2,3},{3,2},{4,5},{5,4},{6,7},{7,6},{8,9},{9,8},{10,11... | collective-permute-start | bytes 1966088 | tf_op jit(solution)/shard_map/ppermute | solution.py:32
  54.3 2.3 %copy-start.7 = (bf16[2,1280,128]{2,1,0:T(8,128)(2,1)}, bf16[2,1280,128]{2,1,0:T(8,128)(2,1)S(1)}, u32[]{:S(2)}) copy-start(bf16[2,1280,128]{2,1,0:T(8,128)(2,1)S(1)} %collective-permute-done.4.refs_2_) | copy-start | bytes 1966084
  56.6 0.8 copy-start.8
  66.3 3.4 %collective-permute-start.6 = (bf16[2,2560,128]{2,1,0:T(8,128)(2,1)}, bf16[2,2560,128]{2,1,0:T(8,128)(2,1)}, u32[]{:S(2)}, u32[]{:S(2)}) collective-permute-start(bf16[2,2560,128]{2,1,0:T(8,128)(2,1)} %get-tuple-element.12), channel_id=1, source_target_pairs={{0,1},{1,0},{2,3},{3,2},{4,5},{5,4},{6,7},{7,6},{8,9},{9,8},{10,11... | collective-permute-start | bytes 3932168 | tf_op jit(solution)/shard_map/ppermute | solution.py:32
  68.3 10.8 %collective-permute-start.23 = (bf16[2,640,128]{2,1,0:T(8,128)(2,1)S(1)}, bf16[2,640,128]{2,1,0:T(8,128)(2,1)S(1)}, u32[]{:S(2)}, u32[]{:S(2)}) collective-permute-start(bf16[2,640,128]{2,1,0:T(8,128)(2,1)S(1)} %get-tuple-element.26), channel_id=1, source_target_pairs={{0,2},{1,3},{2,0},{3,1},{4,6},{5,7},{6,4},{7,5},{8,10},{9,11},{10,... | collective-permute-start | bytes 983048 | tf_op jit(solution)/shard_map/ppermute | solution.py:32
  71.5 14.6 %collective-permute-start.8 = (bf16[2,640,128]{2,1,0:T(8,128)(2,1)S(1)}, bf16[2,640,128]{2,1,0:T(8,128)(2,1)S(1)}, u32[]{:S(2)}, u32[]{:S(2)}) collective-permute-start(bf16[2,640,128]{2,1,0:T(8,128)(2,1)S(1)} %get-tuple-element.28), channel_id=1, source_target_pairs={{0,2},{1,3},{2,0},{3,1},{4,6},{5,7},{6,4},{7,5},{8,10},{9,11},{10,... | collective-permute-start | bytes 983048 | tf_op jit(solution)/shard_map/ppermute | solution.py:32
  72.3 20.8 %collective-permute-start.22 = (bf16[2,640,128]{2,1,0:T(8,128)(2,1)S(1)}, bf16[2,640,128]{2,1,0:T(8,128)(2,1)S(1)}, u32[]{:S(2)}, u32[]{:S(2)}) collective-permute-start(bf16[2,640,128]{2,1,0:T(8,128)(2,1)S(1)} %get-tuple-element.25), channel_id=1, source_target_pairs={{0,2},{1,3},{2,0},{3,1},{4,6},{5,7},{6,4},{7,5},{8,10},{9,11},{10,... | collective-permute-start | bytes 983048 | tf_op jit(solution)/shard_map/ppermute | solution.py:32
  79.1 14.0 %collective-permute-start.24 = (bf16[2,640,128]{2,1,0:T(8,128)(2,1)S(1)}, bf16[2,640,128]{2,1,0:T(8,128)(2,1)S(1)}, u32[]{:S(2)}, u32[]{:S(2)}) collective-permute-start(bf16[2,640,128]{2,1,0:T(8,128)(2,1)S(1)} %add_convert_fusion.1), channel_id=1, source_target_pairs={{0,4},{1,5},{2,6},{3,7},{4,0},{5,1},{6,2},{7,3},{8,12},{9,13},{10,... | collective-permute-start | bytes 983048 | tf_op jit(solution)/shard_map/ppermute | solution.py:32
  81.5 18.0 %collective-permute-start.7 = (bf16[2,640,128]{2,1,0:T(8,128)(2,1)S(1)}, bf16[2,640,128]{2,1,0:T(8,128)(2,1)S(1)}, u32[]{:S(2)}, u32[]{:S(2)}) collective-permute-start(bf16[2,640,128]{2,1,0:T(8,128)(2,1)S(1)} %get-tuple-element.27), channel_id=1, source_target_pairs={{0,2},{1,3},{2,0},{3,1},{4,6},{5,7},{6,4},{7,5},{8,10},{9,11},{10,... | collective-permute-start | bytes 983048 | tf_op jit(solution)/shard_map/ppermute | solution.py:32
  86.2 13.4 %collective-permute-start.9 = (bf16[2,640,128]{2,1,0:T(8,128)(2,1)S(1)}, bf16[2,640,128]{2,1,0:T(8,128)(2,1)S(1)}, u32[]{:S(2)}, u32[]{:S(2)}) collective-permute-start(bf16[2,640,128]{2,1,0:T(8,128)(2,1)S(1)} %add_convert_fusion.3), channel_id=1, source_target_pairs={{0,4},{1,5},{2,6},{3,7},{4,0},{5,1},{6,2},{7,3},{8,12},{9,13},{10,... | collective-permute-start | bytes 983048 | tf_op jit(solution)/shard_map/ppermute | solution.py:32
  93.2 12.5 %collective-permute-start.25 = (bf16[2,640,128]{2,1,0:T(8,128)(2,1)S(1)}, bf16[2,640,128]{2,1,0:T(8,128)(2,1)S(1)}, u32[]{:S(2)}, u32[]{:S(2)}) collective-permute-start(bf16[2,640,128]{2,1,0:T(8,128)(2,1)S(1)} %get-tuple-element.17), channel_id=1, source_target_pairs={{0,12},{1,13},{2,14},{3,15},{4,8},{5,9},{6,10},{7,11},{8,4},{9,5},... | collective-permute-start | bytes 983048 | tf_op jit(solution)/shard_map/ppermute | solution.py:32
  99.7 20.3 %collective-permute-start.10 = (bf16[2,640,128]{2,1,0:T(8,128)(2,1)S(1)}, bf16[2,640,128]{2,1,0:T(8,128)(2,1)S(1)}, u32[]{:S(2)}, u32[]{:S(2)}) collective-permute-start(bf16[2,640,128]{2,1,0:T(8,128)(2,1)S(1)} %get-tuple-element.19), channel_id=1, source_target_pairs={{0,12},{1,13},{2,14},{3,15},{4,8},{5,9},{6,10},{7,11},{8,4},{9,5},... | collective-permute-start | bytes 983048 | tf_op jit(solution)/shard_map/ppermute | solution.py:32
  105.8 20.0 %collective-permute-start.26 = (bf16[2,640,128]{2,1,0:T(8,128)(2,1)S(1)}, bf16[2,640,128]{2,1,0:T(8,128)(2,1)S(1)}, u32[]{:S(2)}, u32[]{:S(2)}) collective-permute-start(bf16[2,640,128]{2,1,0:T(8,128)(2,1)S(1)} %add_convert_fusion), channel_id=1, source_target_pairs={{0,4},{1,5},{2,6},{3,7},{4,0},{5,1},{6,2},{7,3},{8,12},{9,13},{10,... | collective-permute-start | bytes 983048 | tf_op jit(solution)/shard_map/ppermute | solution.py:32
  119.5 13.2 %collective-permute-start.27 = (bf16[2,640,128]{2,1,0:T(8,128)(2,1)S(1)}, bf16[2,640,128]{2,1,0:T(8,128)(2,1)S(1)}, u32[]{:S(2)}, u32[]{:S(2)}) collective-permute-start(bf16[2,640,128]{2,1,0:T(8,128)(2,1)S(1)} %add_convert_fusion), channel_id=1, source_target_pairs={{0,2},{1,3},{2,0},{3,1},{4,6},{5,7},{6,4},{7,5},{8,10},{9,11},{10,... | collective-permute-start | bytes 983048 | tf_op jit(solution)/shard_map/ppermute | solution.py:32
  120.1 12.1 %collective-permute-start.11 = (bf16[2,640,128]{2,1,0:T(8,128)(2,1)S(1)}, bf16[2,640,128]{2,1,0:T(8,128)(2,1)S(1)}, u32[]{:S(2)}, u32[]{:S(2)}) collective-permute-start(bf16[2,640,128]{2,1,0:T(8,128)(2,1)S(1)} %add_convert_fusion.2), channel_id=1, source_target_pairs={{0,4},{1,5},{2,6},{3,7},{4,0},{5,1},{6,2},{7,3},{8,12},{9,13},{10,... | collective-permute-start | bytes 983048 | tf_op jit(solution)/shard_map/ppermute | solution.py:32
  125.3 18.5 %collective-permute-start.12 = (bf16[2,640,128]{2,1,0:T(8,128)(2,1)S(1)}, bf16[2,640,128]{2,1,0:T(8,128)(2,1)S(1)}, u32[]{:S(2)}, u32[]{:S(2)}) collective-permute-start(bf16[2,640,128]{2,1,0:T(8,128)(2,1)S(1)} %add_convert_fusion.2), channel_id=1, source_target_pairs={{0,2},{1,3},{2,0},{3,1},{4,6},{5,7},{6,4},{7,5},{8,10},{9,11},{10,... | collective-permute-start | bytes 983048 | tf_op jit(solution)/shard_map/ppermute | solution.py:32
  125.8 17.2 %collective-permute-start.28 = (bf16[2,640,128]{2,1,0:T(8,128)(2,1)S(1)}, bf16[2,640,128]{2,1,0:T(8,128)(2,1)S(1)}, u32[]{:S(2)}, u32[]{:S(2)}) collective-permute-start(bf16[2,640,128]{2,1,0:T(8,128)(2,1)S(1)} %collective-permute-done.26), channel_id=1, source_target_pairs={{0,2},{1,3},{2,0},{3,1},{4,6},{5,7},{6,4},{7,5},{8,10},{9,11},{10,... | collective-permute-start | bytes 983048 | tf_op jit(solution)/shard_map/ppermute | solution.py:32
  127.5 20.3 %collective-permute-start.29 = (bf16[2,1280,128]{2,1,0:T(8,128)(2,1)S(1)}, bf16[2,1280,128]{2,1,0:T(8,128)(2,1)S(1)}, u32[]{:S(2)}, u32[]{:S(2)}) collective-permute-start(bf16[2,1280,128]{2,1,0:T(8,128)(2,1)S(1)} %pad_maximum_fusion.2.pa), channel_id=1, source_target_pairs={{0,1},{1,0},{2,3},{3,2},{4,5},{5,4},{6,7},{7,6},{8,9},{9,8},{10,11... | collective-permute-start | bytes 1966088 | tf_op jit(solution)/shard_map/ppermute | solution.py:32
  132.2 15.5 %collective-permute-start.13 = (bf16[2,640,128]{2,1,0:T(8,128)(2,1)S(1)}, bf16[2,640,128]{2,1,0:T(8,128)(2,1)S(1)}, u32[]{:S(2)}, u32[]{:S(2)}) collective-permute-start(bf16[2,640,128]{2,1,0:T(8,128)(2,1)S(1)} %collective-permute-done.11), channel_id=1, source_target_pairs={{0,2},{1,3},{2,0},{3,1},{4,6},{5,7},{6,4},{7,5},{8,10},{9,11},{10,... | collective-permute-start | bytes 983048 | tf_op jit(solution)/shard_map/ppermute | solution.py:32
  143.1 4.7 %collective-permute-start.30 = (bf16[2,1280,128]{2,1,0:T(8,128)(2,1)S(1)}, bf16[2,1280,128]{2,1,0:T(8,128)(2,1)S(1)}, u32[]{:S(2)}, u32[]{:S(2)}) collective-permute-start(bf16[2,1280,128]{2,1,0:T(8,128)(2,1)S(1)} %pad_maximum_fusion.3.pb), channel_id=1, source_target_pairs={{0,1},{1,0},{2,3},{3,2},{4,5},{5,4},{6,7},{7,6},{8,9},{9,8},{10,11... | collective-permute-start | bytes 1966088 | tf_op jit(solution)/shard_map/ppermute | solution.py:32
  143.2 4.6 %copy-start = (bf16[6,2,32,5120]{3,2,1,0:T(8,128)(2,1)S(1)}, bf16[6,2,32,5120]{3,2,1,0:T(8,128)(2,1)}, u32[]{:S(2)}) copy-start(bf16[6,2,32,5120]{3,2,1,0:T(8,128)(2,1)} %train.2) | copy-start | bytes 11796484
  143.3 6.6 %collective-permute-start.14 = (bf16[2,1280,128]{2,1,0:T(8,128)(2,1)S(1)}, bf16[2,1280,128]{2,1,0:T(8,128)(2,1)S(1)}, u32[]{:S(2)}, u32[]{:S(2)}) collective-permute-start(bf16[2,1280,128]{2,1,0:T(8,128)(2,1)S(1)} %pad_maximum_fusion.pa), channel_id=1, source_target_pairs={{0,1},{1,0},{2,3},{3,2},{4,5},{5,4},{6,7},{7,6},{8,9},{9,8},{10,11... | collective-permute-start | bytes 1966088 | tf_op jit(solution)/shard_map/ppermute | solution.py:32
  147.8 4.1 %copy-start.1 = (bf16[6,2,32,5120]{3,2,1,0:T(8,128)(2,1)S(1)}, bf16[6,2,32,5120]{3,2,1,0:T(8,128)(2,1)}, u32[]{:S(2)}) copy-start(bf16[6,2,32,5120]{3,2,1,0:T(8,128)(2,1)} %train.3) | copy-start | bytes 11796484
  149.8 4.3 %copy-start.12 = (s32[128]{0:T(128)S(1)}, s32[128]{0:T(128)}, u32[]{:S(2)}) copy-start(s32[128]{0:T(128)} %param.17) | copy-start | bytes 1540
  149.8 2.2 %collective-permute-start.31 = (bf16[2,1280,128]{2,1,0:T(8,128)(2,1)S(1)}, bf16[2,1280,128]{2,1,0:T(8,128)(2,1)S(1)}, u32[]{:S(2)}, u32[]{:S(2)}) collective-permute-start(bf16[2,1280,128]{2,1,0:T(8,128)(2,1)S(1)} %pad_maximum_fusion.1.pb), channel_id=1, source_target_pairs={{0,1},{1,0},{2,3},{3,2},{4,5},{5,4},{6,7},{7,6},{8,9},{9,8},{10,11... | collective-permute-start | bytes 1966088 | tf_op jit(solution)/shard_map/ppermute | solution.py:32

commit v5 on v4

--- a/solution.py
+++ b/solution.py
@@ -74,14 +74,16 @@
     return block, across, swap(block, n, 1), swap(across, n, 1)
 
 
-def sum_near(half, me, n):
-    quarter = half.shape[1] // 2
-    near, away = half[:, :quarter], half[:, quarter:].astype(BF16)
+def sum_near(keep, got, earlier, me, n):
+    quarter = keep.shape[1] // 2
+    near = keep[:, :quarter].astype(F32) + got[:, :quarter].astype(F32)
+    away = (keep[:, quarter:].astype(F32) + got[:, quarter:].astype(F32)).astype(BF16)
+    away = after(away, earlier)
     stages = far_stages(n, 2)
     if not stages or stages[0][1] == 1:
         total = near + swap(away, n, 2).astype(F32)
         block = sum_far(total, me, n, stages)
-        return block, swap(block, n, 2)
+        return block, swap(block, n, 2), total
     bit = stages[0][0]
     place = (me // bit) % 4
     first = (place == 0) | (place == 3)
@@ -89,12 +91,13 @@
     pick = lambda x, y: jnp.where(first, x, y)
     theirs = pick(near[:, high], near[:, low]) + swap(pick(away[:, high], away[:, low]), n, 2).astype(F32)
     mine = pick(near[:, low], near[:, high]) + swap(pick(away[:, low], away[:, high]), n, 2).astype(F32)
+    summed = mine
     mine = mine + swap(theirs.astype(BF16), n, bit).astype(F32)
     mine = mine + swap(mine.astype(BF16), n, 3 * bit).astype(F32)
     mine = sum_far(mine, me, n, stages[1:])
     theirs = swap(mine, n, bit)
     join = lambda x, y: jnp.concatenate([pick(x, y), pick(y, x)], axis=1)
-    return join(mine, theirs), join(swap(mine, n, 2), swap(theirs, n, 2))
+    return join(mine, theirs), join(swap(mine, n, 2), swap(theirs, n, 2)), summed
 
 
 def term_kernel(n, column, first, offsets, me_ref, *refs):
@@ -257,11 +260,11 @@
         earlier = []
         arrays = after(gathered[i], earlier)
         send, keep = terms(me, arrays, offsets, sides[side][1], eig, first, side * layers + first, n)
-        half = keep.astype(F32) + swap(send, n, 1).astype(F32)
-        halves.append(sum_near(half, me[0], n))
+        earlier = [done[2] for done in halves[-1:]]
+        halves.append(sum_near(keep, swap(send, n, 1), earlier, me[0], n))
     total, left = 0.0, ()
     for i, (first, side) in enumerate(chunks):
-        block, across = halves[i]
+        block, across, _ = halves[i]
         corner = swap(after(across, left), n, 1)
         left = (project(me, (block, across, swap(block, n, 1), corner), sides[side][2], first, n, left),)
         if side:

time: 155 us -> 145 us (0.935)
  starting transfers between devices: 48.7 us -> 35.4 us
  waiting for transfers between devices: 75.7 us -> 83 us
  Pallas kernels: 21.7 us -> 19.5 us
    ppermute x32, starting transfers between devices: 48.7 us -> 35.4 us  [swap(): return lax.ppermute(x, AXIS, [(t, t ^ mask) for t in range(n)])]
    ppermute x32, waiting for transfers between devices: 75.7 us -> 83 us  [swap(): return lax.ppermute(x, AXIS, [(t, t ^ mask) for t in range(n)])]
    pallas_call x2, Pallas kernels: 17.8 us -> 15.6 us  [terms(): pl.pallas_call(functools.partial(term_kernel, n, column, first, offsets),...]
  transfers between devices with their start and end apart: 32 -> 32, of which waited for: 17 -> 18; matrix products, arithmetic and copies ran while one was open for 4% -> 3% of each run, Pallas kernels for 13% -> 12%
where the time goes in v5:
time: 145 us; the launch traced here: 144 us
  waiting for transfers between devices  83 us (57%)
  starting transfers between devices  35.4 us (24%)
  Pallas kernels  19.5 us (13%)
  other arithmetic  3.2 us (2%)
  local copies, waits for them, and re-layouts  2.25 us (2%)
    ppermute x32, waiting for transfers between devices, swap(): return lax.ppermute(x, AXIS, [(t, t ^ mask) for t in range(n)])  83 us
    ppermute x32, starting transfers between devices, swap(): return lax.ppermute(x, AXIS, [(t, t ^ mask) for t in range(n)])  35.4 us
    pallas_call x2, Pallas kernels, terms(): pl.pallas_call(functools.partial(term_kernel, n, column, first, offsets),...  15.6 us
    pallas_call x2, Pallas kernels, project(): pl.pallas_call(functools.partial(proj_kernel, n, first), in_specs=[pl.Blo...  3.9 us
  transfers between devices with their start and end apart: 32, of which 18 were waited for; matrix products, arithmetic and copies ran while one was open for 3% of the time, Pallas kernels for 12%

profile of v5, /device:TPU:0, one launch (start us, length us, event | category | flops | bytes accessed | tf_op | source)
XLA Modules:
  0.0 144.5 jit_solution(11475351367016229794)
XLA Ops:
  0.0 3.1 %collective-permute-start.7 = (bf16[2,320,128]{2,1,0:T(8,128)(2,1)}, bf16[2,320,128]{2,1,0:T(8,128)(2,1)S(1)}, u32[]{:S(2)}, u32[]{:S(2)}) collective-permute-start(bf16[2,320,128]{2,1,0:T(8,128)(2,1)} %param.9), channel_id=1, source_target_pairs={{0,4},{1,5},{2,6},{3,7},{4,0},{5,1},{6,2},{7,3},{8,12},{9,13},{10,... | collective-permute-start | bytes 491528 | tf_op jit(solution)/shard_map/ppermute | solution.py:32
  3.1 2.6 %collective-permute-start.8 = (bf16[2,320,128]{2,1,0:T(8,128)(2,1)}, bf16[2,320,128]{2,1,0:T(8,128)(2,1)S(1)}, u32[]{:S(2)}, u32[]{:S(2)}) collective-permute-start(bf16[2,320,128]{2,1,0:T(8,128)(2,1)} %param.9), channel_id=1, source_target_pairs={{0,8},{1,9},{2,10},{3,11},{4,12},{5,13},{6,14},{7,15},{8,0},{9,1},... | collective-permute-start | bytes 491528 | tf_op jit(solution)/shard_map/ppermute | solution.py:32
  5.7 1.0 constant_dynamic-update-slice_fusion.7
  6.7 3.3 %collective-permute-done.7 = bf16[2,320,128]{2,1,0:T(8,128)(2,1)S(1)} collective-permute-done((bf16[2,320,128]{2,1,0:T(8,128)(2,1)}, bf16[2,320,128]{2,1,0:T(8,128)(2,1)S(1)}, u32[]{:S(2)}, u32[]{:S(2)}) %collective-permute-start.7) | collective-permute-done | bytes 163872 | tf_op jit(solution)/shard_map/ppermute | solution.py:32
  10.0 8.4 %collective-permute-done.8 = bf16[2,320,128]{2,1,0:T(8,128)(2,1)S(1)} collective-permute-done((bf16[2,320,128]{2,1,0:T(8,128)(2,1)}, bf16[2,320,128]{2,1,0:T(8,128)(2,1)S(1)}, u32[]{:S(2)}, u32[]{:S(2)}) %collective-permute-start.8) | collective-permute-done | bytes 163872 | tf_op jit(solution)/shard_map/ppermute | solution.py:32
  18.4 1.6 %collective-permute-start.10 = (bf16[2,1280,128]{2,1,0:T(8,128)(2,1)S(1)}, bf16[2,1280,128]{2,1,0:T(8,128)(2,1)S(1)}, u32[]{:S(2)}, u32[]{:S(2)}) collective-permute-start(bf16[2,1280,128]{2,1,0:T(8,128)(2,1)S(1)} %constant_dynamic-update-slice_fusion.4.refs_0_), channel_id=1, source_target_pairs={{0,2},{1,3},{2,0},{3,1},{4,6},{5,7},{6,4},{7,5},{8,10},{9,11},{10,... | collective-permute-start | bytes 1966088 | tf_op jit(solution)/shard_map/ppermute | solution.py:32
  20.0 2.6 %collective-permute-start = (bf16[2,320,128]{2,1,0:T(8,128)(2,1)}, bf16[2,320,128]{2,1,0:T(8,128)(2,1)S(1)}, u32[]{:S(2)}, u32[]{:S(2)}) collective-permute-start(bf16[2,320,128]{2,1,0:T(8,128)(2,1)} %param.10), channel_id=1, source_target_pairs={{0,4},{1,5},{2,6},{3,7},{4,0},{5,1},{6,2},{7,3},{8,12},{9,13},{10,... | collective-permute-start | bytes 491528 | tf_op jit(solution)/shard_map/ppermute | solution.py:32
  22.7 1.0 collective-permute-start.1
  23.6 1.5 %collective-permute-start.2 = (bf16[2,320,128]{2,1,0:T(8,128)(2,1)}, bf16[2,320,128]{2,1,0:T(8,128)(2,1)S(1)}, u32[]{:S(2)}, u32[]{:S(2)}) collective-permute-start(bf16[2,320,128]{2,1,0:T(8,128)(2,1)} %param.10), channel_id=1, source_target_pairs={{0,12},{1,13},{2,14},{3,15},{4,8},{5,9},{6,10},{7,11},{8,4},{9,5},... | collective-permute-start | bytes 491528 | tf_op jit(solution)/shard_map/ppermute | solution.py:32
  25.1 0.1 collective-permute-start.11
  25.2 2.9 %collective-permute-done = bf16[2,320,128]{2,1,0:T(8,128)(2,1)S(1)} collective-permute-done((bf16[2,320,128]{2,1,0:T(8,128)(2,1)}, bf16[2,320,128]{2,1,0:T(8,128)(2,1)S(1)}, u32[]{:S(2)}, u32[]{:S(2)}) %collective-permute-start) | collective-permute-done | bytes 163872 | tf_op jit(solution)/shard_map/ppermute | solution.py:32
  28.1 8.7 %collective-permute-done.1 = bf16[2,320,128]{2,1,0:T(8,128)(2,1)S(1)} collective-permute-done((bf16[2,320,128]{2,1,0:T(8,128)(2,1)}, bf16[2,320,128]{2,1,0:T(8,128)(2,1)S(1)}, u32[]{:S(2)}, u32[]{:S(2)}) %collective-permute-start.1) | collective-permute-done | bytes 163872 | tf_op jit(solution)/shard_map/ppermute | solution.py:32
  36.9 0.1 collective-permute-start.12
  37.1 0.1 copy.12
  37.2 0.6 collective-permute-start.3
  37.8 1.3 collective-permute-done.12.refs_3_
  39.1 0.8 copy-done.6
  40.0 7.8 %terms.3 = (bf16[2,2560,128]{2,1,0:T(8,128)(2,1)S(1)}, bf16[2,2560,128]{2,1,0:T(8,128)(2,1)S(1)}) custom-call(s32[1]{0:T(128)} %bitcast.me_ref, bf16[2,1280,128]{2,1,0:T(8,128)(2,1)} %copy-done.3, bf16[2,1280,128]{2,1,0:T(8,128)(2,1)} %copy-done.4, bf16[2,1280,128]{2,1,0:T(8,128)(2,1)} %copy-done.5, bf16[2,1280,128]{2,1,0:T(8,128)(2,1)} %copy-done.6, ...), custom_call_target="tpu_custom_call" | custom-call | flops 1677721600 | bytes 11796480 | tf_op jit(solution)/shard_map/terms/pallas_call | solution.py:158
  47.8 0.3 collective-permute-start.13
  48.0 0.3 collective-permute-start.4
  48.3 6.1 %collective-permute-done.3.refs_1_ = bf16[2,1280,128]{2,1,0:T(8,128)(2,1)} collective-permute-done((bf16[2,1280,128]{2,1,0:T(8,128)(2,1)S(1)}, bf16[2,1280,128]{2,1,0:T(8,128)(2,1)}, u32[]{:S(2)}, u32[]{:S(2)}) %collective-permute-start.3) | collective-permute-done | bytes 655392 | tf_op jit(solution)/shard_map/ppermute | solution.py:32
  54.5 2.4 %collective-permute-done.5.refs_3_ = bf16[2,1280,128]{2,1,0:T(8,128)(2,1)} collective-permute-done((bf16[2,1280,128]{2,1,0:T(8,128)(2,1)}, bf16[2,1280,128]{2,1,0:T(8,128)(2,1)}, u32[]{:S(2)}, u32[]{:S(2)}) %collective-permute-start.5) | collective-permute-done | bytes 655392 | tf_op jit(solution)/shard_map/ppermute | solution.py:32
  56.9 7.8 %terms.2 = (bf16[2,2560,128]{2,1,0:T(8,128)(2,1)S(1)}, bf16[2,2560,128]{2,1,0:T(8,128)(2,1)S(1)}) custom-call(s32[1]{0:T(128)} %bitcast.me_ref, bf16[2,1280,128]{2,1,0:T(8,128)(2,1)} %copy-done.2, bf16[2,1280,128]{2,1,0:T(8,128)(2,1)} %collective-permute-done.3.refs_1_, bf16[2,1280,128]{2,1,0:T(8,128)(2,1)} %collective-permute-done.4.refs_2_, ...), custom_call_target="tpu_custom_call" | custom-call | flops 1677721600 | bytes 11796480 | tf_op jit(solution)/shard_map/terms/pallas_call | solution.py:158
  64.7 0.3 collective-permute-start.6
  65.0 1.6 %convert_add_fusion = (f32[2,1280,128]{2,1,0:T(8,128)S(1)}, bf16[2,1280,128]{2,1,0:T(8,128)(2,1)S(1)}) fusion(bf16[2,2560,128]{2,1,0:T(8,128)(2,1)} %collective-permute-done.13, bf16[2,2560,128]{2,1,0:T(8,128)(2,1)S(1)} %get-tuple-element.15), kind=kLoop, calls=%fused_computation.1 | loop fusion | flops 2293760 | bytes 4587520 | tf_op jit(solution)/shard_map/add | solution.py:79
  66.6 0.6 collective-permute-start.23
  67.2 1.5 %collective-permute-start.14 = (bf16[2,640,128]{2,1,0:T(8,128)(2,1)S(1)}, bf16[2,640,128]{2,1,0:T(8,128)(2,1)S(1)}, u32[]{:S(2)}, u32[]{:S(2)}) collective-permute-start(bf16[2,640,128]{2,1,0:T(8,128)(2,1)S(1)} %get-tuple-element.37), channel_id=1, source_target_pairs={{0,2},{1,3},{2,0},{3,1},{4,6},{5,7},{6,4},{7,5},{8,10},{9,11},{10,... | collective-permute-start | bytes 983048 | tf_op jit(solution)/shard_map/ppermute | solution.py:32
  68.7 8.5 %collective-permute-done.23 = bf16[2,640,128]{2,1,0:T(8,128)(2,1)S(1)} collective-permute-done((bf16[2,640,128]{2,1,0:T(8,128)(2,1)S(1)}, bf16[2,640,128]{2,1,0:T(8,128)(2,1)S(1)}, u32[]{:S(2)}, u32[]{:S(2)}) %collective-permute-start.23) | collective-permute-done | bytes 327712 | tf_op jit(solution)/shard_map/ppermute | solution.py:32
  77.2 0.1 add_convert_fusion.3
  77.3 2.3 %collective-permute-start.24 = (bf16[2,640,128]{2,1,0:T(8,128)(2,1)S(1)}, bf16[2,640,128]{2,1,0:T(8,128)(2,1)S(1)}, u32[]{:S(2)}, u32[]{:S(2)}) collective-permute-start(bf16[2,640,128]{2,1,0:T(8,128)(2,1)S(1)} %add_convert_fusion.3), channel_id=1, source_target_pairs={{0,4},{1,5},{2,6},{3,7},{4,0},{5,1},{6,2},{7,3},{8,12},{9,13},{10,... | collective-permute-start | bytes 983048 | tf_op jit(solution)/shard_map/ppermute | solution.py:32
  79.7 0.3 convert_add_fusion.1
  80.0 3.7 %collective-permute-done.14 = bf16[2,640,128]{2,1,0:T(8,128)(2,1)S(1)} collective-permute-done((bf16[2,640,128]{2,1,0:T(8,128)(2,1)S(1)}, bf16[2,640,128]{2,1,0:T(8,128)(2,1)S(1)}, u32[]{:S(2)}, u32[]{:S(2)}) %collective-permute-start.14) | collective-permute-done | bytes 327712 | tf_op jit(solution)/shard_map/ppermute | solution.py:32
  83.7 2.8 %collective-permute-done.24 = bf16[2,640,128]{2,1,0:T(8,128)(2,1)S(1)} collective-permute-done((bf16[2,640,128]{2,1,0:T(8,128)(2,1)S(1)}, bf16[2,640,128]{2,1,0:T(8,128)(2,1)S(1)}, u32[]{:S(2)}, u32[]{:S(2)}) %collective-permute-start.24) | collective-permute-done | bytes 327712 | tf_op jit(solution)/shard_map/ppermute | solution.py:32
  86.5 0.1 fusion
  86.7 0.6 collective-permute-start.16
  87.2 2.6 %collective-permute-start.25 = (bf16[2,640,128]{2,1,0:T(8,128)(2,1)S(1)}, bf16[2,640,128]{2,1,0:T(8,128)(2,1)S(1)}, u32[]{:S(2)}, u32[]{:S(2)}) collective-permute-start(bf16[2,640,128]{2,1,0:T(8,128)(2,1)S(1)} %get-tuple-element.19), channel_id=1, source_target_pairs={{0,12},{1,13},{2,14},{3,15},{4,8},{5,9},{6,10},{7,11},{8,4},{9,5},... | collective-permute-start | bytes 983048 | tf_op jit(solution)/shard_map/ppermute | solution.py:32
  89.8 1.5 %collective-permute-start.15 = (bf16[2,640,128]{2,1,0:T(8,128)(2,1)S(1)}, bf16[2,640,128]{2,1,0:T(8,128)(2,1)S(1)}, u32[]{:S(2)}, u32[]{:S(2)}) collective-permute-start(bf16[2,640,128]{2,1,0:T(8,128)(2,1)S(1)} %get-tuple-element.35), channel_id=1, source_target_pairs={{0,2},{1,3},{2,0},{3,1},{4,6},{5,7},{6,4},{7,5},{8,10},{9,11},{10,... | collective-permute-start | bytes 983048 | tf_op jit(solution)/shard_map/ppermute | solution.py:32
  91.3 6.0 %collective-permute-done.16 = bf16[2,640,128]{2,1,0:T(8,128)(2,1)S(1)} collective-permute-done((bf16[2,640,128]{2,1,0:T(8,128)(2,1)S(1)}, bf16[2,640,128]{2,1,0:T(8,128)(2,1)S(1)}, u32[]{:S(2)}, u32[]{:S(2)}) %collective-permute-start.16) | collective-permute-done | bytes 327712 | tf_op jit(solution)/shard_map/ppermute | solution.py:32
  97.4 0.1 add_convert_fusion.5
  97.5 1.8 %collective-permute-start.17 = (bf16[2,640,128]{2,1,0:T(8,128)(2,1)S(1)}, bf16[2,640,128]{2,1,0:T(8,128)(2,1)S(1)}, u32[]{:S(2)}, u32[]{:S(2)}) collective-permute-start(bf16[2,640,128]{2,1,0:T(8,128)(2,1)S(1)} %add_convert_fusion.5), channel_id=1, source_target_pairs={{0,4},{1,5},{2,6},{3,7},{4,0},{5,1},{6,2},{7,3},{8,12},{9,13},{10,... | collective-permute-start | bytes 983048 | tf_op jit(solution)/shard_map/ppermute | solution.py:32
  99.3 0.1 add_convert_fusion.2
  99.4 4.1 %collective-permute-start.26 = (bf16[2,640,128]{2,1,0:T(8,128)(2,1)S(1)}, bf16[2,640,128]{2,1,0:T(8,128)(2,1)S(1)}, u32[]{:S(2)}, u32[]{:S(2)}) collective-permute-start(bf16[2,640,128]{2,1,0:T(8,128)(2,1)S(1)} %add_convert_fusion.2), channel_id=1, source_target_pairs={{0,4},{1,5},{2,6},{3,7},{4,0},{5,1},{6,2},{7,3},{8,12},{9,13},{10,... | collective-permute-start | bytes 983048 | tf_op jit(solution)/shard_map/ppermute | solution.py:32
  103.5 1.5 %collective-permute-start.27 = (bf16[2,640,128]{2,1,0:T(8,128)(2,1)S(1)}, bf16[2,640,128]{2,1,0:T(8,128)(2,1)S(1)}, u32[]{:S(2)}, u32[]{:S(2)}) collective-permute-start(bf16[2,640,128]{2,1,0:T(8,128)(2,1)S(1)} %add_convert_fusion.2), channel_id=1, source_target_pairs={{0,2},{1,3},{2,0},{3,1},{4,6},{5,7},{6,4},{7,5},{8,10},{9,11},{10,... | collective-permute-start | bytes 983048 | tf_op jit(solution)/shard_map/ppermute | solution.py:32
  105.0 0.7 collective-permute-done.17
  105.7 0.2 fusion.3
  105.9 2.6 %collective-permute-start.18 = (bf16[2,640,128]{2,1,0:T(8,128)(2,1)S(1)}, bf16[2,640,128]{2,1,0:T(8,128)(2,1)S(1)}, u32[]{:S(2)}, u32[]{:S(2)}) collective-permute-start(bf16[2,640,128]{2,1,0:T(8,128)(2,1)S(1)} %get-tuple-element.21), channel_id=1, source_target_pairs={{0,12},{1,13},{2,14},{3,15},{4,8},{5,9},{6,10},{7,11},{8,4},{9,5},... | collective-permute-start | bytes 983048 | tf_op jit(solution)/shard_map/ppermute | solution.py:32
  108.5 3.5 %collective-permute-done.26 = bf16[2,640,128]{2,1,0:T(8,128)(2,1)S(1)} collective-permute-done((bf16[2,640,128]{2,1,0:T(8,128)(2,1)S(1)}, bf16[2,640,128]{2,1,0:T(8,128)(2,1)S(1)}, u32[]{:S(2)}, u32[]{:S(2)}) %collective-permute-start.26) | collective-permute-done | bytes 327712 | tf_op jit(solution)/shard_map/ppermute | solution.py:32
  112.0 1.2 collective-permute-start.28
  113.2 0.1 broadcast_select_fusion.3
  113.4 7.6 %collective-permute-done.18 = bf16[2,640,128]{2,1,0:T(8,128)(2,1)S(1)} collective-permute-done((bf16[2,640,128]{2,1,0:T(8,128)(2,1)S(1)}, bf16[2,640,128]{2,1,0:T(8,128)(2,1)S(1)}, u32[]{:S(2)}, u32[]{:S(2)}) %collective-permute-start.18) | collective-permute-done | bytes 327712 | tf_op jit(solution)/shard_map/ppermute | solution.py:32
  121.1 0.1 add_convert_fusion.4
  121.1 0.8 collective-permute-start.19
  122.2 0.1 collective-permute-start.20
  122.2 7.5 %collective-permute-done.19 = bf16[2,640,128]{2,1,0:T(8,128)(2,1)S(1)} collective-permute-done((bf16[2,640,128]{2,1,0:T(8,128)(2,1)S(1)}, bf16[2,640,128]{2,1,0:T(8,128)(2,1)S(1)}, u32[]{:S(2)}, u32[]{:S(2)}) %collective-permute-start.19) | collective-permute-done | bytes 327712 | tf_op jit(solution)/shard_map/ppermute | solution.py:32
  129.7 0.1 broadcast_select_fusion.8
  130.0 1.9 %project.2.rest_0_ = f32[2,192,128]{2,1,0:T(8,128)S(1)} custom-call(s32[1]{0:T(128)} %bitcast.me_ref, bf16[2,1280,128]{2,1,0:T(8,128)(2,1)S(1)} %pad_maximum_fusion.2.pa, bf16[2,1280,128]{2,1,0:T(8,128)(2,1)S(1)} %pad_maximum_fusion.3.pb, bf16[2,1280,128]{2,1,0:T(8,128)(2,1)S(1)} %collective-permute-done.29.pc, ...), custom_call_target="tpu_custom_call" | custom-call | flops 503316480 | bytes 6553600 | tf_op jit(solution)/shard_map/project/pallas_call | solution.py:215
  132.0 0.8 collective-permute-done.20
  132.7 6.6 %collective-permute-done.21 = bf16[2,640,128]{2,1,0:T(8,128)(2,1)S(1)} collective-permute-done((bf16[2,640,128]{2,1,0:T(8,128)(2,1)S(1)}, bf16[2,640,128]{2,1,0:T(8,128)(2,1)S(1)}, u32[]{:S(2)}, u32[]{:S(2)}) %collective-permute-start.21) | collective-permute-done | bytes 327712 | tf_op jit(solution)/shard_map/ppermute | solution.py:32
  139.4 0.1 collective-permute-start.31
  139.5 2.1 %collective-permute-done.31.pd = bf16[2,1280,128]{2,1,0:T(8,128)(2,1)S(1)} collective-permute-done((bf16[2,1280,128]{2,1,0:T(8,128)(2,1)S(1)}, bf16[2,1280,128]{2,1,0:T(8,128)(2,1)S(1)}, u32[]{:S(2)}, u32[]{:S(2)}) %collective-permute-start.31) | collective-permute-done | bytes 655392 | tf_op jit(solution)/shard_map/ppermute | solution.py:32
  141.6 2.0 %project.3 = f32[6,128]{1,0:T(8,128)S(1)} custom-call(s32[1]{0:T(128)} %bitcast.me_ref, bf16[2,1280,128]{2,1,0:T(8,128)(2,1)S(1)} %pad_maximum_fusion.pa, bf16[2,1280,128]{2,1,0:T(8,128)(2,1)S(1)} %pad_maximum_fusion.1.pb, bf16[2,1280,128]{2,1,0:T(8,128)(2,1)S(1)} %collective-permute-done.22.pc, bf16[2,1280,128]{2,1,0:T(8,128)(2,1)S(1)} %collective-permute-done.31.pd, ...), custom_call_target="tpu_custom_call" | custom-call | flops 503316480 | bytes 6553600 | tf_op jit(solution)/shard_map/project/pallas_call | solution.py:215
  143.6 0.1 reshape.8
  143.6 0.1 reduce_sum.9
  143.7 0.8 fusion.1
  (57 shorter events, 0.8 us)
Async XLA Ops:
  0.0 25.1 %copy-start.7 = (bf16[2,320,128]{2,1,0:T(8,128)(2,1)S(1)}, bf16[2,320,128]{2,1,0:T(8,128)(2,1)}, u32[]{:S(2)}) copy-start(bf16[2,320,128]{2,1,0:T(8,128)(2,1)} %param.10) | copy-start | bytes 491524
  0.0 37.0 %copy-start.9 = (f32[2,320]{1,0:T(2,128)S(1)}, f32[2,320]{1,0:T(2,128)}, u32[]{:S(2)}) copy-start(f32[2,320]{1,0:T(2,128)} %param.13) | copy-start | bytes 7684
  0.0 37.0 %copy-start.8 = (f32[2,320]{1,0:T(2,128)S(1)}, f32[2,320]{1,0:T(2,128)}, u32[]{:S(2)}) copy-start(f32[2,320]{1,0:T(2,128)} %param.14) | copy-start | bytes 7684
  0.0 10.0 %collective-permute-start.7 = (bf16[2,320,128]{2,1,0:T(8,128)(2,1)}, bf16[2,320,128]{2,1,0:T(8,128)(2,1)S(1)}, u32[]{:S(2)}, u32[]{:S(2)}) collective-permute-start(bf16[2,320,128]{2,1,0:T(8,128)(2,1)} %param.9), channel_id=1, source_target_pairs={{0,4},{1,5},{2,6},{3,7},{4,0},{5,1},{6,2},{7,3},{8,12},{9,13},{10,... | collective-permute-start | bytes 491528 | tf_op jit(solution)/shard_map/ppermute | solution.py:32
  3.1 15.3 %collective-permute-start.8 = (bf16[2,320,128]{2,1,0:T(8,128)(2,1)}, bf16[2,320,128]{2,1,0:T(8,128)(2,1)S(1)}, u32[]{:S(2)}, u32[]{:S(2)}) collective-permute-start(bf16[2,320,128]{2,1,0:T(8,128)(2,1)} %param.9), channel_id=1, source_target_pairs={{0,8},{1,9},{2,10},{3,11},{4,12},{5,13},{6,14},{7,15},{8,0},{9,1},... | collective-permute-start | bytes 491528 | tf_op jit(solution)/shard_map/ppermute | solution.py:32
  5.7 12.7 %collective-permute-start.9 = (bf16[2,320,128]{2,1,0:T(8,128)(2,1)}, bf16[2,320,128]{2,1,0:T(8,128)(2,1)S(1)}, u32[]{:S(2)}, u32[]{:S(2)}) collective-permute-start(bf16[2,320,128]{2,1,0:T(8,128)(2,1)} %param.9), channel_id=1, source_target_pairs={{0,12},{1,13},{2,14},{3,15},{4,8},{5,9},{6,10},{7,11},{8,4},{9,5},... | collective-permute-start | bytes 491528 | tf_op jit(solution)/shard_map/ppermute | solution.py:32
  18.4 20.7 %copy-start.3 = (bf16[2,1280,128]{2,1,0:T(8,128)(2,1)}, bf16[2,1280,128]{2,1,0:T(8,128)(2,1)S(1)}, u32[]{:S(2)}) copy-start(bf16[2,1280,128]{2,1,0:T(8,128)(2,1)S(1)} %constant_dynamic-update-slice_fusion.4.refs_0_) | copy-start | bytes 1966084
  18.4 18.5 %collective-permute-start.10 = (bf16[2,1280,128]{2,1,0:T(8,128)(2,1)S(1)}, bf16[2,1280,128]{2,1,0:T(8,128)(2,1)S(1)}, u32[]{:S(2)}, u32[]{:S(2)}) collective-permute-start(bf16[2,1280,128]{2,1,0:T(8,128)(2,1)S(1)} %constant_dynamic-update-slice_fusion.4.refs_0_), channel_id=1, source_target_pairs={{0,2},{1,3},{2,0},{3,1},{4,6},{5,7},{6,4},{7,5},{8,10},{9,11},{10,... | collective-permute-start | bytes 1966088 | tf_op jit(solution)/shard_map/ppermute | solution.py:32
  20.0 8.0 %collective-permute-start = (bf16[2,320,128]{2,1,0:T(8,128)(2,1)}, bf16[2,320,128]{2,1,0:T(8,128)(2,1)S(1)}, u32[]{:S(2)}, u32[]{:S(2)}) collective-permute-start(bf16[2,320,128]{2,1,0:T(8,128)(2,1)} %param.10), channel_id=1, source_target_pairs={{0,4},{1,5},{2,6},{3,7},{4,0},{5,1},{6,2},{7,3},{8,12},{9,13},{10,... | collective-permute-start | bytes 491528 | tf_op jit(solution)/shard_map/ppermute | solution.py:32
  22.7 14.2 %collective-permute-start.1 = (bf16[2,320,128]{2,1,0:T(8,128)(2,1)}, bf16[2,320,128]{2,1,0:T(8,128)(2,1)S(1)}, u32[]{:S(2)}, u32[]{:S(2)}) collective-permute-start(bf16[2,320,128]{2,1,0:T(8,128)(2,1)} %param.10), channel_id=1, source_target_pairs={{0,8},{1,9},{2,10},{3,11},{4,12},{5,13},{6,14},{7,15},{8,0},{9,1},... | collective-permute-start | bytes 491528 | tf_op jit(solution)/shard_map/ppermute | solution.py:32
  23.6 13.2 %collective-permute-start.2 = (bf16[2,320,128]{2,1,0:T(8,128)(2,1)}, bf16[2,320,128]{2,1,0:T(8,128)(2,1)S(1)}, u32[]{:S(2)}, u32[]{:S(2)}) collective-permute-start(bf16[2,320,128]{2,1,0:T(8,128)(2,1)} %param.10), channel_id=1, source_target_pairs={{0,12},{1,13},{2,14},{3,15},{4,8},{5,9},{6,10},{7,11},{8,4},{9,5},... | collective-permute-start | bytes 491528 | tf_op jit(solution)/shard_map/ppermute | solution.py:32
  25.1 12.6 %collective-permute-start.11 = (bf16[2,1280,128]{2,1,0:T(8,128)(2,1)S(1)}, bf16[2,1280,128]{2,1,0:T(8,128)(2,1)S(1)}, u32[]{:S(2)}, u32[]{:S(2)}) collective-permute-start(bf16[2,1280,128]{2,1,0:T(8,128)(2,1)S(1)} %constant_dynamic-update-slice_fusion.4.refs_0_), channel_id=1, source_target_pairs={{0,1},{1,0},{2,3},{3,2},{4,5},{5,4},{6,7},{7,6},{8,9},{9,8},{10,11... | collective-permute-start | bytes 1966088 | tf_op jit(solution)/shard_map/ppermute | solution.py:32
  36.9 11.1 %copy-start.2 = (bf16[2,1280,128]{2,1,0:T(8,128)(2,1)}, bf16[2,1280,128]{2,1,0:T(8,128)(2,1)S(1)}, u32[]{:S(2)}) copy-start(bf16[2,1280,128]{2,1,0:T(8,128)(2,1)S(1)} %constant_dynamic-update-slice_fusion.refs_0_) | copy-start | bytes 1966084
  36.9 2.2 %copy-start.4 = (bf16[2,1280,128]{2,1,0:T(8,128)(2,1)}, bf16[2,1280,128]{2,1,0:T(8,128)(2,1)S(1)}, u32[]{:S(2)}) copy-start(bf16[2,1280,128]{2,1,0:T(8,128)(2,1)S(1)} %collective-permute-done.10.refs_1_) | copy-start | bytes 1966084
  36.9 2.2 %collective-permute-start.12 = (bf16[2,1280,128]{2,1,0:T(8,128)(2,1)S(1)}, bf16[2,1280,128]{2,1,0:T(8,128)(2,1)S(1)}, u32[]{:S(2)}, u32[]{:S(2)}) collective-permute-start(bf16[2,1280,128]{2,1,0:T(8,128)(2,1)S(1)} %collective-permute-done.10.refs_1_), channel_id=1, source_target_pairs={{0,1},{1,0},{2,3},{3,2},{4,5},{5,4},{6,7},{7,6},{8,9},{9,8},{10,11... | collective-permute-start | bytes 1966088 | tf_op jit(solution)/shard_map/ppermute | solution.py:32
  37.2 17.3 %collective-permute-start.3 = (bf16[2,1280,128]{2,1,0:T(8,128)(2,1)S(1)}, bf16[2,1280,128]{2,1,0:T(8,128)(2,1)}, u32[]{:S(2)}, u32[]{:S(2)}) collective-permute-start(bf16[2,1280,128]{2,1,0:T(8,128)(2,1)S(1)} %constant_dynamic-update-slice_fusion.refs_0_), channel_id=1, source_target_pairs={{0,2},{1,3},{2,0},{3,1},{4,6},{5,7},{6,4},{7,5},{8,10},{9,11},{10,... | collective-permute-start | bytes 1966088 | tf_op jit(solution)/shard_map/ppermute | solution.py:32
  37.8 1.3 copy-start.5
  39.1 0.9 copy-start.6
  47.8 17.2 %collective-permute-start.13 = (bf16[2,2560,128]{2,1,0:T(8,128)(2,1)S(1)}, bf16[2,2560,128]{2,1,0:T(8,128)(2,1)}, u32[]{:S(2)}, u32[]{:S(2)}) collective-permute-start(bf16[2,2560,128]{2,1,0:T(8,128)(2,1)S(1)} %get-tuple-element.16), channel_id=1, source_target_pairs={{0,1},{1,0},{2,3},{3,2},{4,5},{5,4},{6,7},{7,6},{8,9},{9,8},{10,11... | collective-permute-start | bytes 3932168 | tf_op jit(solution)/shard_map/ppermute | solution.py:32
  48.0 6.5 %collective-permute-start.4 = (bf16[2,1280,128]{2,1,0:T(8,128)(2,1)S(1)}, bf16[2,1280,128]{2,1,0:T(8,128)(2,1)}, u32[]{:S(2)}, u32[]{:S(2)}) collective-permute-start(bf16[2,1280,128]{2,1,0:T(8,128)(2,1)S(1)} %constant_dynamic-update-slice_fusion.refs_0_), channel_id=1, source_target_pairs={{0,1},{1,0},{2,3},{3,2},{4,5},{5,4},{6,7},{7,6},{8,9},{9,8},{10,11... | collective-permute-start | bytes 1966088 | tf_op jit(solution)/shard_map/ppermute | solution.py:32
  54.5 2.4 %collective-permute-start.5 = (bf16[2,1280,128]{2,1,0:T(8,128)(2,1)}, bf16[2,1280,128]{2,1,0:T(8,128)(2,1)}, u32[]{:S(2)}, u32[]{:S(2)}) collective-permute-start(bf16[2,1280,128]{2,1,0:T(8,128)(2,1)} %collective-permute-done.3.refs_1_), channel_id=1, source_target_pairs={{0,1},{1,0},{2,3},{3,2},{4,5},{5,4},{6,7},{7,6},{8,9},{9,8},{10,11... | collective-permute-start | bytes 1966088 | tf_op jit(solution)/shard_map/ppermute | solution.py:32
  64.7 15.0 %collective-permute-start.6 = (bf16[2,2560,128]{2,1,0:T(8,128)(2,1)S(1)}, bf16[2,2560,128]{2,1,0:T(8,128)(2,1)S(1)}, u32[]{:S(2)}, u32[]{:S(2)}) collective-permute-start(bf16[2,2560,128]{2,1,0:T(8,128)(2,1)S(1)} %get-tuple-element.13), channel_id=1, source_target_pairs={{0,1},{1,0},{2,3},{3,2},{4,5},{5,4},{6,7},{7,6},{8,9},{9,8},{10,11... | collective-permute-start | bytes 3932168 | tf_op jit(solution)/shard_map/ppermute | solution.py:32
  66.6 10.6 %collective-permute-start.23 = (bf16[2,640,128]{2,1,0:T(8,128)(2,1)S(1)}, bf16[2,640,128]{2,1,0:T(8,128)(2,1)S(1)}, u32[]{:S(2)}, u32[]{:S(2)}) collective-permute-start(bf16[2,640,128]{2,1,0:T(8,128)(2,1)S(1)} %get-tuple-element.38), channel_id=1, source_target_pairs={{0,2},{1,3},{2,0},{3,1},{4,6},{5,7},{6,4},{7,5},{8,10},{9,11},{10,... | collective-permute-start | bytes 983048 | tf_op jit(solution)/shard_map/ppermute | solution.py:32
  67.2 16.5 %collective-permute-start.14 = (bf16[2,640,128]{2,1,0:T(8,128)(2,1)S(1)}, bf16[2,640,128]{2,1,0:T(8,128)(2,1)S(1)}, u32[]{:S(2)}, u32[]{:S(2)}) collective-permute-start(bf16[2,640,128]{2,1,0:T(8,128)(2,1)S(1)} %get-tuple-element.37), channel_id=1, source_target_pairs={{0,2},{1,3},{2,0},{3,1},{4,6},{5,7},{6,4},{7,5},{8,10},{9,11},{10,... | collective-permute-start | bytes 983048 | tf_op jit(solution)/shard_map/ppermute | solution.py:32
  77.3 9.1 %collective-permute-start.24 = (bf16[2,640,128]{2,1,0:T(8,128)(2,1)S(1)}, bf16[2,640,128]{2,1,0:T(8,128)(2,1)S(1)}, u32[]{:S(2)}, u32[]{:S(2)}) collective-permute-start(bf16[2,640,128]{2,1,0:T(8,128)(2,1)S(1)} %add_convert_fusion.3), channel_id=1, source_target_pairs={{0,4},{1,5},{2,6},{3,7},{4,0},{5,1},{6,2},{7,3},{8,12},{9,13},{10,... | collective-permute-start | bytes 983048 | tf_op jit(solution)/shard_map/ppermute | solution.py:32
  86.7 10.7 %collective-permute-start.16 = (bf16[2,640,128]{2,1,0:T(8,128)(2,1)S(1)}, bf16[2,640,128]{2,1,0:T(8,128)(2,1)S(1)}, u32[]{:S(2)}, u32[]{:S(2)}) collective-permute-start(bf16[2,640,128]{2,1,0:T(8,128)(2,1)S(1)} %get-tuple-element.36), channel_id=1, source_target_pairs={{0,2},{1,3},{2,0},{3,1},{4,6},{5,7},{6,4},{7,5},{8,10},{9,11},{10,... | collective-permute-start | bytes 983048 | tf_op jit(solution)/shard_map/ppermute | solution.py:32
  87.2 12.0 %collective-permute-start.25 = (bf16[2,640,128]{2,1,0:T(8,128)(2,1)S(1)}, bf16[2,640,128]{2,1,0:T(8,128)(2,1)S(1)}, u32[]{:S(2)}, u32[]{:S(2)}) collective-permute-start(bf16[2,640,128]{2,1,0:T(8,128)(2,1)S(1)} %get-tuple-element.19), channel_id=1, source_target_pairs={{0,12},{1,13},{2,14},{3,15},{4,8},{5,9},{6,10},{7,11},{8,4},{9,5},... | collective-permute-start | bytes 983048 | tf_op jit(solution)/shard_map/ppermute | solution.py:32
  89.8 15.2 %collective-permute-start.15 = (bf16[2,640,128]{2,1,0:T(8,128)(2,1)S(1)}, bf16[2,640,128]{2,1,0:T(8,128)(2,1)S(1)}, u32[]{:S(2)}, u32[]{:S(2)}) collective-permute-start(bf16[2,640,128]{2,1,0:T(8,128)(2,1)S(1)} %get-tuple-element.35), channel_id=1, source_target_pairs={{0,2},{1,3},{2,0},{3,1},{4,6},{5,7},{6,4},{7,5},{8,10},{9,11},{10,... | collective-permute-start | bytes 983048 | tf_op jit(solution)/shard_map/ppermute | solution.py:32
  97.5 8.3 %collective-permute-start.17 = (bf16[2,640,128]{2,1,0:T(8,128)(2,1)S(1)}, bf16[2,640,128]{2,1,0:T(8,128)(2,1)S(1)}, u32[]{:S(2)}, u32[]{:S(2)}) collective-permute-start(bf16[2,640,128]{2,1,0:T(8,128)(2,1)S(1)} %add_convert_fusion.5), channel_id=1, source_target_pairs={{0,4},{1,5},{2,6},{3,7},{4,0},{5,1},{6,2},{7,3},{8,12},{9,13},{10,... | collective-permute-start | bytes 983048 | tf_op jit(solution)/shard_map/ppermute | solution.py:32
  99.4 12.6 %collective-permute-start.26 = (bf16[2,640,128]{2,1,0:T(8,128)(2,1)S(1)}, bf16[2,640,128]{2,1,0:T(8,128)(2,1)S(1)}, u32[]{:S(2)}, u32[]{:S(2)}) collective-permute-start(bf16[2,640,128]{2,1,0:T(8,128)(2,1)S(1)} %add_convert_fusion.2), channel_id=1, source_target_pairs={{0,4},{1,5},{2,6},{3,7},{4,0},{5,1},{6,2},{7,3},{8,12},{9,13},{10,... | collective-permute-start | bytes 983048 | tf_op jit(solution)/shard_map/ppermute | solution.py:32
  103.5 18.4 %collective-permute-start.27 = (bf16[2,640,128]{2,1,0:T(8,128)(2,1)S(1)}, bf16[2,640,128]{2,1,0:T(8,128)(2,1)S(1)}, u32[]{:S(2)}, u32[]{:S(2)}) collective-permute-start(bf16[2,640,128]{2,1,0:T(8,128)(2,1)S(1)} %add_convert_fusion.2), channel_id=1, source_target_pairs={{0,2},{1,3},{2,0},{3,1},{4,6},{5,7},{6,4},{7,5},{8,10},{9,11},{10,... | collective-permute-start | bytes 983048 | tf_op jit(solution)/shard_map/ppermute | solution.py:32
  105.9 15.2 %collective-permute-start.18 = (bf16[2,640,128]{2,1,0:T(8,128)(2,1)S(1)}, bf16[2,640,128]{2,1,0:T(8,128)(2,1)S(1)}, u32[]{:S(2)}, u32[]{:S(2)}) collective-permute-start(bf16[2,640,128]{2,1,0:T(8,128)(2,1)S(1)} %get-tuple-element.21), channel_id=1, source_target_pairs={{0,12},{1,13},{2,14},{3,15},{4,8},{5,9},{6,10},{7,11},{8,4},{9,5},... | collective-permute-start | bytes 983048 | tf_op jit(solution)/shard_map/ppermute | solution.py:32
  112.0 9.9 %collective-permute-start.28 = (bf16[2,640,128]{2,1,0:T(8,128)(2,1)S(1)}, bf16[2,640,128]{2,1,0:T(8,128)(2,1)S(1)}, u32[]{:S(2)}, u32[]{:S(2)}) collective-permute-start(bf16[2,640,128]{2,1,0:T(8,128)(2,1)S(1)} %collective-permute-done.26), channel_id=1, source_target_pairs={{0,2},{1,3},{2,0},{3,1},{4,6},{5,7},{6,4},{7,5},{8,10},{9,11},{10,... | collective-permute-start | bytes 983048 | tf_op jit(solution)/shard_map/ppermute | solution.py:32
  113.3 16.6 %collective-permute-start.29 = (bf16[2,1280,128]{2,1,0:T(8,128)(2,1)S(1)}, bf16[2,1280,128]{2,1,0:T(8,128)(2,1)S(1)}, u32[]{:S(2)}, u32[]{:S(2)}) collective-permute-start(bf16[2,1280,128]{2,1,0:T(8,128)(2,1)S(1)} %pad_maximum_fusion.2.pa), channel_id=1, source_target_pairs={{0,1},{1,0},{2,3},{3,2},{4,5},{5,4},{6,7},{7,6},{8,9},{9,8},{10,11... | collective-permute-start | bytes 1966088 | tf_op jit(solution)/shard_map/ppermute | solution.py:32
  121.1 8.6 %collective-permute-start.19 = (bf16[2,640,128]{2,1,0:T(8,128)(2,1)S(1)}, bf16[2,640,128]{2,1,0:T(8,128)(2,1)S(1)}, u32[]{:S(2)}, u32[]{:S(2)}) collective-permute-start(bf16[2,640,128]{2,1,0:T(8,128)(2,1)S(1)} %add_convert_fusion.4), channel_id=1, source_target_pairs={{0,4},{1,5},{2,6},{3,7},{4,0},{5,1},{6,2},{7,3},{8,12},{9,13},{10,... | collective-permute-start | bytes 983048 | tf_op jit(solution)/shard_map/ppermute | solution.py:32
  122.0 8.0 %copy-start = (bf16[6,2,32,5120]{3,2,1,0:T(8,128)(2,1)S(1)}, bf16[6,2,32,5120]{3,2,1,0:T(8,128)(2,1)}, u32[]{:S(2)}) copy-start(bf16[6,2,32,5120]{3,2,1,0:T(8,128)(2,1)} %train.2) | copy-start | bytes 11796484
  122.1 7.9 %collective-permute-start.30 = (bf16[2,1280,128]{2,1,0:T(8,128)(2,1)S(1)}, bf16[2,1280,128]{2,1,0:T(8,128)(2,1)S(1)}, u32[]{:S(2)}, u32[]{:S(2)}) collective-permute-start(bf16[2,1280,128]{2,1,0:T(8,128)(2,1)S(1)} %pad_maximum_fusion.3.pb), channel_id=1, source_target_pairs={{0,1},{1,0},{2,3},{3,2},{4,5},{5,4},{6,7},{7,6},{8,9},{9,8},{10,11... | collective-permute-start | bytes 1966088 | tf_op jit(solution)/shard_map/ppermute | solution.py:32
  122.2 10.6 %collective-permute-start.20 = (bf16[2,640,128]{2,1,0:T(8,128)(2,1)S(1)}, bf16[2,640,128]{2,1,0:T(8,128)(2,1)S(1)}, u32[]{:S(2)}, u32[]{:S(2)}) collective-permute-start(bf16[2,640,128]{2,1,0:T(8,128)(2,1)S(1)} %add_convert_fusion.4), channel_id=1, source_target_pairs={{0,2},{1,3},{2,0},{3,1},{4,6},{5,7},{6,4},{7,5},{8,10},{9,11},{10,... | collective-permute-start | bytes 983048 | tf_op jit(solution)/shard_map/ppermute | solution.py:32
  129.7 9.6 %collective-permute-start.21 = (bf16[2,640,128]{2,1,0:T(8,128)(2,1)S(1)}, bf16[2,640,128]{2,1,0:T(8,128)(2,1)S(1)}, u32[]{:S(2)}, u32[]{:S(2)}) collective-permute-start(bf16[2,640,128]{2,1,0:T(8,128)(2,1)S(1)} %collective-permute-done.19), channel_id=1, source_target_pairs={{0,2},{1,3},{2,0},{3,1},{4,6},{5,7},{6,4},{7,5},{8,10},{9,11},{10,... | collective-permute-start | bytes 983048 | tf_op jit(solution)/shard_map/ppermute | solution.py:32
  129.9 9.6 %collective-permute-start.22 = (bf16[2,1280,128]{2,1,0:T(8,128)(2,1)S(1)}, bf16[2,1280,128]{2,1,0:T(8,128)(2,1)S(1)}, u32[]{:S(2)}, u32[]{:S(2)}) collective-permute-start(bf16[2,1280,128]{2,1,0:T(8,128)(2,1)S(1)} %pad_maximum_fusion.pa), channel_id=1, source_target_pairs={{0,1},{1,0},{2,3},{3,2},{4,5},{5,4},{6,7},{7,6},{8,9},{9,8},{10,11... | collective-permute-start | bytes 1966088 | tf_op jit(solution)/shard_map/ppermute | solution.py:32
  130.0 11.6 %copy-start.1 = (bf16[6,2,32,5120]{3,2,1,0:T(8,128)(2,1)S(1)}, bf16[6,2,32,5120]{3,2,1,0:T(8,128)(2,1)}, u32[]{:S(2)}) copy-start(bf16[6,2,32,5120]{3,2,1,0:T(8,128)(2,1)} %train.3) | copy-start | bytes 11796484
  139.4 4.3 %copy-start.10 = (s32[128]{0:T(128)S(1)}, s32[128]{0:T(128)}, u32[]{:S(2)}) copy-start(s32[128]{0:T(128)} %param.17) | copy-start | bytes 1540
  139.4 2.2 %collective-permute-start.31 = (bf16[2,1280,128]{2,1,0:T(8,128)(2,1)S(1)}, bf16[2,1280,128]{2,1,0:T(8,128)(2,1)S(1)}, u32[]{:S(2)}, u32[]{:S(2)}) collective-permute-start(bf16[2,1280,128]{2,1,0:T(8,128)(2,1)S(1)} %pad_maximum_fusion.1.pb), channel_id=1, source_target_pairs={{0,1},{1,0},{2,3},{3,2},{4,5},{5,4},{6,7},{7,6},{8,9},{9,8},{10,11... | collective-permute-start | bytes 1966088 | tf_op jit(solution)/shard_map/ppermute | solution.py:32
